TPU v7x, 512 devices: a whole 4x4x16 slice. The times are simulated.
512 devices in a mesh: tm: 32 (over y, x, core), stream: 16 (over z).
Axes of the slice: x: 4, y: 4, z: 16, core: 2. Of those that a mesh axis runs over, the one named last changes fastest.
Arguments:
- tokens: bfloat16 [65536, 2048], P(('tm', 'stream')), may hold values from -6 to 6
- w_query: bfloat16 [2048, 2048], P('stream'), may hold values from -0.125 to 0.125
- w_key: bfloat16 [2048, 2048], P('stream'), may hold values from -0.125 to 0.125
- w_value: bfloat16 [2048, 2048], P('stream'), may hold values from -0.125 to 0.125
- decay_proj: bfloat16 [2048, 16], P('stream'), may hold values from -0.125 to 0.125
- beta_proj: bfloat16 [2048, 16], P('stream'), may hold values from -0.125 to 0.125
- decay_rate: float32 [16], replicated, may hold values from 1.5258789e-05 to 0.1
- beta_bias: float32 [16], replicated, may hold values from -7 to 0
- norm_gain: float32 [128], replicated, may hold values from 0.5 to 1.5
Outputs:
- mixed: bfloat16 [65536, 2048], P(('tm', 'stream'))
All inputs are finite; a program needn't handle non-finite values.
Results may differ from a plain program's by a relative error of at most 0.0073.
Values may be sent and summed in bfloat16 or wider, within the bound.
No kernel may reach another device: no remote copies, remote signals or barrier semaphores. Data moves between devices by JAX's collectives and lax.ppermute only.
A program may use at most 128 MiB of HBM per device.

v0:
```python
import jax
import jax.numpy as jnp
from jax import lax
from jax.sharding import Mesh
from jax.sharding import PartitionSpec as P

HEADS = 16
DK = 128
DV = 128
GROUP = 256
TM = ("tm_0", "tm_1", "tm_2")
TM_STREAM = ("tm_0", "tm_1", "tm_2", "stream")


highest_precision = lax.Precision.HIGHEST


def in_one_piece(arrays, axis, dim, along):
    widths = [a.shape[along] for a in arrays]
    both = jnp.concatenate(arrays, axis=along)
    whole = lax.all_gather(both, axis, axis=dim, tiled=True)
    return tuple(jnp.split(whole, [sum(widths[:k]) for k in range(1, len(widths))], axis=along))


def nothing_yet(x, identity):
    return jax.tree.map(
        lambda a, e: jnp.broadcast_to(jnp.asarray(e, a.dtype), a.shape), x, identity
    )


def carried_in(x, axes, combine, identity):
    before = start = nothing_yet(x, identity)
    subtotal = x
    for axis in reversed(axes):
        length, place = (lax.axis_size(axis), lax.axis_index(axis))
        pieces = jax.tree.map(lambda part: lax.all_gather(part, axis), subtotal)
        inside, subtotal = (start, start)
        for k in range(length):
            passed = k < place
            subtotal = combine(subtotal, jax.tree.map(lambda part: part[k], pieces))
            inside = jax.tree.map(lambda new, old: jnp.where(passed, new, old), subtotal, inside)
        before = combine(inside, before)
    return before


def add_rows(inputs, piece):
    return jnp.dot(inputs, piece, preferred_element_type=jnp.float32)


def compose_pairs(earlier, later):
    first_map, first_shift = earlier
    second_map, second_shift = later
    joined_map = jnp.einsum("udf,ufe->ude", first_map, second_map, precision=highest_precision)
    joined_shift = (
        jnp.einsum("ued,udf->uef", first_shift, second_map, precision=highest_precision)
        + second_shift
    )
    return (joined_map, joined_shift)


def shards(
    tokens, w_query, w_key, w_value, decay_proj, beta_proj, decay_rate, beta_bias, norm_gain
):
    local_rows = tokens.shape[0]
    streams = lax.axis_size("stream")
    per_device = HEADS // streams

    def fold_one(piece):
        return add_rows(tokens, piece)

    raw_query = fold_one(lax.all_gather(w_query, "stream", axis=0, tiled=True))
    raw_key = fold_one(lax.all_gather(w_key, "stream", axis=0, tiled=True))
    raw_value = fold_one(lax.all_gather(w_value, "stream", axis=0, tiled=True))
    pieces = in_one_piece((decay_proj, beta_proj), "stream", 0, 1)
    decay_logit, beta_logit = tuple((add_rows(tokens, piece) for piece in pieces))
    query_heads = raw_query.reshape(local_rows, HEADS, DK)
    key_heads = raw_key.reshape(local_rows, HEADS, DK)
    queries = (
        (
            query_heads
            * lax.rsqrt(jnp.sum(query_heads * query_heads, -1, keepdims=True) + 1e-06)
            * DK ** (-0.5)
        )
        .astype(jnp.bfloat16)
        .reshape(local_rows, HEADS * DK)
    )
    key_rows = (
        (key_heads * lax.rsqrt(jnp.sum(key_heads * key_heads, -1, keepdims=True) + 1e-06))
        .astype(jnp.bfloat16)
        .reshape(local_rows, HEADS * DK)
    )
    values = raw_value.astype(jnp.bfloat16)
    log_decay = (-decay_rate * jax.nn.softplus(decay_logit)).astype(jnp.bfloat16)
    strength = jax.nn.sigmoid(beta_logit + beta_bias).astype(jnp.bfloat16)
    got_query, got_key, got_value, got_decay, got_strength = (
        lax.all_to_all(queries, "stream", split_axis=1, concat_axis=0, tiled=True),
        lax.all_to_all(key_rows, "stream", split_axis=1, concat_axis=0, tiled=True),
        lax.all_to_all(values, "stream", split_axis=1, concat_axis=0, tiled=True),
        lax.all_to_all(log_decay, "stream", split_axis=1, concat_axis=0, tiled=True),
        lax.all_to_all(strength, "stream", split_axis=1, concat_axis=0, tiled=True),
    )
    block_rows = got_query.shape[0]
    num_blocks = block_rows // GROUP
    query_b = (
        got_query.reshape(num_blocks, GROUP, per_device, DK)
        .astype(jnp.float32)
        .transpose(0, 2, 1, 3)
    )
    key_b = (
        got_key.reshape(num_blocks, GROUP, per_device, DK).astype(jnp.float32).transpose(0, 2, 1, 3)
    )
    value_b = (
        got_value.reshape(num_blocks, GROUP, per_device, DV)
        .astype(jnp.float32)
        .transpose(0, 2, 1, 3)
    )
    decay_b = (
        got_decay.reshape(num_blocks, GROUP, per_device).astype(jnp.float32).transpose(0, 2, 1)
    )
    strength_b = (
        got_strength.reshape(num_blocks, GROUP, per_device).astype(jnp.float32).transpose(0, 2, 1)
    )
    positions = jnp.arange(GROUP)
    strict = positions[:, None] > positions[None, :]
    inclusive_mask = positions[:, None] >= positions[None, :]
    identity = jnp.eye(GROUP, dtype=jnp.float32)
    key_identity = jnp.eye(DK, dtype=jnp.float32)
    cumulative = jnp.cumsum(decay_b, axis=2)
    growth = jnp.exp(cumulative)
    last_log = cumulative[..., -1:]
    tail = jnp.exp(last_log - cumulative)
    key_products = jnp.einsum("nucd,numd->nucm", key_b, key_b, precision=highest_precision)
    spread = cumulative[..., :, None] - cumulative[..., None, :]
    decay_matrix = jnp.exp(jnp.where(inclusive_mask, spread, 0.0))
    lower = (
        jnp.where(strict, strength_b[..., :, None] * decay_matrix * key_products, 0.0) + identity
    )
    right_side = jnp.concatenate(
        [(strength_b * growth)[..., None] * key_b, strength_b[..., None] * value_b], -1
    )
    solved = jax.scipy.linalg.solve_triangular(lower, right_side, lower=True, unit_diagonal=True)
    weights_w = solved[..., :DK]
    updates = solved[..., DK:]
    key_tail = tail[..., None] * key_b
    attention_scores = jnp.where(
        inclusive_mask,
        jnp.einsum("nucd,numd->nucm", query_b, key_b, precision=highest_precision) * decay_matrix,
        0.0,
    )
    query_grown = growth[..., None] * query_b
    block_map = jnp.exp(last_log)[..., None] * key_identity - jnp.einsum(
        "nucd,nuce->nude", weights_w, key_tail, precision=highest_precision
    )
    block_shift = jnp.einsum("nuce,nucd->nued", updates, key_tail, precision=highest_precision)

    def compose_step(carry, pair):
        return (compose_pairs(carry, pair), carry)

    start_map = jnp.broadcast_to(key_identity, (per_device, DK, DK))
    start_shift = jnp.zeros((per_device, DV, DK), jnp.float32)
    totals, prefixes = lax.scan(compose_step, (start_map, start_shift), (block_map, block_shift))
    total_map, total_shift = totals
    prefix_map, prefix_shift = prefixes
    scanned = carried_in((total_map, total_shift), TM, compose_pairs, (start_map, start_shift))
    state_in = scanned[1]
    block_states = (
        jnp.einsum("ued,nudf->nuef", state_in, prefix_map, precision=highest_precision)
        + prefix_shift
    )
    fresh = updates - jnp.einsum(
        "nucd,nued->nuce", weights_w, block_states, precision=highest_precision
    )
    read = jnp.einsum(
        "nucd,nued->nuce", query_grown, block_states, precision=highest_precision
    ) + jnp.einsum("nucm,nume->nuce", attention_scores, fresh, precision=highest_precision)
    readout = read.transpose(0, 2, 1, 3).reshape(block_rows, per_device * DV).astype(jnp.bfloat16)
    returned = lax.all_to_all(readout, "stream", split_axis=0, concat_axis=1, tiled=True)
    head_read = returned.reshape(local_rows, HEADS, DV).astype(jnp.float32)
    normed = (
        head_read
        * lax.rsqrt(jnp.mean(head_read * head_read, -1, keepdims=True) + 1e-06)
        * norm_gain
    )
    return normed.reshape(local_rows, HEADS * DV).astype(jnp.bfloat16)


def solution(mesh):
    finer = Mesh(
        mesh.devices.reshape(4, 4, 2, mesh.shape["stream"]), ("tm_0", "tm_1", "tm_2", "stream")
    )
    return jax.shard_map(
        shards,
        mesh=finer,
        in_specs=(
            P(TM_STREAM, None),
            P("stream", None),
            P("stream", None),
            P("stream", None),
            P("stream", None),
            P("stream", None),
            P(),
            P(),
            P(),
        ),
        out_specs=P(TM_STREAM, None),
        check_vma=False,
    )
```

profile of v0, /device:TPU:34, one launch (start us, length us, event | category | flops | bytes accessed | tf_op | source)
XLA Modules:
  0.0 717.1 jit_solution(13404925184703037204)
XLA Ops:
  10.1 34.2 %all_gather.48 = bf16[2048,32]{0,1:T(8,128)(2,1)S(1)} all-gather(bf16[128,32]{0,1:T(8,128)(2,1)S(1)} %pad_maximum_fusion), channel_id=1, replica_groups=mesh['tm_0'=4,'tm_1'=4,'tm_2'=2,'stream'=16] {'stream'}, dimensions={0}, use_global_device_ids=true | all-gather | bytes 139264 | tf_op jit(solution)/shard_map/all_gather | solution.py:21
  45.2 9.1 %all-to-all-start = ((bf16[128,16,1]{0,2,1:T(2,128)(2,1)}), bf16[128,16,1]{0,2,1:T(2,128)(2,1)S(1)}, u32[]{:S(2)}, u32[]{:S(2)}) async-start(bf16[128,16,1]{0,2,1:T(2,128)(2,1)} %copy.65), calls=%async_computation | async-start | bytes 16384 | tf_op jit(solution)/shard_map/all_to_all | solution.py:99
  56.8 8.6 %all-to-all-done = bf16[128,16,1]{0,2,1:T(2,128)(2,1)S(1)} async-done(((bf16[128,16,1]{0,2,1:T(2,128)(2,1)}), bf16[128,16,1]{0,2,1:T(2,128)(2,1)S(1)}, u32[]{:S(2)}, u32[]{:S(2)}) %all-to-all-start) | async-done | bytes 4128 | tf_op jit(solution)/shard_map/all_to_all | solution.py:99
  65.4 4.6 all-to-all-start.2
  70.8 47.6 %all-gather.14.cloned.1.call-done = bf16[2048,2048]{1,0:T(8,128)(2,1)} async-done(((bf16[128,2048]{1,0:T(8,128)(2,1)}), bf16[2048,2048]{1,0:T(8,128)(2,1)}) %all-gather.14.cloned.1.call-update) | async-done | bytes 8388624 | tf_op jit(solution)/shard_map/all_gather | solution.py:73
  118.4 4.6 fusion.21
  124.0 11.4 %all-to-all-start.4 = ((bf16[128,16,128]{2,0,1:T(8,128)(2,1)}), bf16[128,16,128]{2,0,1:T(8,128)(2,1)S(1)}, u32[]{:S(2)}, u32[]{:S(2)}) async-start(bf16[128,16,128]{2,0,1:T(8,128)(2,1)} %bitcast.256), calls=%async_computation.4 | async-start | bytes 1048576 | tf_op jit(solution)/shard_map/all_to_all | solution.py:98
  135.6 109.5 %all-gather.12.cloned.1.call-done = bf16[2048,2048]{1,0:T(8,128)(2,1)} async-done(((bf16[128,2048]{1,0:T(8,128)(2,1)}), bf16[2048,2048]{1,0:T(8,128)(2,1)}) %all-gather.12.cloned.1.call-update) | async-done | bytes 8388624 | tf_op jit(solution)/shard_map/all_gather | solution.py:72
  245.0 4.6 fusion.143
  250.7 1.2 copy_bitcast_fusion.1
  251.9 11.1 %all-to-all-start.3 = ((bf16[128,16,128]{2,0,1:T(8,128)(2,1)}), bf16[128,16,128]{2,0,1:T(8,128)(2,1)S(1)}, u32[]{:S(2)}, u32[]{:S(2)}) async-start(bf16[128,16,128]{2,0,1:T(8,128)(2,1)} %copy_bitcast_fusion.1), calls=%async_computation.3 | async-start | bytes 1048576 | tf_op jit(solution)/shard_map/all_to_all | solution.py:97
  263.3 109.3 %all-gather.10.cloned.1.call-done = bf16[2048,2048]{1,0:T(8,128)(2,1)} async-done(((bf16[128,2048]{1,0:T(8,128)(2,1)}), bf16[2048,2048]{1,0:T(8,128)(2,1)}) %all-gather.10.cloned.1.call-update) | async-done | bytes 8388624 | tf_op jit(solution)/shard_map/all_gather | solution.py:71
  372.6 4.6 fusion.142
  378.3 1.2 copy_bitcast_fusion.2
  379.6 1.3 broadcast_multiply_fusion
  380.9 11.2 %all-to-all-start.1 = ((bf16[128,16,128]{2,0,1:T(8,128)(2,1)}), bf16[128,16,128]{2,0,1:T(8,128)(2,1)}, u32[]{:S(2)}, u32[]{:S(2)}) async-start(bf16[128,16,128]{2,0,1:T(8,128)(2,1)} %copy_bitcast_fusion.2), calls=%async_computation.1 | async-start | bytes 1048576 | tf_op jit(solution)/shard_map/all_to_all | solution.py:96
  392.1 2.1 select_add_fusion
  394.3 5.6 while.18
  394.9 2.2 bitcast_dynamic-update-slice_fusion.6
  397.7 2.2 bitcast_dynamic-update-slice_fusion.6
  399.9 158.6 %custom-call.4 = f32[8,2,128,128]{2,3,1,0:T(8,128)} custom-call(f32[8,2,128,128]{3,2,1,0:T(8,128)} %bitcast.294), custom_call_target="InvertDiagBlocksLowerTriangular" | custom-call | tf_op jit(solution)/shard_map/jit(_solve_triangular)/vmap()/triangular_solve | solution.py:141
  564.4 2.9 convolution_bitcast_fusion.3
  567.4 2.9 fusion.22
  570.3 31.5 %while.17 = (s32[]{:T(128)}, f32[1,128,128]{1,2,0:T(8,128)S(1)}, f32[1,128,128]{1,2,0:T(8,128)S(1)}, f32[8,1,128,128]{2,3,1,0:T(8,128)}, f32[8,1,128,128]{2,3,1,...) while((s32[]{:T(128)}, f32[1,128,128]{1,2,0:T(8,128)S(1)}, ...), condition=%wide.region_5.6_spmd, body=%wide.region_4.5_spmd.sunk | while | flops 50348032 | bytes 1245293 | solution.py:161
  571.9 1.1 fusion.189
  573.0 1.1 convolution_bitcast_fusion.7
  575.8 1.1 fusion.189
  577.0 1.1 convolution_bitcast_fusion.7
  580.9 1.1 convolution_bitcast_fusion.7
  583.7 1.1 fusion.189
  584.8 1.1 convolution_bitcast_fusion.7
  588.7 1.1 convolution_bitcast_fusion.7
  592.6 1.1 convolution_bitcast_fusion.7
  596.6 1.1 convolution_bitcast_fusion.7
  600.5 1.1 convolution_bitcast_fusion.7
  601.9 1.9 all-gather
  605.3 12.5 %all-gather.1 = f32[512,128]{1,0:T(8,128)S(1)} all-gather(f32[128,128]{1,0:T(8,128)S(1)} %fusion.92), channel_id=3, replica_groups=mesh['tm_0'=4,'tm_1'=4,'tm_2'=2,'stream'=16] {'tm_1'}, dimensions={0}, use_global_device_ids=true | all-gather | bytes 327680 | tf_op jit(solution)/shard_map/all_gather | solution.py:36
  619.9 2.2 all-gather.3
  623.6 12.7 %all-gather.2 = f32[512,128]{1,0:T(8,128)S(1)} all-gather(f32[128,128]{1,0:T(8,128)S(1)} %fusion.98), channel_id=4, replica_groups=mesh['tm_0'=4,'tm_1'=4,'tm_2'=2,'stream'=16] {'tm_0'}, dimensions={0}, use_global_device_ids=true | all-gather | bytes 327680 | tf_op jit(solution)/shard_map/all_gather | solution.py:36
  637.4 12.3 %all-gather.4 = f32[512,128]{1,0:T(8,128)S(1)} all-gather(f32[128,128]{1,0:T(8,128)S(1)} %convolution_add_fusion.7), channel_id=6, replica_groups=mesh['tm_0'=4,'tm_1'=4,'tm_2'=2,'stream'=16] {'tm_1'}, dimensions={0}, use_global_device_ids=true | all-gather | bytes 327680 | tf_op jit(solution)/shard_map/all_gather | solution.py:36
  651.1 12.3 %all-gather.5 = f32[512,128]{1,0:T(8,128)S(1)} all-gather(f32[128,128]{1,0:T(8,128)S(1)} %convolution_add_fusion.4), channel_id=7, replica_groups=mesh['tm_0'=4,'tm_1'=4,'tm_2'=2,'stream'=16] {'tm_0'}, dimensions={0}, use_global_device_ids=true | all-gather | bytes 327680 | tf_op jit(solution)/shard_map/all_gather | solution.py:36
  666.3 2.0 fusion.17
  668.4 1.6 fusion.145
  670.0 2.2 fusion.47
  672.2 3.3 fusion.18
  675.5 12.0 %all-to-all-start.5 = ((bf16[16,128,128]{2,1,0:T(8,128)(2,1)}), bf16[16,128,128]{2,1,0:T(8,128)(2,1)S(1)}, u32[]{:S(2)}, u32[]{:S(2)}) async-start(bf16[16,128,128]{2,1,0:T(8,128)(2,1)} %bitcast.59), calls=%async_computation.5 | async-start | bytes 1048576 | tf_op jit(solution)/shard_map/all_to_all | solution.py:177
  687.6 21.5 %all-to-all-done.5 = bf16[16,128,128]{2,1,0:T(8,128)(2,1)S(1)} async-done(((bf16[16,128,128]{2,1,0:T(8,128)(2,1)}), bf16[16,128,128]{2,1,0:T(8,128)(2,1)S(1)}, u32[]{:S(2)}, u32[]{:S(2)}) %all-to-all-start.5) | async-done | bytes 524320 | tf_op jit(solution)/shard_map/all_to_all | solution.py:177
  709.4 1.1 fusion.40
  (178 shorter events, 47.6 us)
Async XLA Ops:
  6.5 37.8 %copy-start = (bf16[128,2048]{1,0:T(8,128)(2,1)S(1)}, bf16[128,2048]{1,0:T(8,128)(2,1)}, u32[]{:S(2)}) copy-start(bf16[128,2048]{1,0:T(8,128)(2,1)} %param.11) | copy-start | bytes 1572868
  6.5 48.7 %copy-start.21 = (f32[16]{0:T(128)S(1)}, f32[16]{0:T(128)}, u32[]{:S(2)}) copy-start(f32[16]{0:T(128)} %param.18) | copy-start | bytes 196
  6.5 111.9 %all-gather.14.cloned.1.call-start = ((), (), s32[]{:S(2)}) async-start(), calls=%async_computation.8 | async-start | bytes 8912896 | tf_op jit(solution)/shard_map/all_gather | solution.py:73
  7.3 237.8 %all-gather.12.cloned.1.call-start = ((), (), s32[]{:S(2)}) async-start(), calls=%async_computation.7 | async-start | bytes 8912896 | tf_op jit(solution)/shard_map/all_gather | solution.py:72
  8.0 364.6 %all-gather.10.cloned.1.call-start = ((), (), s32[]{:S(2)}) async-start(), calls=%async_computation.6 | async-start | bytes 8912896 | tf_op jit(solution)/shard_map/all_gather | solution.py:71
  45.2 20.2 %all-to-all-start = ((bf16[128,16,1]{0,2,1:T(2,128)(2,1)}), bf16[128,16,1]{0,2,1:T(2,128)(2,1)S(1)}, u32[]{:S(2)}, u32[]{:S(2)}) async-start(bf16[128,16,1]{0,2,1:T(2,128)(2,1)} %copy.65), calls=%async_computation | async-start | bytes 16384 | tf_op jit(solution)/shard_map/all_to_all | solution.py:99
  54.3 337.8 %copy-start.15 = (pred[256,256]{1,0:T(8,128)(4,1)}, pred[256,256]{1,0:T(8,128)(4,1)S(1)}, u32[]{:S(2)}) copy-start(pred[256,256]{1,0:T(8,128)(4,1)S(1)} %iota_compare_fusion.2) | copy-start | bytes 196612
  65.4 58.6 %all-to-all-start.2 = ((bf16[128,16,1]{0,2,1:T(2,128)(2,1)}), bf16[128,16,1]{0,2,1:T(2,128)(2,1)S(1)}, u32[]{:S(2)}, u32[]{:S(2)}) async-start(bf16[128,16,1]{0,2,1:T(2,128)(2,1)} %copy.68), calls=%async_computation.2 | async-start | bytes 16384 | tf_op jit(solution)/shard_map/all_to_all | solution.py:100
  124.0 127.9 %all-to-all-start.4 = ((bf16[128,16,128]{2,0,1:T(8,128)(2,1)}), bf16[128,16,128]{2,0,1:T(8,128)(2,1)S(1)}, u32[]{:S(2)}, u32[]{:S(2)}) async-start(bf16[128,16,128]{2,0,1:T(8,128)(2,1)} %bitcast.256), calls=%async_computation.4 | async-start | bytes 1048576 | tf_op jit(solution)/shard_map/all_to_all | solution.py:98
  251.9 125.4 %copy-start.5 = (bf16[128,16,128]{2,0,1:T(8,128)(2,1)}, bf16[128,16,128]{2,0,1:T(8,128)(2,1)S(1)}, u32[]{:S(2)}) copy-start(bf16[128,16,128]{2,0,1:T(8,128)(2,1)S(1)} %all-to-all-done.4) | copy-start | bytes 1572868
  251.9 129.1 %all-to-all-start.3 = ((bf16[128,16,128]{2,0,1:T(8,128)(2,1)}), bf16[128,16,128]{2,0,1:T(8,128)(2,1)S(1)}, u32[]{:S(2)}, u32[]{:S(2)}) async-start(bf16[128,16,128]{2,0,1:T(8,128)(2,1)} %copy_bitcast_fusion.1), calls=%async_computation.3 | async-start | bytes 1048576 | tf_op jit(solution)/shard_map/all_to_all | solution.py:97
  377.9 1.6 copy-start.6
  379.5 12.6 %copy-start.17 = (pred[256,256]{1,0:T(8,128)(4,1)S(1)}, pred[256,256]{1,0:T(8,128)(4,1)}, u32[]{:S(2)}) copy-start(pred[256,256]{1,0:T(8,128)(4,1)} %get-tuple-element.118) | copy-start | bytes 196612
  380.9 287.4 %all-to-all-start.1 = ((bf16[128,16,128]{2,0,1:T(8,128)(2,1)}), bf16[128,16,128]{2,0,1:T(8,128)(2,1)}, u32[]{:S(2)}, u32[]{:S(2)}) async-start(bf16[128,16,128]{2,0,1:T(8,128)(2,1)} %copy_bitcast_fusion.2), calls=%async_computation.1 | async-start | bytes 1048576 | tf_op jit(solution)/shard_map/all_to_all | solution.py:96
  558.5 1.2 copy-start.3
  559.8 1.2 copy-start.8
  603.8 0.8 copy-start.7
  604.6 0.6 copy-start.10
  605.3 18.3 %copy-start.9 = (f32[128,128]{1,0:T(8,128)}, f32[128,128]{1,0:T(8,128)S(1)}, u32[]{:S(2)}) copy-start(f32[128,128]{1,0:T(8,128)S(1)} %fusion.92) | copy-start | bytes 196612
  619.9 31.0 %copy-start.11 = (f32[128,128]{1,0:T(8,128)S(1)}, f32[128,128]{1,0:T(8,128)}, u32[]{:S(2)}) copy-start(f32[128,128]{1,0:T(8,128)} %copy-done.10) | copy-start | bytes 196612
  619.9 44.2 %copy-start.12 = (f32[128,128]{1,0:T(8,128)S(1)}, f32[128,128]{1,0:T(8,128)}, u32[]{:S(2)}) copy-start(f32[128,128]{1,0:T(8,128)} %fusion.88) | copy-start | bytes 196612
  622.1 42.4 %copy-start.19 = (f32[128]{0:T(128)S(1)}, f32[128]{0:T(128)}, u32[]{:S(2)}) copy-start(f32[128]{0:T(128)} %multiply_reduce_fusion.1) | copy-start | bytes 1540
  623.4 41.3 %copy-start.18 = (f32[128]{0:T(128)S(1)}, f32[128]{0:T(128)}, u32[]{:S(2)}) copy-start(f32[128]{0:T(128)} %multiply_reduce_fusion) | copy-start | bytes 1540
  623.6 41.3 %copy-start.13 = (f32[8,1,128,128]{2,3,1,0:T(8,128)S(1)}, f32[8,1,128,128]{2,3,1,0:T(8,128)}, u32[]{:S(2)}) copy-start(f32[8,1,128,128]{2,3,1,0:T(8,128)} %get-tuple-element.48) | copy-start | bytes 1572868
  623.6 41.3 %copy-start.14 = (f32[8,1,128,128]{2,3,1,0:T(8,128)S(1)}, f32[8,1,128,128]{2,3,1,0:T(8,128)}, u32[]{:S(2)}) copy-start(f32[8,1,128,128]{2,3,1,0:T(8,128)} %get-tuple-element.45) | copy-start | bytes 1572868
  665.5 0.8 copy-start.1
  668.4 1.6 copy-start.2
  668.4 3.8 copy-start.4
  668.4 3.9 copy-start.16
  672.2 15.3 %copy-start.20 = (f32[128]{0:T(128)S(1)}, f32[128]{0:T(128)}, u32[]{:S(2)}) copy-start(f32[128]{0:T(128)} %param.19) | copy-start | bytes 1540
  675.5 33.5 %all-to-all-start.5 = ((bf16[16,128,128]{2,1,0:T(8,128)(2,1)}), bf16[16,128,128]{2,1,0:T(8,128)(2,1)S(1)}, u32[]{:S(2)}, u32[]{:S(2)}) async-start(bf16[16,128,128]{2,1,0:T(8,128)(2,1)} %bitcast.59), calls=%async_computation.5 | async-start | bytes 1048576 | tf_op jit(solution)/shard_map/all_to_all | solution.py:177
Sparse Core Ops, SparseCore 0:
  9.4 108.9 all-gather.13
  120.5 124.5 all-gather.11
  247.1 125.4 all-gather.9
where the time goes:
time: 719 us; the launch traced here: 717 us
  waiting for transfers between devices  299 us (42%)
  other arithmetic  171 us (24%)
  blocking collectives  88 us (12%)
  matrix products  59.8 us (8%)
  starting transfers between devices  59.5 us (8%)
  local copies, waits for them, and re-layouts  26.1 us (4%)
  between operations  13.7 us (2%)
    another operation x3, other arithmetic, shards(): jax.scipy.linalg.solve_triangular(lower, right_side, lower=True, unit_dia...  159 us
    all_gather x1, waiting for transfers between devices, shards(): raw_key = fold_one(lax.all_gather(w_key, 'stream', axis=0, tiled=True))  109 us
    all_gather x1, waiting for transfers between devices, shards(): raw_query = fold_one(lax.all_gather(w_query, 'stream', axis=0, tiled=True))  109 us
    all_gather x6, blocking collectives, carried_in(): pieces = jax.tree.map(lambda part: lax.all_gather(part, axis), subtotal)  53.8 us
    all_gather x1, waiting for transfers between devices, shards(): raw_value = fold_one(lax.all_gather(w_value, 'stream', axis=0, tiled=True))  47.6 us
    all_gather x1, blocking collectives, in_one_piece(): whole = lax.all_gather(both, axis, axis=dim, tiled=True)  34.2 us
    all_to_all x1, waiting for transfers between devices, shards(): lax.all_to_all(readout, 'stream', split_axis=0, concat_axis=1, tiled=True)  21.5 us
    dot_general x5, matrix products, add_rows(): return jnp.dot(inputs, piece, preferred_element_type=jnp.float32)  14.4 us
  transfers between devices with their start and end apart: 9, of which 5 were waited for; matrix products, arithmetic and copies ran while one was open for 34% of the time, Pallas kernels for 0%

commit v1 on v0

v1 whole, which is shorter than its diff:
```python
import jax
import jax.numpy as jnp
from jax import lax
from jax.experimental import pallas as pl
from jax.experimental.pallas import tpu as pltpu
from jax.sharding import Mesh
from jax.sharding import PartitionSpec as P

HEADS = 16
DK = 128
DV = 128
CHUNK = 128
GANG = 8
WIDE = 512
TM_STREAM = ("tm_0", "tm_1", "tm_2", "stream")
f32 = jnp.float32
bf16 = jnp.bfloat16


def mm(a, b, ca=1, cb=0):
    return lax.dot_general(
        a.astype(bf16), b.astype(bf16), (((ca,), (cb,)), ((), ())), preferred_element_type=f32
    )


def mm_exact(a, b, ca=1, cb=0):
    return lax.dot_general(
        a, b, (((ca,), (cb,)), ((), ())), precision=lax.Precision.HIGHEST, preferred_element_type=f32
    )


def chunk_kernel(gate_ref, raw_ref, reach_ref, own_ref, total_ref):
    rate, bias = gate_ref[0], gate_ref[1]
    row = lax.broadcasted_iota(jnp.int32, (CHUNK, CHUNK), 0)
    col = lax.broadcasted_iota(jnp.int32, (CHUNK, CHUNK), 1)
    strict, inclusive = row > col, row >= col
    eye = jnp.where(row == col, 1.0, 0.0).astype(f32)
    ones_below = jnp.where(inclusive, 1.0, 0.0).astype(bf16)
    total_ref[0:DK, :] = eye
    total_ref[DK:, :] = jnp.zeros((DV, DK), f32)

    def below(size):
        return (
            (row // (2 * size) == col // (2 * size))
            & ((row // size) % 2 == 1)
            & ((col // size) % 2 == 0)
        )

    def gang(step, carry):
        starts = [pl.multiple_of((step * GANG + i) * CHUNK, CHUNK) for i in range(GANG)]
        each = range(GANG)
        q, k, v, beta, grow, scale_row, beta_row, tail, last, decay = ([] for _ in range(10))
        for i in each:
            raw_q = raw_ref[pl.ds(starts[i], CHUNK), 0:128]
            raw_k = raw_ref[pl.ds(starts[i], CHUNK), 128:256]
            raw_v = raw_ref[pl.ds(starts[i], CHUNK), 256:384]
            logits = raw_ref[pl.ds(starts[i], CHUNK), 384:512]
            q.append(
                (
                    raw_q
                    * lax.rsqrt(jnp.sum(raw_q * raw_q, -1, keepdims=True) + 1e-06)
                    * DK ** (-0.5)
                ).astype(bf16)
            )
            k.append(
                (raw_k * lax.rsqrt(jnp.sum(raw_k * raw_k, -1, keepdims=True) + 1e-06)).astype(bf16)
            )
            v.append(raw_v.astype(bf16))
            x = logits[:, 0:1]
            softplus = jnp.maximum(x, 0.0) + jnp.log1p(jnp.exp(-jnp.abs(x)))
            log_decay = (-rate * softplus).astype(bf16)
            strength = (1.0 / (1.0 + jnp.exp(-(logits[:, 1:2] + bias)))).astype(bf16).astype(f32)
            g = mm(ones_below, jnp.broadcast_to(log_decay, (CHUNK, CHUNK)))
            b = jnp.broadcast_to(strength, (CHUNK, CHUNK))
            turned = jnp.where(col < 64, g, b).T
            g_row, b_row = turned[0:1, :], turned[64:65, :]
            g_last = g_row[:, CHUNK - 1 : CHUNK]
            beta.append(b)
            grow.append(jnp.exp(g))
            beta_row.append(b_row)
            scale_row.append(b_row * jnp.exp(g_row))
            tail.append(jnp.exp(g_last - g))
            last.append(jnp.exp(g_last))
            decay.append(jnp.exp(jnp.where(inclusive, g - g_row, 0.0)))
        both = [mm(jnp.concatenate([q[i], k[i]], 0), k[i], 1, 1) for i in each]
        scores = [jnp.where(inclusive, both[i][:CHUNK] * decay[i], 0.0) for i in each]
        lower = [jnp.where(strict, beta[i] * decay[i] * both[i][CHUNK:], 0.0) for i in each]
        inverse = [eye - jnp.where(below(1), lower[i], 0.0) for i in each]
        for size in (2, 4, 8, 16, 32, 64):
            mask = below(size)
            inner = [mm(jnp.where(mask, lower[i], 0.0), inverse[i]) for i in each]
            inverse = [inverse[i] - mm(inverse[i], inner[i]) for i in each]
        rounded = [inverse[i].astype(bf16) for i in each]
        high = [lower[i].astype(bf16) for i in each]
        low = [(lower[i] - high[i].astype(f32)).astype(bf16) for i in each]
        rest = [
            eye - rounded[i].astype(f32) - mm(high[i], rounded[i]) - mm(low[i], rounded[i])
            for i in each
        ]
        inverse = [rounded[i].astype(f32) + mm(rounded[i], rest[i]) for i in each]
        w = [mm(inverse[i] * scale_row[i], k[i]) for i in each]
        u = [mm(inverse[i] * beta_row[i], v[i]) for i in each]
        wu = [jnp.concatenate([w[i], u[i]], 1) for i in each]
        tail2 = [jnp.concatenate([tail[i], tail[i]], 1) for i in each]
        change = [mm(wu[i] * tail2[i], k[i], 0, 0) for i in each]
        inside = [mm(scores[i], wu[i]) for i in each]
        reach = [grow[i] * q[i].astype(f32) - inside[i][:, :DK] for i in each]
        state = total_ref[...]
        for i in each:
            out = mm(reach[i], state, 1, 1)
            reach_ref[pl.ds(starts[i], CHUNK), :] = out[:, :DK].astype(bf16)
            own_ref[pl.ds(starts[i], CHUNK), :] = out[:, DK:] + inside[i][:, DK:]
            moved = mm(state, change[i][:DK])
            state = last[i] * state - moved
            state = jnp.concatenate([state[:DK], state[DK:] + change[i][DK:]], 0)
        total_ref[...] = state
        return carry

    lax.fori_loop(0, raw_ref.shape[0] // (CHUNK * GANG), gang, 0)


def join_kernel(place_ref, mine_ref, other_ref, prefix_ref, total_ref):
    place, core = place_ref[0], place_ref[1]
    row = lax.broadcasted_iota(jnp.int32, (DK + DV, DK), 0)
    col = lax.broadcasted_iota(jnp.int32, (DK + DV, DK), 1)
    state = jnp.where(row == col, 1.0, 0.0).astype(f32)
    prefix_ref[...] = state
    for j in range(8):
        piece = jnp.where(core == j % 2, mine_ref[j // 2], other_ref[j // 2])
        moved = mm_exact(state, piece[:DK])
        state = jnp.concatenate([moved[:DK], moved[DK:] + piece[DK:]], 0)

        @pl.when(place == j + 1)
        def _():
            prefix_ref[...] = state

    total_ref[...] = state


def read_kernel(place_ref, outer_ref, prefix_ref, reach_ref, own_ref, read_ref):
    place = place_ref[2]
    state = jnp.zeros((DV, DK), f32)
    for j in range(3):
        moved = mm_exact(state, outer_ref[j, :DK]) + outer_ref[j, DK:]
        state = jnp.where(j < place, moved, state)
    state = mm_exact(state, prefix_ref[:DK]) + prefix_ref[DK:]
    read_ref[...] = (mm(reach_ref[...], state, 1, 1) + own_ref[...]).astype(bf16)


def ring_gather(x, axis):
    size, me = lax.axis_size(axis), lax.axis_index(axis)
    out = jnp.zeros((size,) + x.shape, x.dtype)
    for shift in range(size):
        piece = x
        if shift:
            piece = lax.ppermute(x, axis, [(i, (i + shift) % size) for i in range(size)])
        out = lax.dynamic_update_index_in_dim(out, piece, lax.rem(me - shift + size, size), 0)
    return out


def shards(
    tokens, w_query, w_key, w_value, decay_proj, beta_proj, decay_rate, beta_bias, norm_gain
):
    local_rows = tokens.shape[0]
    streams = lax.axis_size("stream")
    head = lax.axis_index("stream")
    at_y, at_x, at_c = lax.axis_index("tm_0"), lax.axis_index("tm_1"), lax.axis_index("tm_2")
    vmem = pl.BlockSpec(memory_space=pltpu.VMEM)
    smem = pl.BlockSpec(memory_space=pltpu.SMEM)

    shares = 16
    rows = w_query.shape[0] // shares
    first = (at_y * 4 + at_x) * rows

    def share(w, width):
        return lax.dynamic_slice_in_dim(w, first, rows, 0).reshape(rows, HEADS, width)

    weights = jnp.concatenate(
        [
            share(w_query, DK),
            share(w_key, DK),
            share(w_value, DV),
            share(decay_proj, 1),
            share(beta_proj, 1),
            jnp.zeros((rows, HEADS, WIDE - 386), bf16),
        ],
        -1,
    ).transpose(1, 0, 2)
    all_tokens = lax.all_gather(tokens, "stream", axis=0, tiled=True)
    weights = lax.all_to_all(weights, "stream", split_axis=0, concat_axis=0, tiled=True)
    weights = ring_gather(ring_gather(weights, "tm_1"), "tm_0")
    weights = weights.transpose(2, 0, 1, 3, 4).reshape(streams * shares * rows, WIDE)

    raw = jnp.dot(all_tokens, weights, preferred_element_type=f32)
    block_rows = raw.shape[0]
    gates = jnp.stack(
        [
            lax.dynamic_index_in_dim(decay_rate, head, 0, False),
            lax.dynamic_index_in_dim(beta_bias, head, 0, False),
        ]
    )
    reach, own, total = pl.pallas_call(
        chunk_kernel,
        out_shape=(
            jax.ShapeDtypeStruct((block_rows, DK), bf16),
            jax.ShapeDtypeStruct((block_rows, DV), f32),
            jax.ShapeDtypeStruct((DK + DV, DK), f32),
        ),
        in_specs=[smem, vmem],
        out_specs=(vmem, vmem, vmem),
        compiler_params=pltpu.CompilerParams(vmem_limit_bytes=48 * 2**20),
    )(gates, raw)

    place = jnp.stack([at_x * 2 + at_c, at_c, at_y]).astype(jnp.int32)
    mine = lax.all_gather(total, "tm_1", axis=0)
    other = lax.ppermute(mine, "tm_2", [(0, 1), (1, 0)])
    prefix, subtotal = pl.pallas_call(
        join_kernel,
        out_shape=(jax.ShapeDtypeStruct((DK + DV, DK), f32),) * 2,
        in_specs=[smem, vmem, vmem],
        out_specs=(vmem, vmem),
    )(place, mine, other)
    outer = lax.all_gather(subtotal, "tm_0", axis=0)
    readout = pl.pallas_call(
        read_kernel,
        out_shape=jax.ShapeDtypeStruct((block_rows, DV), bf16),
        in_specs=[smem, vmem, vmem, vmem, vmem],
        out_specs=vmem,
        compiler_params=pltpu.CompilerParams(vmem_limit_bytes=32 * 2**20),
    )(place, outer, prefix, reach, own)
    returned = lax.all_to_all(readout, "stream", split_axis=0, concat_axis=1, tiled=True)
    head_read = returned.reshape(local_rows, HEADS, DV).astype(f32)
    normed = (
        head_read
        * lax.rsqrt(jnp.mean(head_read * head_read, -1, keepdims=True) + 1e-06)
        * norm_gain
    )
    return normed.reshape(local_rows, HEADS * DV).astype(bf16)


def solution(mesh):
    finer = Mesh(
        mesh.devices.reshape(4, 4, 2, mesh.shape["stream"]), ("tm_0", "tm_1", "tm_2", "stream")
    )
    return jax.shard_map(
        shards,
        mesh=finer,
        in_specs=(
            P(TM_STREAM, None),
            P("stream", None),
            P("stream", None),
            P("stream", None),
            P("stream", None),
            P("stream", None),
            P(),
            P(),
            P(),
        ),
        out_specs=P(TM_STREAM, None),
        check_vma=False,
    )
```

time: 719 us -> 224 us (0.31)
  the two profiles are of different devices: /device:TPU:34 before, /device:TPU:66 now
where the time goes in v1:
time: 224 us; the launch traced here: 223 us
  waiting for transfers between devices  93.7 us (42%)
  starting transfers between devices  48.6 us (22%)
  blocking collectives  27.1 us (12%)
  Pallas kernels  17.6 us (8%)
  between operations  13.6 us (6%)
  local copies, waits for them, and re-layouts  11.5 us (5%)
  matrix products  7.54 us (3%)
  other arithmetic  3.49 us (2%)
    all_gather x1, waiting for transfers between devices, shards(): all_tokens = lax.all_gather(tokens, 'stream', axis=0, tiled=True)  37.4 us
    all_to_all x1, waiting for transfers between devices, shards(): lax.all_to_all(readout, 'stream', split_axis=0, concat_axis=1, tiled=True)  27.6 us
    ppermute x6, starting transfers between devices, ring_gather(): lax.ppermute(x, axis, [(i, (i + shift) % size) for i in range(size)])  22 us
    all_to_all x1, starting transfers between devices, shards(): lax.all_to_all(weights, 'stream', split_axis=0, concat_axis=0, tiled=True)  14.8 us
    all_gather x1, blocking collectives, shards(): outer = lax.all_gather(subtotal, 'tm_0', axis=0)  13.6 us
    all_to_all x1, waiting for transfers between devices, shards(): lax.all_to_all(weights, 'stream', split_axis=0, concat_axis=0, tiled=True)  13.5 us
    all_gather x1, blocking collectives, shards(): mine = lax.all_gather(total, 'tm_1', axis=0)  13.4 us
    ppermute x6, waiting for transfers between devices, ring_gather(): lax.ppermute(x, axis, [(i, (i + shift) % size) for i in range(size)])  13.2 us
  transfers between devices with their start and end apart: 10, of which 9 were waited for; matrix products, arithmetic and copies ran while one was open for 5% of the time, Pallas kernels for 0%

profile of v1, /device:TPU:66, one launch (start us, length us, event | category | flops | bytes accessed | tf_op | source)
XLA Modules:
  0.0 223.0 jit_solution(12567094745550736263)
XLA Ops:
  6.5 0.0 copy-start
  6.5 0.7 all-gather.4.cloned.1.call-update
  7.3 0.8 constant_dynamic-slice_fusion
  8.1 0.1 copy.29
  8.1 0.1 copy.18
  8.3 0.1 copy.30
  8.4 0.1 copy.19
  8.6 0.8 dynamic-slice_bitcast_fusion
  9.4 0.8 concatenate.3
  10.1 14.8 %all-to-all-start = ((bf16[16,8,512]{2,1,0:T(8,128)(2,1)}), bf16[16,8,512]{2,1,0:T(8,128)(2,1)S(1)}, u32[]{:S(2)}, u32[]{:S(2)}) async-start(bf16[16,8,512]{2,1,0:T(8,128)(2,1)} %bitcast.8), calls=%async_computation | async-start | bytes 262144 | tf_op jit(solution)/shard_map/all_to_all | solution.py:190
  24.9 13.5 %all-to-all-done = bf16[16,8,512]{2,1,0:T(8,128)(2,1)S(1)} async-done(((bf16[16,8,512]{2,1,0:T(8,128)(2,1)}), bf16[16,8,512]{2,1,0:T(8,128)(2,1)S(1)}, u32[]{:S(2)}, u32[]{:S(2)}) %all-to-all-start) | async-done | bytes 131104 | tf_op jit(solution)/shard_map/all_to_all | solution.py:190
  38.4 3.4 %collective-permute-start = (bf16[16,8,512]{2,1,0:T(8,128)(2,1)S(1)}, bf16[16,8,512]{2,1,0:T(8,128)(2,1)S(1)}, u32[]{:S(2)}, u32[]{:S(2)}) collective-permute-start(bf16[16,8,512]{2,1,0:T(8,128)(2,1)S(1)} %all-to-all-done), channel_id=1, source_target_pairs={{0,32},{32,64},{64,96},{96,0},{1,33},{33,65},{65,97},{97,1},{2,34}... | collective-permute-start | bytes 393224 | tf_op jit(solution)/shard_map/ppermute | solution.py:156
  41.8 3.0 %collective-permute-start.1 = (bf16[16,8,512]{2,1,0:T(8,128)(2,1)S(1)}, bf16[16,8,512]{2,1,0:T(8,128)(2,1)S(1)}, u32[]{:S(2)}, u32[]{:S(2)}) collective-permute-start(bf16[16,8,512]{2,1,0:T(8,128)(2,1)S(1)} %all-to-all-done), channel_id=1, source_target_pairs={{0,64},{32,96},{64,0},{96,32},{1,65},{33,97},{65,1},{97,33},{2,66}... | collective-permute-start | bytes 393224 | tf_op jit(solution)/shard_map/ppermute | solution.py:156
  44.9 4.1 %collective-permute-start.2 = (bf16[16,8,512]{2,1,0:T(8,128)(2,1)S(1)}, bf16[16,8,512]{2,1,0:T(8,128)(2,1)S(1)}, u32[]{:S(2)}, u32[]{:S(2)}) collective-permute-start(bf16[16,8,512]{2,1,0:T(8,128)(2,1)S(1)} %all-to-all-done), channel_id=1, source_target_pairs={{0,96},{32,0},{64,32},{96,64},{1,97},{33,1},{65,33},{97,65},{2,98}... | collective-permute-start | bytes 393224 | tf_op jit(solution)/shard_map/ppermute | solution.py:156
  49.0 0.0 collective-permute-done
  49.0 1.2 collective-permute-done.1
  50.2 1.5 collective-permute-done.2
  51.7 3.5 %collective-permute-start.3 = (bf16[4,16,8,512]{3,2,0,1:T(8,128)(2,1)S(1)}, bf16[4,16,8,512]{3,2,0,1:T(8,128)(2,1)S(1)}, u32[]{:S(2)}, u32[]{:S(2)}) collective-permute-start(bf16[4,16,8,512]{3,2,0,1:T(8,128)(2,1)S(1)} %bitcast_dynamic-update-slice_fusion.7), channel_id=1, source_target_pairs={{0,128},{128,256},{256,384},{384,0},{1,129},{129,257},{257,385},{3... | collective-permute-start | bytes 1572872 | tf_op jit(solution)/shard_map/ppermute | solution.py:156
  55.2 0.6 dynamic_slice.22
  55.9 0.6 dynamic_slice.23
  56.4 4.8 %collective-permute-start.4 = (bf16[4,16,8,512]{3,2,0,1:T(8,128)(2,1)S(1)}, bf16[4,16,8,512]{3,2,0,1:T(8,128)(2,1)S(1)}, u32[]{:S(2)}, u32[]{:S(2)}) collective-permute-start(bf16[4,16,8,512]{3,2,0,1:T(8,128)(2,1)S(1)} %bitcast_dynamic-update-slice_fusion.7), channel_id=1, source_target_pairs={{0,256},{128,384},{256,0},{384,128},{1,257},{129,385},{257,1},{385... | collective-permute-start | bytes 1572872 | tf_op jit(solution)/shard_map/ppermute | solution.py:156
  61.2 1.4 pad_maximum_fusion.gate_ref
  62.6 3.2 %collective-permute-start.5 = (bf16[4,16,8,512]{3,2,0,1:T(8,128)(2,1)S(1)}, bf16[4,16,8,512]{3,2,0,1:T(8,128)(2,1)S(1)}, u32[]{:S(2)}, u32[]{:S(2)}) collective-permute-start(bf16[4,16,8,512]{3,2,0,1:T(8,128)(2,1)S(1)} %bitcast_dynamic-update-slice_fusion.7), channel_id=1, source_target_pairs={{0,384},{128,0},{256,128},{384,256},{1,385},{129,1},{257,129},{385... | collective-permute-start | bytes 1572872 | tf_op jit(solution)/shard_map/ppermute | solution.py:156
  65.9 1.7 broadcast_in_dim.37
  67.5 0.8 bitcast_dynamic-update-slice_fusion.2
  68.3 0.3 collective-permute-done.3
  68.6 0.9 bitcast_dynamic-update-slice_fusion.1
  69.5 8.6 %collective-permute-done.4 = bf16[4,16,8,512]{3,2,0,1:T(8,128)(2,1)S(1)} collective-permute-done((bf16[4,16,8,512]{3,2,0,1:T(8,128)(2,1)S(1)}, bf16[4,16,8,512]{3,2,0,1:T(8,128)(2,1)S(1)}, u32[]{:S(2)}, u32[]{:S(2)}) %collective-permute-start.4) | collective-permute-done | bytes 524320 | tf_op jit(solution)/shard_map/ppermute | solution.py:156
  78.0 0.8 bitcast_dynamic-update-slice_fusion
  78.8 1.7 collective-permute-done.5
  80.6 0.8 bitcast_dynamic-update-slice_fusion.3
  81.4 37.4 %all-gather.4.cloned.1.call-done = bf16[2048,2048]{1,0:T(8,128)(2,1)} async-done(((bf16[128,2048]{1,0:T(8,128)(2,1)}), bf16[2048,2048]{1,0:T(8,128)(2,1)}) %all-gather.4.cloned.1.call-update) | async-done | bytes 8388624 | tf_op jit(solution)/shard_map/all_gather | solution.py:189
  118.8 7.5 %convolution_bitcast_fusion.raw_ref = f32[2048,512]{1,0:T(8,128)S(1)} fusion(bf16[2048,2048]{1,0:T(8,128)(2,1)} %all-gather.4.cloned.1.call-done, bf16[2048,512]{1,0:T(8,128)(2,1)} %bitcast.24), kind=kOutput, calls=%fused_computation | convolution fusion | flops 4294967296 | bytes 14680064 | tf_op jit(solution)/shard_map/dot_general | solution.py:194
  126.3 10.5 %shard_map.91 = (bf16[2048,128]{1,0:T(8,128)(2,1)S(1)}, f32[2048,128]{1,0:T(8,128)S(1)}, f32[256,128]{1,0:T(8,128)S(1)}) custom-call(f32[2]{0:T(128)S(1)} %pad_maximum_fusion.gate_ref, f32[2048,512]{1,0:T(8,128)S(1)} %convolution_bitcast_fusion.raw_ref), custom_call_target="tpu_custom_call" | custom-call | tf_op jit(solution)/shard_map/pallas_call | solution.py:202
  136.8 13.4 %all-gather = f32[1024,128]{1,0:T(8,128)S(1)} all-gather(f32[256,128]{1,0:T(8,128)S(1)} %get-tuple-element.10), channel_id=2, replica_groups=mesh['tm_0'=4,'tm_1'=4,'tm_2'=2,'stream'=16] {'tm_1'}, dimensions={0}, use_global_device_ids=true | all-gather | bytes 655360 | tf_op jit(solution)/shard_map/all_gather | solution.py:215
  150.3 1.9 collective-permute-start.6
  152.2 0.6 pad_add_fusion.place_ref
  152.8 1.2 collective-permute-done.6.other_ref
  154.1 0.8 copy-done.4
  154.9 4.6 %shard_map.92 = (f32[256,128]{1,0:T(8,128)}, f32[256,128]{1,0:T(8,128)}) custom-call(s32[3]{0:T(128)} %pad_add_fusion.place_ref, f32[4,256,128]{2,1,0:T(8,128)} %bitcast.70, f32[4,256,128]{2,1,0:T(8,128)} %copy-done.4), custom_call_target="tpu_custom_call" | custom-call | tf_op jit(solution)/shard_map/pallas_call | solution.py:217
  159.5 13.6 %all-gather.1 = f32[1024,128]{1,0:T(8,128)S(1)} all-gather(f32[256,128]{1,0:T(8,128)} %get-tuple-element.11), channel_id=3, replica_groups=mesh['tm_0'=4,'tm_1'=4,'tm_2'=2,'stream'=16] {'tm_0'}, dimensions={0}, use_global_device_ids=true | all-gather | bytes 655360 | tf_op jit(solution)/shard_map/all_gather | solution.py:223
  173.1 0.9 copy-done.1
  174.0 0.7 copy-done.2
  174.7 2.5 %shard_map.93 = bf16[2048,128]{1,0:T(8,128)(2,1)} custom-call(s32[3]{0:T(128)S(1)} %copy-done.2, f32[4,256,128]{2,1,0:T(8,128)S(1)} %bitcast.68, f32[256,128]{1,0:T(8,128)S(1)} %copy-done.1, bf16[2048,128]{1,0:T(8,128)(2,1)S(1)} %get-tuple-element.13.reach_ref, f32[2048,128]{1,0:T(8,128)S(1)} %get-tuple-element.14.own_ref), custom_call_target="tpu_custom_call" | custom-call | tf_op jit(solution)/shard_map/pallas_call | solution.py:224
  177.2 9.9 %all-to-all-start.1 = ((bf16[16,128,128]{2,1,0:T(8,128)(2,1)}), bf16[16,128,128]{2,1,0:T(8,128)(2,1)S(1)}, u32[]{:S(2)}, u32[]{:S(2)}) async-start(bf16[16,128,128]{2,1,0:T(8,128)(2,1)} %bitcast.28), calls=%async_computation.1 | async-start | bytes 1048576 | tf_op jit(solution)/shard_map/all_to_all | solution.py:231
  187.1 27.6 %all-to-all-done.1 = bf16[16,128,128]{2,1,0:T(8,128)(2,1)S(1)} async-done(((bf16[16,128,128]{2,1,0:T(8,128)(2,1)}), bf16[16,128,128]{2,1,0:T(8,128)(2,1)S(1)}, u32[]{:S(2)}, u32[]{:S(2)}) %all-to-all-start.1) | async-done | bytes 524320 | tf_op jit(solution)/shard_map/all_to_all | solution.py:231
  214.7 0.3 fusion.2
  215.0 1.1 fusion.3
  (22 shorter events, 0.2 us)
Async XLA Ops:
  6.5 2.0 copy-start
  6.5 48.7 %copy-start.6 = (f32[16]{0:T(128)S(1)}, f32[16]{0:T(128)}, u32[]{:S(2)}) copy-start(f32[16]{0:T(128)} %param.15) | copy-start | bytes 196
  6.5 49.3 %copy-start.7 = (f32[16]{0:T(128)S(1)}, f32[16]{0:T(128)}, u32[]{:S(2)}) copy-start(f32[16]{0:T(128)} %param.16) | copy-start | bytes 196
  6.5 112.2 %all-gather.4.cloned.1.call-start = ((), (), s32[]{:S(2)}) async-start(), calls=%async_computation.2 | async-start | bytes 8912896 | tf_op jit(solution)/shard_map/all_gather | solution.py:189
  10.1 28.3 %all-to-all-start = ((bf16[16,8,512]{2,1,0:T(8,128)(2,1)}), bf16[16,8,512]{2,1,0:T(8,128)(2,1)S(1)}, u32[]{:S(2)}, u32[]{:S(2)}) async-start(bf16[16,8,512]{2,1,0:T(8,128)(2,1)} %bitcast.8), calls=%async_computation | async-start | bytes 262144 | tf_op jit(solution)/shard_map/all_to_all | solution.py:190
  38.4 10.6 %collective-permute-start = (bf16[16,8,512]{2,1,0:T(8,128)(2,1)S(1)}, bf16[16,8,512]{2,1,0:T(8,128)(2,1)S(1)}, u32[]{:S(2)}, u32[]{:S(2)}) collective-permute-start(bf16[16,8,512]{2,1,0:T(8,128)(2,1)S(1)} %all-to-all-done), channel_id=1, source_target_pairs={{0,32},{32,64},{64,96},{96,0},{1,33},{33,65},{65,97},{97,1},{2,34}... | collective-permute-start | bytes 393224 | tf_op jit(solution)/shard_map/ppermute | solution.py:156
  41.8 8.4 %collective-permute-start.1 = (bf16[16,8,512]{2,1,0:T(8,128)(2,1)S(1)}, bf16[16,8,512]{2,1,0:T(8,128)(2,1)S(1)}, u32[]{:S(2)}, u32[]{:S(2)}) collective-permute-start(bf16[16,8,512]{2,1,0:T(8,128)(2,1)S(1)} %all-to-all-done), channel_id=1, source_target_pairs={{0,64},{32,96},{64,0},{96,32},{1,65},{33,97},{65,1},{97,33},{2,66}... | collective-permute-start | bytes 393224 | tf_op jit(solution)/shard_map/ppermute | solution.py:156
  44.9 6.9 %collective-permute-start.2 = (bf16[16,8,512]{2,1,0:T(8,128)(2,1)S(1)}, bf16[16,8,512]{2,1,0:T(8,128)(2,1)S(1)}, u32[]{:S(2)}, u32[]{:S(2)}) collective-permute-start(bf16[16,8,512]{2,1,0:T(8,128)(2,1)S(1)} %all-to-all-done), channel_id=1, source_target_pairs={{0,96},{32,0},{64,32},{96,64},{1,97},{33,1},{65,33},{97,65},{2,98}... | collective-permute-start | bytes 393224 | tf_op jit(solution)/shard_map/ppermute | solution.py:156
  51.7 16.9 %collective-permute-start.3 = (bf16[4,16,8,512]{3,2,0,1:T(8,128)(2,1)S(1)}, bf16[4,16,8,512]{3,2,0,1:T(8,128)(2,1)S(1)}, u32[]{:S(2)}, u32[]{:S(2)}) collective-permute-start(bf16[4,16,8,512]{3,2,0,1:T(8,128)(2,1)S(1)} %bitcast_dynamic-update-slice_fusion.7), channel_id=1, source_target_pairs={{0,128},{128,256},{256,384},{384,0},{1,129},{129,257},{257,385},{3... | collective-permute-start | bytes 1572872 | tf_op jit(solution)/shard_map/ppermute | solution.py:156
  56.4 21.6 %collective-permute-start.4 = (bf16[4,16,8,512]{3,2,0,1:T(8,128)(2,1)S(1)}, bf16[4,16,8,512]{3,2,0,1:T(8,128)(2,1)S(1)}, u32[]{:S(2)}, u32[]{:S(2)}) collective-permute-start(bf16[4,16,8,512]{3,2,0,1:T(8,128)(2,1)S(1)} %bitcast_dynamic-update-slice_fusion.7), channel_id=1, source_target_pairs={{0,256},{128,384},{256,0},{384,128},{1,257},{129,385},{257,1},{385... | collective-permute-start | bytes 1572872 | tf_op jit(solution)/shard_map/ppermute | solution.py:156
  62.6 18.0 %collective-permute-start.5 = (bf16[4,16,8,512]{3,2,0,1:T(8,128)(2,1)S(1)}, bf16[4,16,8,512]{3,2,0,1:T(8,128)(2,1)S(1)}, u32[]{:S(2)}, u32[]{:S(2)}) collective-permute-start(bf16[4,16,8,512]{3,2,0,1:T(8,128)(2,1)S(1)} %bitcast_dynamic-update-slice_fusion.7), channel_id=1, source_target_pairs={{0,384},{128,0},{256,128},{384,256},{1,385},{129,1},{257,129},{385... | collective-permute-start | bytes 1572872 | tf_op jit(solution)/shard_map/ppermute | solution.py:156
  150.3 3.8 %copy-start.3 = (f32[1024,128]{1,0:T(8,128)}, f32[1024,128]{1,0:T(8,128)S(1)}, u32[]{:S(2)}) copy-start(f32[1024,128]{1,0:T(8,128)S(1)} %all-gather) | copy-start | bytes 1572868
  150.3 3.8 %collective-permute-start.6 = (f32[4,256,128]{2,1,0:T(8,128)S(1)}, f32[4,256,128]{2,1,0:T(8,128)S(1)}, u32[]{:S(2)}, u32[]{:S(2)}) collective-permute-start(f32[4,256,128]{2,1,0:T(8,128)S(1)} %bitcast.69), channel_id=1, source_target_pairs={{0,16},{16,0},{1,17},{17,1},{2,18},{18,2},{3,19},{19,3},{4,20},{20... | collective-permute-start | bytes 1572872 | tf_op jit(solution)/shard_map/ppermute | solution.py:216
  154.1 0.8 copy-start.4
  159.5 27.6 %copy-start.5 = (f32[128]{0:T(128)S(1)}, f32[128]{0:T(128)}, u32[]{:S(2)}) copy-start(f32[128]{0:T(128)} %param.17) | copy-start | bytes 1540
  173.1 0.9 copy-start.1
  174.0 0.7 copy-start.2
  177.2 37.5 %all-to-all-start.1 = ((bf16[16,128,128]{2,1,0:T(8,128)(2,1)}), bf16[16,128,128]{2,1,0:T(8,128)(2,1)S(1)}, u32[]{:S(2)}, u32[]{:S(2)}) async-start(bf16[16,128,128]{2,1,0:T(8,128)(2,1)} %bitcast.28), calls=%async_computation.1 | async-start | bytes 1048576 | tf_op jit(solution)/shard_map/all_to_all | solution.py:231
Sparse Core Ops, SparseCore 0:
  9.4 109.2 all-gather.3

commit v2 on v1

v2 whole, which is shorter than its diff:
```python
import jax
import jax.numpy as jnp
from jax import lax
from jax.experimental import pallas as pl
from jax.experimental.pallas import tpu as pltpu
from jax.sharding import Mesh
from jax.sharding import PartitionSpec as P

HEADS = 16
DK = 128
DV = 128
CHUNK = 128
GANG = 8
SIDE = 4
MAP_ROWS = 272
SPLIT = ("tm_0", "tm_1", "tm_2", "zh", "zl")
STREAM = ("zh", "zl")
f32 = jnp.float32
bf16 = jnp.bfloat16


def mm(a, b, ca=1, cb=0):
    return lax.dot_general(
        a.astype(bf16), b.astype(bf16), (((ca,), (cb,)), ((), ())), preferred_element_type=f32
    )


def mm_exact(a, b, ca=1, cb=0):
    return lax.dot_general(
        a, b, (((ca,), (cb,)), ((), ())), precision=lax.Precision.HIGHEST, preferred_element_type=f32
    )


def chunk_kernel(gate_ref, *refs):
    raw_refs, (logit_ref, reach_ref, own_ref, total_ref) = refs[:SIDE], refs[SIDE:]
    chunks = raw_refs[0].shape[0] // CHUNK
    row = lax.broadcasted_iota(jnp.int32, (CHUNK, CHUNK), 0)
    col = lax.broadcasted_iota(jnp.int32, (CHUNK, CHUNK), 1)
    strict, inclusive = row > col, row >= col
    eye = jnp.where(row == col, 1.0, 0.0).astype(f32)
    ones_below = jnp.where(inclusive, 1.0, 0.0).astype(bf16)

    def below(size):
        return (
            (row // (2 * size) == col // (2 * size))
            & ((row // size) % 2 == 1)
            & ((col // size) % 2 == 0)
        )

    for step in range(SIDE * chunks // GANG):
        units = [divmod(step * GANG + i, chunks) for i in range(GANG)]
        starts = [j * CHUNK for _, j in units]
        each = range(GANG)
        q, k, v, beta, grow, scale_row, beta_row, tail, last, decay = ([] for _ in range(10))
        for i in each:
            raw_ref, mine = raw_refs[units[i][0]], units[i][0]
            rate, bias = gate_ref[2 * mine], gate_ref[2 * mine + 1]
            raw_q = raw_ref[pl.ds(starts[i], CHUNK), 0:128]
            raw_k = raw_ref[pl.ds(starts[i], CHUNK), 128:256]
            raw_v = raw_ref[pl.ds(starts[i], CHUNK), 256:384]
            logits = logit_ref[pl.ds(starts[i], CHUNK), :]
            q.append(
                (
                    raw_q
                    * lax.rsqrt(jnp.sum(raw_q * raw_q, -1, keepdims=True) + 1e-06)
                    * DK ** (-0.5)
                ).astype(bf16)
            )
            k.append(
                (raw_k * lax.rsqrt(jnp.sum(raw_k * raw_k, -1, keepdims=True) + 1e-06)).astype(bf16)
            )
            v.append(raw_v.astype(bf16))
            x = logits[:, 2 * mine : 2 * mine + 1]
            softplus = jnp.maximum(x, 0.0) + jnp.log1p(jnp.exp(-jnp.abs(x)))
            log_decay = (-rate * softplus).astype(bf16)
            strength = (1.0 / (1.0 + jnp.exp(-(logits[:, 2 * mine + 1 : 2 * mine + 2] + bias)))).astype(bf16).astype(f32)
            g = mm(ones_below, jnp.broadcast_to(log_decay, (CHUNK, CHUNK)))
            b = jnp.broadcast_to(strength, (CHUNK, CHUNK))
            turned = jnp.where(col < 64, g, b).T
            g_row, b_row = turned[0:1, :], turned[64:65, :]
            g_last = g_row[:, CHUNK - 1 : CHUNK]
            beta.append(b)
            grow.append(jnp.exp(g))
            beta_row.append(b_row)
            scale_row.append(b_row * jnp.exp(g_row))
            tail.append(jnp.exp(g_last - g))
            last.append(jnp.exp(g_last))
            decay.append(jnp.exp(jnp.where(inclusive, g - g_row, 0.0)))
        both = [mm(jnp.concatenate([q[i], k[i]], 0), k[i], 1, 1) for i in each]
        scores = [jnp.where(inclusive, both[i][:CHUNK] * decay[i], 0.0) for i in each]
        lower = [jnp.where(strict, beta[i] * decay[i] * both[i][CHUNK:], 0.0) for i in each]
        inverse = [eye - jnp.where(below(1), lower[i], 0.0) for i in each]
        for size in (2, 4, 8, 16, 32, 64):
            mask = below(size)
            inner = [mm(jnp.where(mask, lower[i], 0.0), inverse[i]) for i in each]
            inverse = [inverse[i] - mm(inverse[i], inner[i]) for i in each]
        rounded = [inverse[i].astype(bf16) for i in each]
        high = [lower[i].astype(bf16) for i in each]
        low = [(lower[i] - high[i].astype(f32)).astype(bf16) for i in each]
        rest = [
            eye - rounded[i].astype(f32) - mm(high[i], rounded[i]) - mm(low[i], rounded[i])
            for i in each
        ]
        inverse = [rounded[i].astype(f32) + mm(rounded[i], rest[i]) for i in each]
        w = [mm(inverse[i] * scale_row[i], k[i]) for i in each]
        u = [mm(inverse[i] * beta_row[i], v[i]) for i in each]
        wu = [jnp.concatenate([w[i], u[i]], 1) for i in each]
        tail2 = [jnp.concatenate([tail[i], tail[i]], 1) for i in each]
        change = [mm(wu[i] * tail2[i], k[i], 0, 0) for i in each]
        inside = [mm(scores[i], wu[i]) for i in each]
        reach = [grow[i] * q[i].astype(f32) - inside[i][:, :DK] for i in each]
        for i in each:
            mine, j = units[i]
            if j == 0:
                state = jnp.concatenate([eye, jnp.zeros((DV, DK), f32)], 0)
                kept = jnp.ones((1, 1), f32)
            out = mm(reach[i], state, 1, 1)
            reach_ref[mine, pl.ds(starts[i], CHUNK), :] = out[:, :DK].astype(bf16)
            own_ref[mine, pl.ds(starts[i], CHUNK), :] = out[:, DK:] + inside[i][:, DK:]
            moved = mm(state, change[i][:DK])
            state = last[i] * state - moved
            state = jnp.concatenate([state[:DK], state[DK:] + change[i][DK:]], 0)
            kept = kept * last[i]
            if j == chunks - 1:
                part = kept.astype(bf16).astype(f32)
                total_ref[mine, 0:DK, :] = (state[:DK] - kept * eye).astype(bf16)
                total_ref[mine, DK : DK + DV, :] = state[DK:].astype(bf16)
                total_ref[mine, DK + DV :, :] = jnp.concatenate(
                    [jnp.broadcast_to(part, (8, DK)), jnp.broadcast_to(kept - part, (8, DK))], 0
                ).astype(bf16)


def widen_map(packed, eye):
    kept = packed[DK + DV : DK + DV + 1].astype(f32) + packed[DK + DV + 8 : DK + DV + 9].astype(f32)
    return packed[:DK].astype(f32) + kept * eye, packed[DK : DK + DV].astype(f32)


def group_kernel(place_ref, *refs):
    part_refs, (prefix_ref, total_ref) = refs[:SIDE], refs[SIDE:]
    zh = place_ref[3]
    row = lax.broadcasted_iota(jnp.int32, (DK + DV, DK), 0)
    col = lax.broadcasted_iota(jnp.int32, (DK + DV, DK), 1)
    state = jnp.where(row == col, 1.0, 0.0).astype(f32)
    eye = state[:DK]
    for j in range(SIDE):
        prefix_ref[j] = state
        packed = part_refs[0][...]
        for shift in range(1, SIDE):
            packed = jnp.where(lax.rem(zh - shift + SIDE, SIDE) == j, part_refs[shift][...], packed)
        step, added = widen_map(packed, eye)
        moved = mm_exact(state, step)
        state = jnp.concatenate([moved[:DK], moved[DK:] + added], 0)
    total_ref[...] = state


def join_kernel(place_ref, mine_ref, other_ref, prefix_ref, total_ref):
    place, core = place_ref[0], place_ref[1]
    row = lax.broadcasted_iota(jnp.int32, (DK + DV, DK), 0)
    col = lax.broadcasted_iota(jnp.int32, (DK + DV, DK), 1)
    state = jnp.where(row == col, 1.0, 0.0).astype(f32)
    prefix_ref[...] = state
    for j in range(8):
        piece = jnp.where(core == j % 2, mine_ref[j // 2], other_ref[j // 2])
        moved = mm_exact(state, piece[:DK])
        state = jnp.concatenate([moved[:DK], moved[DK:] + piece[DK:]], 0)

        @pl.when(place == j + 1)
        def _():
            prefix_ref[...] = state

    total_ref[...] = state


def state_kernel(place_ref, outer_ref, prefix_ref, inner_ref, state_ref):
    place = place_ref[2]
    state = jnp.zeros((DV, DK), f32)
    for j in range(3):
        moved = mm_exact(state, outer_ref[j, :DK]) + outer_ref[j, DK:]
        state = jnp.where(j < place, moved, state)
    state = mm_exact(state, prefix_ref[:DK]) + prefix_ref[DK:]
    for j in range(SIDE):
        state_ref[j] = (mm_exact(state, inner_ref[j, :DK]) + inner_ref[j, DK:]).astype(bf16)


def read_kernel(place_ref, *refs):
    state_refs, (reach_ref, own_ref, read_ref) = refs[:SIDE], refs[SIDE:]
    at_y, zh = place_ref[2], place_ref[3]
    for k in range(SIDE):
        head = lax.rem(at_y - k + SIDE, SIDE)
        state = state_refs[0][...]
        for shift in range(1, SIDE):
            state = jnp.where(lax.rem(zh - shift + SIDE, SIDE) == head, state_refs[shift][...], state)
        read_ref[head] = (mm(reach_ref[k], state, 1, 1) + own_ref[k]).astype(bf16)


def shifted(x, axis, shift):
    size = lax.axis_size(axis)
    return lax.ppermute(x, axis, [(i, (i + shift) % size) for i in range(size)])


def ring_gather(x, axis):
    size, me = lax.axis_size(axis), lax.axis_index(axis)
    out = jnp.zeros((size,) + x.shape, x.dtype)
    for shift in range(size):
        piece = shifted(x, axis, shift) if shift else x
        out = lax.dynamic_update_index_in_dim(out, piece, lax.rem(me - shift + size, size), 0)
    return out


def shards(
    tokens, w_query, w_key, w_value, decay_proj, beta_proj, decay_rate, beta_bias, norm_gain
):
    local_rows = tokens.shape[0]
    at_y, at_x, at_c = lax.axis_index("tm_0"), lax.axis_index("tm_1"), lax.axis_index("tm_2")
    zh, zl = lax.axis_index("zh"), lax.axis_index("zl")
    vmem = pl.BlockSpec(memory_space=pltpu.VMEM)
    smem = pl.BlockSpec(memory_space=pltpu.SMEM)

    rows = w_query.shape[0] // 8
    first = (at_x * 2 + at_c) * rows

    def share(w):
        w = lax.dynamic_slice_in_dim(w, first, rows, 0).reshape(rows, SIDE, SIDE, DK)
        return lax.dynamic_index_in_dim(w, at_y, 2, False)

    weights = jnp.concatenate([share(w_query), share(w_key), share(w_value)], -1).transpose(1, 0, 2)
    run = lax.all_gather(tokens, "zl", axis=0, tiled=True)
    weights = lax.all_to_all(weights, "zl", split_axis=0, concat_axis=0, tiled=True)
    weights = ring_gather(weights, "zh")
    weights = ring_gather(weights, "tm_1")
    gates = jnp.concatenate([decay_proj, beta_proj], 1)
    gates = lax.all_gather(gates, "zl", axis=0, tiled=True)
    gates = lax.all_gather(gates, "zh", axis=0, tiled=True)
    heads = zl * SIDE + jnp.remainder(at_y - jnp.arange(SIDE), SIDE)
    wanted = jnp.stack([heads, heads + HEADS], 1).reshape(2 * SIDE)
    wanted = jnp.concatenate([wanted, jnp.full((128 - 2 * SIDE,), -1, wanted.dtype)])
    pick = (jnp.arange(2 * HEADS)[:, None] == wanted[None, :]).astype(bf16)
    gates = jnp.dot(gates, pick, preferred_element_type=f32).astype(bf16)
    logits = jnp.dot(run, gates, preferred_element_type=f32)
    both = jnp.concatenate([decay_rate, beta_bias])
    levels = jnp.sum(jnp.where(pick > 0, both[:, None], 0.0), 0)[: 2 * SIDE]

    raws = []
    for k in range(SIDE):
        own = shifted(weights, "tm_0", k) if k else weights
        other = shifted(own, "tm_2", 1)
        pair = jnp.stack([jnp.where(at_c == 0, own, other), jnp.where(at_c == 0, other, own)])
        matrix = pair.transpose(2, 3, 1, 0, 4, 5).reshape(tokens.shape[1], 3 * DK)
        raws.append(jnp.dot(run, matrix, preferred_element_type=f32))
    run_rows = run.shape[0]
    reach, own, total = pl.pallas_call(
        chunk_kernel,
        out_shape=(
            jax.ShapeDtypeStruct((SIDE, run_rows, DK), bf16),
            jax.ShapeDtypeStruct((SIDE, run_rows, DV), f32),
            jax.ShapeDtypeStruct((SIDE, MAP_ROWS, DK), bf16),
        ),
        in_specs=[smem] + [vmem] * 5,
        out_specs=(vmem, vmem, vmem),
        compiler_params=pltpu.CompilerParams(vmem_limit_bytes=48 * 2**20),
    )(levels, *raws, logits)

    place = jnp.stack([at_x * 2 + at_c, at_c, at_y, zh]).astype(jnp.int32)
    parts = []
    for shift in range(SIDE):
        sent = lax.dynamic_index_in_dim(total, jnp.remainder(at_y - zh - shift, SIDE), 0, False)
        parts.append(shifted(sent, "zh", shift) if shift else sent)
    inner, block = pl.pallas_call(
        group_kernel,
        out_shape=(
            jax.ShapeDtypeStruct((SIDE, DK + DV, DK), f32),
            jax.ShapeDtypeStruct((DK + DV, DK), f32),
        ),
        in_specs=[smem] + [vmem] * SIDE,
        out_specs=(vmem, vmem),
    )(place, *parts)
    mine = lax.all_gather(block, "tm_1", axis=0)
    other = lax.ppermute(mine, "tm_2", [(0, 1), (1, 0)])
    prefix, subtotal = pl.pallas_call(
        join_kernel,
        out_shape=(jax.ShapeDtypeStruct((DK + DV, DK), f32),) * 2,
        in_specs=[smem, vmem, vmem],
        out_specs=(vmem, vmem),
    )(place, mine, other)
    outer = lax.all_gather(subtotal, "tm_0", axis=0)
    states = pl.pallas_call(
        state_kernel,
        out_shape=jax.ShapeDtypeStruct((SIDE, DV, DK), bf16),
        in_specs=[smem] + [vmem] * 3,
        out_specs=vmem,
    )(place, outer, prefix, inner)
    arrived = []
    for shift in range(SIDE):
        sent = lax.dynamic_index_in_dim(states, jnp.remainder(zh + shift, SIDE), 0, False)
        arrived.append(shifted(sent, "zh", shift) if shift else sent)
    readout = pl.pallas_call(
        read_kernel,
        out_shape=jax.ShapeDtypeStruct((SIDE, run_rows, DV), bf16),
        in_specs=[smem] + [vmem] * (SIDE + 2),
        out_specs=vmem,
        compiler_params=pltpu.CompilerParams(vmem_limit_bytes=32 * 2**20),
    )(place, *arrived, reach, own)
    returned = lax.all_to_all(
        readout.reshape(SIDE, SIDE, local_rows, DV), "zl", split_axis=1, concat_axis=0, tiled=True
    )
    head_read = returned.reshape(HEADS, local_rows, DV).transpose(1, 0, 2).astype(f32)
    normed = (
        head_read
        * lax.rsqrt(jnp.mean(head_read * head_read, -1, keepdims=True) + 1e-06)
        * norm_gain
    )
    return normed.reshape(local_rows, HEADS * DV).astype(bf16)


def solution(mesh):
    finer = Mesh(mesh.devices.reshape(4, 4, 2, SIDE, SIDE), SPLIT)
    return jax.shard_map(
        shards,
        mesh=finer,
        in_specs=(
            P(SPLIT, None),
            P(STREAM, None),
            P(STREAM, None),
            P(STREAM, None),
            P(STREAM, None),
            P(STREAM, None),
            P(),
            P(),
            P(),
        ),
        out_specs=P(SPLIT, None),
        check_vma=False,
    )
```

time: 224 us -> 297 us (1.33)
  the two profiles are of different devices: /device:TPU:66 before, /device:TPU:2 now
where the time goes in v2:
time: 297 us; the launch traced here: 295 us
  starting transfers between devices  93.9 us (32%)
  blocking collectives  79.9 us (27%)
  waiting for transfers between devices  54.3 us (18%)
  Pallas kernels  21 us (7%)
  between operations  14.2 us (5%)
  local copies, waits for them, and re-layouts  13.2 us (4%)
  matrix products  11.6 us (4%)
  other arithmetic  7.21 us (2%)
    ppermute x19, starting transfers between devices, shifted(): return lax.ppermute(x, axis, [(i, (i + shift) % size) for i in range(size)])  86.1 us
    ppermute x19, waiting for transfers between devices, shifted(): return lax.ppermute(x, axis, [(i, (i + shift) % size) for i in range(size)])  46.9 us
    all_gather x1, blocking collectives, shards(): gates = lax.all_gather(gates, 'zh', axis=0, tiled=True)  25.3 us
    all_gather x1, blocking collectives, shards(): outer = lax.all_gather(subtotal, 'tm_0', axis=0)  16 us
    all_to_all x1, blocking collectives, shards(): lax.all_to_all(readout.reshape(SIDE, SIDE, local_rows, DV), 'zl', split_a...  14 us
    all_gather x1, blocking collectives, shards(): mine = lax.all_gather(block, 'tm_1', axis=0)  12.8 us
    all_gather x1, blocking collectives, shards(): gates = lax.all_gather(gates, 'zl', axis=0, tiled=True)  11.8 us
    pallas_call x1, Pallas kernels, shards(): pl.pallas_call(chunk_kernel, out_shape=(jax.ShapeDtypeStruct((SIDE, run_r...  9.47 us
  transfers between devices with their start and end apart: 22, of which 11 were waited for; matrix products, arithmetic and copies ran while one was open for 4% of the time, Pallas kernels for 0%

profile of v2, /device:TPU:2, one launch (start us, length us, event | category | flops | bytes accessed | tf_op | source)
XLA Modules:
  0.0 295.4 jit_solution(518361510311545039)
XLA Ops:
  8.5 5.9 %all-to-all-start = ((bf16[4,16,384]{2,1,0:T(8,128)(2,1)}), bf16[4,16,384]{2,1,0:T(8,128)(2,1)S(1)}, u32[]{:S(2)}, u32[]{:S(2)}) async-start(bf16[4,16,384]{2,1,0:T(8,128)(2,1)} %maximum_bitcast_fusion.3), calls=%async_computation | async-start | bytes 98304 | tf_op jit(solution)/shard_map/all_to_all | solution.py:228
  15.2 4.9 %all-to-all-done = bf16[4,16,384]{2,1,0:T(8,128)(2,1)S(1)} async-done(((bf16[4,16,384]{2,1,0:T(8,128)(2,1)}), bf16[4,16,384]{2,1,0:T(8,128)(2,1)S(1)}, u32[]{:S(2)}, u32[]{:S(2)}) %all-to-all-start) | async-done | bytes 49184 | tf_op jit(solution)/shard_map/all_to_all | solution.py:228
  20.1 9.1 %collective-permute-start = (bf16[4,16,384]{2,1,0:T(8,128)(2,1)S(1)}, bf16[4,16,384]{2,1,0:T(8,128)(2,1)S(1)}, u32[]{:S(2)}, u32[]{:S(2)}) collective-permute-start(bf16[4,16,384]{2,1,0:T(8,128)(2,1)S(1)} %all-to-all-done), channel_id=1, source_target_pairs={{0,4},{4,8},{8,12},{12,0},{1,5},{5,9},{9,13},{13,1},{2,6},{6,10},{... | collective-permute-start | bytes 147464 | tf_op jit(solution)/shard_map/ppermute | solution.py:198
  29.1 8.3 %collective-permute-start.1 = (bf16[4,16,384]{2,1,0:T(8,128)(2,1)S(1)}, bf16[4,16,384]{2,1,0:T(8,128)(2,1)S(1)}, u32[]{:S(2)}, u32[]{:S(2)}) collective-permute-start(bf16[4,16,384]{2,1,0:T(8,128)(2,1)S(1)} %all-to-all-done), channel_id=1, source_target_pairs={{0,8},{4,12},{8,0},{12,4},{1,9},{5,13},{9,1},{13,5},{2,10},{6,14},... | collective-permute-start | bytes 147464 | tf_op jit(solution)/shard_map/ppermute | solution.py:198
  37.4 5.5 %collective-permute-start.2 = (bf16[4,16,384]{2,1,0:T(8,128)(2,1)S(1)}, bf16[4,16,384]{2,1,0:T(8,128)(2,1)S(1)}, u32[]{:S(2)}, u32[]{:S(2)}) collective-permute-start(bf16[4,16,384]{2,1,0:T(8,128)(2,1)S(1)} %all-to-all-done), channel_id=1, source_target_pairs={{0,12},{4,0},{8,4},{12,8},{1,13},{5,1},{9,5},{13,9},{2,14},{6,2},{... | collective-permute-start | bytes 147464 | tf_op jit(solution)/shard_map/ppermute | solution.py:198
  44.1 3.9 %collective-permute-done.2 = bf16[4,16,384]{2,1,0:T(8,128)(2,1)S(1)} collective-permute-done((bf16[4,16,384]{2,1,0:T(8,128)(2,1)S(1)}, bf16[4,16,384]{2,1,0:T(8,128)(2,1)S(1)}, u32[]{:S(2)}, u32[]{:S(2)}) %collective-permute-start.2) | collective-permute-done | bytes 49184 | tf_op jit(solution)/shard_map/ppermute | solution.py:198
  47.9 3.4 %collective-permute-start.3 = (bf16[4,4,16,384]{3,2,1,0:T(8,128)(2,1)S(1)}, bf16[4,4,16,384]{3,2,1,0:T(8,128)(2,1)S(1)}, u32[]{:S(2)}, u32[]{:S(2)}) collective-permute-start(bf16[4,4,16,384]{3,2,1,0:T(8,128)(2,1)S(1)} %bitcast_dynamic-update-slice_fusion.4), channel_id=1, source_target_pairs={{0,32},{32,64},{64,96},{96,0},{1,33},{33,65},{65,97},{97,1},{2,34}... | collective-permute-start | bytes 589832 | tf_op jit(solution)/shard_map/ppermute | solution.py:198
  51.3 2.9 collective-permute-start.4
  54.3 4.2 %collective-permute-start.5 = (bf16[4,4,16,384]{3,2,1,0:T(8,128)(2,1)S(1)}, bf16[4,4,16,384]{3,2,1,0:T(8,128)(2,1)S(1)}, u32[]{:S(2)}, u32[]{:S(2)}) collective-permute-start(bf16[4,4,16,384]{3,2,1,0:T(8,128)(2,1)S(1)} %bitcast_dynamic-update-slice_fusion.4), channel_id=1, source_target_pairs={{0,96},{32,0},{64,32},{96,64},{1,97},{33,1},{65,33},{97,65},{2,98}... | collective-permute-start | bytes 589832 | tf_op jit(solution)/shard_map/ppermute | solution.py:198
  58.7 2.6 collective-permute-done.4
  61.3 2.0 collective-permute-done.5
  63.3 4.9 %collective-permute-start.11 = (bf16[4,4,4,16,384]{4,3,0,2,1:T(8,128)(2,1)S(1)}, bf16[4,4,4,16,384]{4,3,0,2,1:T(8,128)(2,1)}, u32[]{:S(2)}, u32[]{:S(2)}) collective-permute-start(bf16[4,4,4,16,384]{4,3,0,2,1:T(8,128)(2,1)S(1)} %bitcast_dynamic-update-slice_fusion.3), channel_id=1, source_target_pairs={{0,384},{128,0},{256,128},{384,256},{1,385},{129,1},{257,129},{385... | collective-permute-start | bytes 2359304 | tf_op jit(solution)/shard_map/ppermute | solution.py:198
  68.2 2.6 collective-permute-start.9
  70.8 2.9 collective-permute-start.7
  73.7 1.9 collective-permute-start.6
  75.7 23.1 %collective-permute-done.11 = bf16[4,4,4,16,384]{4,3,0,2,1:T(8,128)(2,1)} collective-permute-done((bf16[4,4,4,16,384]{4,3,0,2,1:T(8,128)(2,1)S(1)}, bf16[4,4,4,16,384]{4,3,0,2,1:T(8,128)(2,1)}, u32[]{:S(2)}, u32[]{:S(2)}) %collective-permute-start.11) | collective-permute-done | bytes 786464 | tf_op jit(solution)/shard_map/ppermute | solution.py:198
  98.7 1.9 collective-permute-start.12
  100.8 11.8 %all_gather.22 = bf16[512,32]{0,1:T(8,128)(2,1)S(1)} all-gather(bf16[128,32]{0,1:T(8,128)(2,1)S(1)} %pad_maximum_fusion.1), channel_id=1, replica_groups=mesh['tm_0'=4,'tm_1'=4,'tm_2'=2,'zh'=4,'zl'=4] {'zl'}, dimensions={0}, use_global_device_ids=true | all-gather | bytes 40960 | tf_op jit(solution)/shard_map/all_gather | solution.py:232
  112.7 25.3 %all_gather.23 = bf16[2048,32]{0,1:T(8,128)(2,1)S(1)} all-gather(bf16[512,32]{0,1:T(8,128)(2,1)S(1)} %all_gather.22), channel_id=1, replica_groups=mesh['tm_0'=4,'tm_1'=4,'tm_2'=2,'zh'=4,'zl'=4] {'zh'}, dimensions={0}, use_global_device_ids=true | all-gather | bytes 163840 | tf_op jit(solution)/shard_map/all_gather | solution.py:233
  138.1 1.9 collective-permute-start.10
  140.1 2.6 collective-permute-start.8
  144.0 1.3 pad_maximum_fusion
  145.3 1.5 select_bitcast_fusion.1
  147.0 1.4 copy.58
  148.8 1.4 copy.56
  150.5 1.4 copy.54
  151.8 3.4 %convolution_bitcast_fusion.refs_3_ = f32[512,384]{1,0:T(8,128)S(1)} fusion(bf16[512,2048]{1,0:T(8,128)(2,1)} %all-gather.4.cloned.1.call-done, bf16[2048,384]{1,0:T(8,128)(2,1)} %bitcast.132), kind=kOutput, calls=%fused_computation.5 | convolution fusion | flops 805306368 | bytes 4456448 | tf_op jit(solution)/shard_map/dot_general | solution.py:249
  156.7 2.1 convolution_bitcast_fusion.2.refs_1_
  158.9 2.1 convolution_bitcast_fusion.3.refs_0_
  161.0 2.7 fusion.1.refs_4_
  165.9 9.5 %shard_map.91 = (bf16[4,512,128]{2,1,0:T(8,128)(2,1)S(1)}, f32[4,512,128]{2,1,0:T(8,128)S(1)}, bf16[4,272,128]{2,1,0:T(8,128)(2,1)S(1)}) custom-call(f32[8]{0:T(128)S(1)} %bitcast.126, f32[512,384]{1,0:T(8,128)S(1)} %copy-done.2, f32[512,384]{1,0:T(8,128)S(1)} %copy-done.1, f32[512,384]{1,0:T(8,128)S(1)} %convolution_bitcast_fusion.1.refs_2_, ...), custom_call_target="tpu_custom_call" | custom-call | tf_op jit(solution)/shard_map/pallas_call | solution.py:251
  176.9 2.9 collective-permute-start.13
  179.8 7.3 %collective-permute-start.14 = (bf16[272,128]{1,0:T(8,128)(2,1)S(1)}, bf16[272,128]{1,0:T(8,128)(2,1)S(1)}, u32[]{:S(2)}, u32[]{:S(2)}) collective-permute-start(bf16[272,128]{1,0:T(8,128)(2,1)S(1)} %get-tuple-element.28), channel_id=1, source_target_pairs={{0,8},{4,12},{8,0},{12,4},{1,9},{5,13},{9,1},{13,5},{2,10},{6,14},... | collective-permute-start | bytes 208904 | tf_op jit(solution)/shard_map/ppermute | solution.py:198
  187.1 6.8 %collective-permute-start.15 = (bf16[272,128]{1,0:T(8,128)(2,1)S(1)}, bf16[272,128]{1,0:T(8,128)(2,1)S(1)}, u32[]{:S(2)}, u32[]{:S(2)}) collective-permute-start(bf16[272,128]{1,0:T(8,128)(2,1)S(1)} %get-tuple-element.27), channel_id=1, source_target_pairs={{0,12},{4,0},{8,4},{12,8},{1,13},{5,1},{9,5},{13,9},{2,14},{6,2},{... | collective-permute-start | bytes 208904 | tf_op jit(solution)/shard_map/ppermute | solution.py:198
  195.1 8.3 %collective-permute-done.15.refs_3_ = bf16[272,128]{1,0:T(8,128)(2,1)S(1)} collective-permute-done((bf16[272,128]{1,0:T(8,128)(2,1)S(1)}, bf16[272,128]{1,0:T(8,128)(2,1)S(1)}, u32[]{:S(2)}, u32[]{:S(2)}) %collective-permute-start.15) | collective-permute-done | bytes 69664 | tf_op jit(solution)/shard_map/ppermute | solution.py:198
  204.0 2.9 shard_map.92
  206.9 12.8 %all-gather = f32[1024,128]{1,0:T(8,128)S(1)} all-gather(f32[256,128]{1,0:T(8,128)} %get-tuple-element.13), channel_id=2, replica_groups=mesh['tm_0'=4,'tm_1'=4,'tm_2'=2,'zh'=4,'zl'=4] {'tm_1'}, dimensions={0}, use_global_device_ids=true | all-gather | bytes 655360 | tf_op jit(solution)/shard_map/all_gather | solution.py:277
  219.7 1.9 collective-permute-start.16
  221.7 1.8 collective-permute-done.16.other_ref
  224.3 4.6 %shard_map.93 = (f32[256,128]{1,0:T(8,128)}, f32[256,128]{1,0:T(8,128)}) custom-call(s32[4]{0:T(128)} %pad_add_fusion.1.place_ref, f32[4,256,128]{2,1,0:T(8,128)} %bitcast.129, f32[4,256,128]{2,1,0:T(8,128)} %copy-done.10), custom_call_target="tpu_custom_call" | custom-call | tf_op jit(solution)/shard_map/pallas_call | solution.py:279
  228.9 16.0 %all-gather.1 = f32[1024,128]{1,0:T(8,128)} all-gather(f32[256,128]{1,0:T(8,128)} %get-tuple-element.14), channel_id=3, replica_groups=mesh['tm_0'=4,'tm_1'=4,'tm_2'=2,'zh'=4,'zl'=4] {'tm_0'}, dimensions={0}, use_global_device_ids=true | all-gather | bytes 655360 | tf_op jit(solution)/shard_map/all_gather | solution.py:285
  244.9 3.1 %shard_map.94 = bf16[4,128,128]{2,1,0:T(8,128)(2,1)} custom-call(s32[4]{0:T(128)} %pad_add_fusion.1.place_ref, f32[4,256,128]{2,1,0:T(8,128)} %bitcast.127, f32[256,128]{1,0:T(8,128)} %get-tuple-element.15.prefix_ref, f32[4,256,128]{2,1,0:T(8,128)} %get-tuple-element.16.inner_ref), custom_call_target="tpu_custom_call" | custom-call | tf_op jit(solution)/shard_map/pallas_call | solution.py:286
  248.9 5.7 %collective-permute-start.17 = (bf16[128,128]{1,0:T(8,128)(2,1)S(1)}, bf16[128,128]{1,0:T(8,128)(2,1)S(1)}, u32[]{:S(2)}, u32[]{:S(2)}) collective-permute-start(bf16[128,128]{1,0:T(8,128)(2,1)S(1)} %get-tuple-element.33), channel_id=1, source_target_pairs={{0,4},{4,8},{8,12},{12,0},{1,5},{5,9},{9,13},{13,1},{2,6},{6,10},{... | collective-permute-start | bytes 98312 | tf_op jit(solution)/shard_map/ppermute | solution.py:198
  254.6 7.3 %collective-permute-start.18 = (bf16[128,128]{1,0:T(8,128)(2,1)S(1)}, bf16[128,128]{1,0:T(8,128)(2,1)S(1)}, u32[]{:S(2)}, u32[]{:S(2)}) collective-permute-start(bf16[128,128]{1,0:T(8,128)(2,1)S(1)} %get-tuple-element.32), channel_id=1, source_target_pairs={{0,8},{4,12},{8,0},{12,4},{1,9},{5,13},{9,1},{13,5},{2,10},{6,14},... | collective-permute-start | bytes 98312 | tf_op jit(solution)/shard_map/ppermute | solution.py:198
  261.8 4.2 %collective-permute-start.19 = (bf16[128,128]{1,0:T(8,128)(2,1)S(1)}, bf16[128,128]{1,0:T(8,128)(2,1)S(1)}, u32[]{:S(2)}, u32[]{:S(2)}) collective-permute-start(bf16[128,128]{1,0:T(8,128)(2,1)S(1)} %get-tuple-element.31), channel_id=1, source_target_pairs={{0,12},{4,0},{8,4},{12,8},{1,13},{5,1},{9,5},{13,9},{2,14},{6,2},{... | collective-permute-start | bytes 98312 | tf_op jit(solution)/shard_map/ppermute | solution.py:198
  266.1 3.0 %collective-permute-done.18.refs_2_ = bf16[128,128]{1,0:T(8,128)(2,1)S(1)} collective-permute-done((bf16[128,128]{1,0:T(8,128)(2,1)S(1)}, bf16[128,128]{1,0:T(8,128)(2,1)S(1)}, u32[]{:S(2)}, u32[]{:S(2)}) %collective-permute-start.18) | collective-permute-done | bytes 32800 | tf_op jit(solution)/shard_map/ppermute | solution.py:198
  269.1 2.5 collective-permute-done.19.refs_3_
  272.5 14.0 %all_to_all.14 = bf16[4,4,128,128]{3,2,0,1:T(8,128)(2,1)S(1)} all-to-all(bf16[4,4,128,128]{3,2,0,1:T(8,128)(2,1)S(1)} %copy.61), channel_id=1, replica_groups=mesh['tm_0'=4,'tm_1'=4,'tm_2'=2,'zh'=4,'zl'=4] {'zl'}, dimensions={1} | all-to-all | bytes 1048576 | tf_op jit(solution)/shard_map/all_to_all | solution.py:303
  (101 shorter events, 17.8 us)
Async XLA Ops:
  6.5 1.2 copy-start
  8.5 11.6 %all-to-all-start = ((bf16[4,16,384]{2,1,0:T(8,128)(2,1)}), bf16[4,16,384]{2,1,0:T(8,128)(2,1)S(1)}, u32[]{:S(2)}, u32[]{:S(2)}) async-start(bf16[4,16,384]{2,1,0:T(8,128)(2,1)} %maximum_bitcast_fusion.3), calls=%async_computation | async-start | bytes 98304 | tf_op jit(solution)/shard_map/all_to_all | solution.py:228
  14.3 137.5 %all-gather.4.cloned.1.call-start = ((), (), s32[]{:S(2)}) async-start(), calls=%async_computation.2 | async-start | bytes 2621440 | tf_op jit(solution)/shard_map/all_gather | solution.py:227
  15.1 60.5 %copy-start.14 = (bf16[128,16]{0,1:T(8,128)(2,1)S(1)}, bf16[128,16]{0,1:T(8,128)(2,1)}, u32[]{:S(2)}) copy-start(bf16[128,16]{0,1:T(8,128)(2,1)} %param.14) | copy-start | bytes 12292
  15.1 60.5 %copy-start.15 = (bf16[128,16]{0,1:T(8,128)(2,1)S(1)}, bf16[128,16]{0,1:T(8,128)(2,1)}, u32[]{:S(2)}) copy-start(bf16[128,16]{0,1:T(8,128)(2,1)} %param.13) | copy-start | bytes 12292
  20.1 22.9 %collective-permute-start = (bf16[4,16,384]{2,1,0:T(8,128)(2,1)S(1)}, bf16[4,16,384]{2,1,0:T(8,128)(2,1)S(1)}, u32[]{:S(2)}, u32[]{:S(2)}) collective-permute-start(bf16[4,16,384]{2,1,0:T(8,128)(2,1)S(1)} %all-to-all-done), channel_id=1, source_target_pairs={{0,4},{4,8},{8,12},{12,0},{1,5},{5,9},{9,13},{13,1},{2,6},{6,10},{... | collective-permute-start | bytes 147464 | tf_op jit(solution)/shard_map/ppermute | solution.py:198
  29.1 14.9 %collective-permute-start.1 = (bf16[4,16,384]{2,1,0:T(8,128)(2,1)S(1)}, bf16[4,16,384]{2,1,0:T(8,128)(2,1)S(1)}, u32[]{:S(2)}, u32[]{:S(2)}) collective-permute-start(bf16[4,16,384]{2,1,0:T(8,128)(2,1)S(1)} %all-to-all-done), channel_id=1, source_target_pairs={{0,8},{4,12},{8,0},{12,4},{1,9},{5,13},{9,1},{13,5},{2,10},{6,14},... | collective-permute-start | bytes 147464 | tf_op jit(solution)/shard_map/ppermute | solution.py:198
  37.4 10.5 %collective-permute-start.2 = (bf16[4,16,384]{2,1,0:T(8,128)(2,1)S(1)}, bf16[4,16,384]{2,1,0:T(8,128)(2,1)S(1)}, u32[]{:S(2)}, u32[]{:S(2)}) collective-permute-start(bf16[4,16,384]{2,1,0:T(8,128)(2,1)S(1)} %all-to-all-done), channel_id=1, source_target_pairs={{0,12},{4,0},{8,4},{12,8},{1,13},{5,1},{9,5},{13,9},{2,14},{6,2},{... | collective-permute-start | bytes 147464 | tf_op jit(solution)/shard_map/ppermute | solution.py:198
  42.9 95.0 %copy-start.18 = (f32[16]{0:T(128)S(1)}, f32[16]{0:T(128)}, u32[]{:S(2)}) copy-start(f32[16]{0:T(128)} %param.16) | copy-start | bytes 196
  42.9 95.0 %copy-start.19 = (f32[16]{0:T(128)S(1)}, f32[16]{0:T(128)}, u32[]{:S(2)}) copy-start(f32[16]{0:T(128)} %param.15) | copy-start | bytes 196
  47.9 10.7 %collective-permute-start.3 = (bf16[4,4,16,384]{3,2,1,0:T(8,128)(2,1)S(1)}, bf16[4,4,16,384]{3,2,1,0:T(8,128)(2,1)S(1)}, u32[]{:S(2)}, u32[]{:S(2)}) collective-permute-start(bf16[4,4,16,384]{3,2,1,0:T(8,128)(2,1)S(1)} %bitcast_dynamic-update-slice_fusion.4), channel_id=1, source_target_pairs={{0,32},{32,64},{64,96},{96,0},{1,33},{33,65},{65,97},{97,1},{2,34}... | collective-permute-start | bytes 589832 | tf_op jit(solution)/shard_map/ppermute | solution.py:198
  51.3 9.9 %collective-permute-start.4 = (bf16[4,4,16,384]{3,2,1,0:T(8,128)(2,1)S(1)}, bf16[4,4,16,384]{3,2,1,0:T(8,128)(2,1)S(1)}, u32[]{:S(2)}, u32[]{:S(2)}) collective-permute-start(bf16[4,4,16,384]{3,2,1,0:T(8,128)(2,1)S(1)} %bitcast_dynamic-update-slice_fusion.4), channel_id=1, source_target_pairs={{0,64},{32,96},{64,0},{96,32},{1,65},{33,97},{65,1},{97,33},{2,66}... | collective-permute-start | bytes 589832 | tf_op jit(solution)/shard_map/ppermute | solution.py:198
  54.3 9.0 %collective-permute-start.5 = (bf16[4,4,16,384]{3,2,1,0:T(8,128)(2,1)S(1)}, bf16[4,4,16,384]{3,2,1,0:T(8,128)(2,1)S(1)}, u32[]{:S(2)}, u32[]{:S(2)}) collective-permute-start(bf16[4,4,16,384]{3,2,1,0:T(8,128)(2,1)S(1)} %bitcast_dynamic-update-slice_fusion.4), channel_id=1, source_target_pairs={{0,96},{32,0},{64,32},{96,64},{1,97},{33,1},{65,33},{97,65},{2,98}... | collective-permute-start | bytes 589832 | tf_op jit(solution)/shard_map/ppermute | solution.py:198
  63.3 35.4 %collective-permute-start.11 = (bf16[4,4,4,16,384]{4,3,0,2,1:T(8,128)(2,1)S(1)}, bf16[4,4,4,16,384]{4,3,0,2,1:T(8,128)(2,1)}, u32[]{:S(2)}, u32[]{:S(2)}) collective-permute-start(bf16[4,4,4,16,384]{4,3,0,2,1:T(8,128)(2,1)S(1)} %bitcast_dynamic-update-slice_fusion.3), channel_id=1, source_target_pairs={{0,384},{128,0},{256,128},{384,256},{1,385},{129,1},{257,129},{385... | collective-permute-start | bytes 2359304 | tf_op jit(solution)/shard_map/ppermute | solution.py:198
  68.2 69.9 %collective-permute-start.9 = (bf16[4,4,4,16,384]{4,3,0,2,1:T(8,128)(2,1)S(1)}, bf16[4,4,4,16,384]{4,3,0,2,1:T(8,128)(2,1)S(1)}, u32[]{:S(2)}, u32[]{:S(2)}) collective-permute-start(bf16[4,4,4,16,384]{4,3,0,2,1:T(8,128)(2,1)S(1)} %bitcast_dynamic-update-slice_fusion.3), channel_id=1, source_target_pairs={{0,256},{128,384},{256,0},{384,128},{1,257},{129,385},{257,1},{385... | collective-permute-start | bytes 2359304 | tf_op jit(solution)/shard_map/ppermute | solution.py:198
  70.8 69.3 %collective-permute-start.7 = (bf16[4,4,4,16,384]{4,3,0,2,1:T(8,128)(2,1)S(1)}, bf16[4,4,4,16,384]{4,3,0,2,1:T(8,128)(2,1)S(1)}, u32[]{:S(2)}, u32[]{:S(2)}) collective-permute-start(bf16[4,4,4,16,384]{4,3,0,2,1:T(8,128)(2,1)S(1)} %bitcast_dynamic-update-slice_fusion.3), channel_id=1, source_target_pairs={{0,128},{128,256},{256,384},{384,0},{1,129},{129,257},{257,385},{3... | collective-permute-start | bytes 2359304 | tf_op jit(solution)/shard_map/ppermute | solution.py:198
  73.7 69.0 %collective-permute-start.6 = (bf16[4,4,4,16,384]{4,3,0,2,1:T(8,128)(2,1)S(1)}, bf16[4,4,4,16,384]{4,3,0,2,1:T(8,128)(2,1)}, u32[]{:S(2)}, u32[]{:S(2)}) collective-permute-start(bf16[4,4,4,16,384]{4,3,0,2,1:T(8,128)(2,1)S(1)} %bitcast_dynamic-update-slice_fusion.3), channel_id=1, source_target_pairs={{0,16},{16,0},{1,17},{17,1},{2,18},{18,2},{3,19},{19,3},{4,20},{20... | collective-permute-start | bytes 2359304 | tf_op jit(solution)/shard_map/ppermute | solution.py:198
  98.7 46.6 %collective-permute-start.12 = (bf16[4,4,4,16,384]{4,3,0,2,1:T(8,128)(2,1)}, bf16[4,4,4,16,384]{4,3,0,2,1:T(8,128)(2,1)}, u32[]{:S(2)}, u32[]{:S(2)}) collective-permute-start(bf16[4,4,4,16,384]{4,3,0,2,1:T(8,128)(2,1)} %collective-permute-done.11), channel_id=1, source_target_pairs={{0,16},{16,0},{1,17},{17,1},{2,18},{18,2},{3,19},{19,3},{4,20},{20... | collective-permute-start | bytes 2359304 | tf_op jit(solution)/shard_map/ppermute | solution.py:198
  138.1 10.3 %collective-permute-start.10 = (bf16[4,4,4,16,384]{4,3,0,2,1:T(8,128)(2,1)S(1)}, bf16[4,4,4,16,384]{4,3,0,2,1:T(8,128)(2,1)S(1)}, u32[]{:S(2)}, u32[]{:S(2)}) collective-permute-start(bf16[4,4,4,16,384]{4,3,0,2,1:T(8,128)(2,1)S(1)} %collective-permute-done.9), channel_id=1, source_target_pairs={{0,16},{16,0},{1,17},{17,1},{2,18},{18,2},{3,19},{19,3},{4,20},{20... | collective-permute-start | bytes 2359304 | tf_op jit(solution)/shard_map/ppermute | solution.py:198
  140.1 10.1 %collective-permute-start.8 = (bf16[4,4,4,16,384]{4,3,0,2,1:T(8,128)(2,1)S(1)}, bf16[4,4,4,16,384]{4,3,0,2,1:T(8,128)(2,1)S(1)}, u32[]{:S(2)}, u32[]{:S(2)}) collective-permute-start(bf16[4,4,4,16,384]{4,3,0,2,1:T(8,128)(2,1)S(1)} %collective-permute-done.7), channel_id=1, source_target_pairs={{0,16},{16,0},{1,17},{17,1},{2,18},{18,2},{3,19},{19,3},{4,20},{20... | collective-permute-start | bytes 2359304 | tf_op jit(solution)/shard_map/ppermute | solution.py:198
  151.8 3.4 %copy-start.8 = (bf16[4,4,4,2,16,384]{5,4,3,2,1,0:T(8,128)(2,1)S(1)}, bf16[4,4,4,2,16,384]{5,4,3,2,1,0:T(8,128)(2,1)}, u32[]{:S(2)}) copy-start(bf16[4,4,4,2,16,384]{5,4,3,2,1,0:T(8,128)(2,1)} %copy.56) | copy-start | bytes 4718596
  151.8 3.5 %copy-start.17 = (bf16[512,2048]{1,0:T(8,128)(2,1)S(1)}, bf16[512,2048]{1,0:T(8,128)(2,1)}, u32[]{:S(2)}) copy-start(bf16[512,2048]{1,0:T(8,128)(2,1)} %all-gather.4.cloned.1.call-done) | copy-start | bytes 6291460
  155.3 1.4 copy-start.9
  156.7 2.2 copy-start.7
  163.7 1.1 copy-start.1
  164.8 1.1 copy-start.2
  175.4 0.8 copy-start.3
  176.9 17.7 %collective-permute-start.13 = (bf16[272,128]{1,0:T(8,128)(2,1)S(1)}, bf16[272,128]{1,0:T(8,128)(2,1)S(1)}, u32[]{:S(2)}, u32[]{:S(2)}) collective-permute-start(bf16[272,128]{1,0:T(8,128)(2,1)S(1)} %get-tuple-element.29), channel_id=1, source_target_pairs={{0,4},{4,8},{8,12},{12,0},{1,5},{5,9},{9,13},{13,1},{2,6},{6,10},{... | collective-permute-start | bytes 208904 | tf_op jit(solution)/shard_map/ppermute | solution.py:198
  179.8 15.2 %collective-permute-start.14 = (bf16[272,128]{1,0:T(8,128)(2,1)S(1)}, bf16[272,128]{1,0:T(8,128)(2,1)S(1)}, u32[]{:S(2)}, u32[]{:S(2)}) collective-permute-start(bf16[272,128]{1,0:T(8,128)(2,1)S(1)} %get-tuple-element.28), channel_id=1, source_target_pairs={{0,8},{4,12},{8,0},{12,4},{1,9},{5,13},{9,1},{13,5},{2,10},{6,14},... | collective-permute-start | bytes 208904 | tf_op jit(solution)/shard_map/ppermute | solution.py:198
  187.1 16.3 %collective-permute-start.15 = (bf16[272,128]{1,0:T(8,128)(2,1)S(1)}, bf16[272,128]{1,0:T(8,128)(2,1)S(1)}, u32[]{:S(2)}, u32[]{:S(2)}) collective-permute-start(bf16[272,128]{1,0:T(8,128)(2,1)S(1)} %get-tuple-element.27), channel_id=1, source_target_pairs={{0,12},{4,0},{8,4},{12,8},{1,13},{5,1},{9,5},{13,9},{2,14},{6,2},{... | collective-permute-start | bytes 208904 | tf_op jit(solution)/shard_map/ppermute | solution.py:198
  194.6 8.8 %copy-start.11 = (bf16[272,128]{1,0:T(8,128)(2,1)}, bf16[272,128]{1,0:T(8,128)(2,1)S(1)}, u32[]{:S(2)}) copy-start(bf16[272,128]{1,0:T(8,128)(2,1)S(1)} %collective-permute-done.13.refs_1_) | copy-start | bytes 208900
  195.1 8.3 %copy-start.12 = (bf16[272,128]{1,0:T(8,128)(2,1)}, bf16[272,128]{1,0:T(8,128)(2,1)S(1)}, u32[]{:S(2)}) copy-start(bf16[272,128]{1,0:T(8,128)(2,1)S(1)} %collective-permute-done.14.refs_2_) | copy-start | bytes 208900
  203.4 0.6 copy-start.13
  219.7 3.8 %copy-start.6 = (f32[1024,128]{1,0:T(8,128)}, f32[1024,128]{1,0:T(8,128)S(1)}, u32[]{:S(2)}) copy-start(f32[1024,128]{1,0:T(8,128)S(1)} %all-gather) | copy-start | bytes 1572868
  219.7 3.8 %collective-permute-start.16 = (f32[4,256,128]{2,1,0:T(8,128)S(1)}, f32[4,256,128]{2,1,0:T(8,128)S(1)}, u32[]{:S(2)}, u32[]{:S(2)}) collective-permute-start(f32[4,256,128]{2,1,0:T(8,128)S(1)} %bitcast.128), channel_id=1, source_target_pairs={{0,16},{16,0},{1,17},{17,1},{2,18},{18,2},{3,19},{19,3},{4,20},{20... | collective-permute-start | bytes 1572872 | tf_op jit(solution)/shard_map/ppermute | solution.py:278
  221.7 49.9 %copy-start.4 = (bf16[4,512,128]{2,1,0:T(8,128)(2,1)S(1)}, bf16[4,512,128]{2,1,0:T(8,128)(2,1)}, u32[]{:S(2)}) copy-start(bf16[4,512,128]{2,1,0:T(8,128)(2,1)} %copy-done.3) | copy-start | bytes 1572868
  221.7 49.9 %copy-start.5 = (s32[4]{0:T(128)S(1)}, s32[4]{0:T(128)}, u32[]{:S(2)}) copy-start(s32[4]{0:T(128)} %pad_add_fusion.1.place_ref) | copy-start | bytes 52
  223.5 0.8 copy-start.10
  248.9 17.2 %collective-permute-start.17 = (bf16[128,128]{1,0:T(8,128)(2,1)S(1)}, bf16[128,128]{1,0:T(8,128)(2,1)S(1)}, u32[]{:S(2)}, u32[]{:S(2)}) collective-permute-start(bf16[128,128]{1,0:T(8,128)(2,1)S(1)} %get-tuple-element.33), channel_id=1, source_target_pairs={{0,4},{4,8},{8,12},{12,0},{1,5},{5,9},{9,13},{13,1},{2,6},{6,10},{... | collective-permute-start | bytes 98312 | tf_op jit(solution)/shard_map/ppermute | solution.py:198
  254.6 14.5 %collective-permute-start.18 = (bf16[128,128]{1,0:T(8,128)(2,1)S(1)}, bf16[128,128]{1,0:T(8,128)(2,1)S(1)}, u32[]{:S(2)}, u32[]{:S(2)}) collective-permute-start(bf16[128,128]{1,0:T(8,128)(2,1)S(1)} %get-tuple-element.32), channel_id=1, source_target_pairs={{0,8},{4,12},{8,0},{12,4},{1,9},{5,13},{9,1},{13,5},{2,10},{6,14},... | collective-permute-start | bytes 98312 | tf_op jit(solution)/shard_map/ppermute | solution.py:198
  261.8 9.7 %collective-permute-start.19 = (bf16[128,128]{1,0:T(8,128)(2,1)S(1)}, bf16[128,128]{1,0:T(8,128)(2,1)S(1)}, u32[]{:S(2)}, u32[]{:S(2)}) collective-permute-start(bf16[128,128]{1,0:T(8,128)(2,1)S(1)} %get-tuple-element.31), channel_id=1, source_target_pairs={{0,12},{4,0},{8,4},{12,8},{1,13},{5,1},{9,5},{13,9},{2,14},{6,2},{... | collective-permute-start | bytes 98312 | tf_op jit(solution)/shard_map/ppermute | solution.py:198
  272.4 14.4 %copy-start.16 = (f32[128]{0:T(128)S(1)}, f32[128]{0:T(128)}, u32[]{:S(2)}) copy-start(f32[128]{0:T(128)} %param.17) | copy-start | bytes 1540
Sparse Core Ops, SparseCore 0:
  17.3 62.5 all-gather.3

commit v3 on v2

--- a/solution.py
+++ b/solution.py
@@ -31,9 +31,39 @@
     )
 
 
-def chunk_kernel(gate_ref, *refs):
-    raw_refs, (logit_ref, reach_ref, own_ref, total_ref) = refs[:SIDE], refs[SIDE:]
-    chunks = raw_refs[0].shape[0] // CHUNK
+def chunk_kernel(place_ref, rate_ref, bias_ref, *refs):
+    token_ref, first_ref, own_refs, other_refs = refs[0], refs[1], refs[2 : SIDE + 1], refs[SIDE + 1 : 2 * SIDE + 1]
+    reach_ref, own_ref, total_ref, matrix_ref, raw_ref, logit_ref = refs[2 * SIDE + 1 :]
+    core, at_y, group = place_ref[1], place_ref[2], place_ref[4]
+    chunks = token_ref.shape[0] // CHUNK
+    places = [lax.rem(place_ref[5] - x + SIDE, SIDE) for x in range(SIDE)]
+    lane = lax.broadcasted_iota(jnp.int32, (1, 128), 1)
+    keep = [jnp.where((lane // SIDE) % 2 == c, 1.0, 0.0).astype(bf16) for c in range(2)]
+
+    def gate_rows(z, carry):
+        for x in range(SIDE):
+            for c in range(2):
+                at = pl.ds(pl.multiple_of(z * 128 + (places[x] * 2 + c) * 16, 16), 16)
+                matrix_ref[at, 0:128] = first_ref[x, z, :, 384:512] * keep[c]
+        return carry
+
+    lax.fori_loop(0, first_ref.shape[1], gate_rows, 0)
+    logit_ref[...] = jnp.dot(token_ref[...], matrix_ref[:, 0:128], preferred_element_type=f32)
+
+    for k in range(SIDE):
+
+        def head_rows(z, carry, k=k):
+            for x in range(SIDE):
+                mine = own_refs[k - 1][x, z] if k else first_ref[x, z, :, 0:384]
+                other = other_refs[k][x, z]
+                for c in range(2):
+                    at = pl.ds(pl.multiple_of(z * 128 + (places[x] * 2 + c) * 16, 16), 16)
+                    matrix_ref[at, :] = jnp.where(core == c, mine, other)
+            return carry
+
+        lax.fori_loop(0, first_ref.shape[1], head_rows, 0)
+        raw_ref[k] = jnp.dot(token_ref[...], matrix_ref[...], preferred_element_type=f32)
+
     row = lax.broadcasted_iota(jnp.int32, (CHUNK, CHUNK), 0)
     col = lax.broadcasted_iota(jnp.int32, (CHUNK, CHUNK), 1)
     strict, inclusive = row > col, row >= col
@@ -53,11 +83,12 @@
         each = range(GANG)
         q, k, v, beta, grow, scale_row, beta_row, tail, last, decay = ([] for _ in range(10))
         for i in each:
-            raw_ref, mine = raw_refs[units[i][0]], units[i][0]
-            rate, bias = gate_ref[2 * mine], gate_ref[2 * mine + 1]
-            raw_q = raw_ref[pl.ds(starts[i], CHUNK), 0:128]
-            raw_k = raw_ref[pl.ds(starts[i], CHUNK), 128:256]
-            raw_v = raw_ref[pl.ds(starts[i], CHUNK), 256:384]
+            mine = units[i][0]
+            head = lax.rem(at_y - mine + SIDE, SIDE)
+            rate, bias = rate_ref[group * SIDE + head], bias_ref[group * SIDE + head]
+            raw_q = raw_ref[mine, pl.ds(starts[i], CHUNK), 0:128]
+            raw_k = raw_ref[mine, pl.ds(starts[i], CHUNK), 128:256]
+            raw_v = raw_ref[mine, pl.ds(starts[i], CHUNK), 256:384]
             logits = logit_ref[pl.ds(starts[i], CHUNK), :]
             q.append(
                 (
@@ -70,10 +101,12 @@
                 (raw_k * lax.rsqrt(jnp.sum(raw_k * raw_k, -1, keepdims=True) + 1e-06)).astype(bf16)
             )
             v.append(raw_v.astype(bf16))
-            x = logits[:, 2 * mine : 2 * mine + 1]
+            of_head = (lane % SIDE == head) & (lane < 4 * SIDE)
+            x = jnp.sum(jnp.where(of_head & (lane < 2 * SIDE), logits, 0.0), -1, keepdims=True)
+            y = jnp.sum(jnp.where(of_head & (lane >= 2 * SIDE), logits, 0.0), -1, keepdims=True)
             softplus = jnp.maximum(x, 0.0) + jnp.log1p(jnp.exp(-jnp.abs(x)))
             log_decay = (-rate * softplus).astype(bf16)
-            strength = (1.0 / (1.0 + jnp.exp(-(logits[:, 2 * mine + 1 : 2 * mine + 2] + bias)))).astype(bf16).astype(f32)
+            strength = (1.0 / (1.0 + jnp.exp(-(y + bias)))).astype(bf16).astype(f32)
             g = mm(ones_below, jnp.broadcast_to(log_decay, (CHUNK, CHUNK)))
             b = jnp.broadcast_to(strength, (CHUNK, CHUNK))
             turned = jnp.where(col < 64, g, b).T
@@ -111,21 +144,22 @@
         reach = [grow[i] * q[i].astype(f32) - inside[i][:, :DK] for i in each]
         for i in each:
             mine, j = units[i]
+            head = lax.rem(at_y - mine + SIDE, SIDE)
             if j == 0:
                 state = jnp.concatenate([eye, jnp.zeros((DV, DK), f32)], 0)
                 kept = jnp.ones((1, 1), f32)
             out = mm(reach[i], state, 1, 1)
-            reach_ref[mine, pl.ds(starts[i], CHUNK), :] = out[:, :DK].astype(bf16)
-            own_ref[mine, pl.ds(starts[i], CHUNK), :] = out[:, DK:] + inside[i][:, DK:]
+            reach_ref[head, pl.ds(starts[i], CHUNK), :] = out[:, :DK].astype(bf16)
+            own_ref[head, pl.ds(starts[i], CHUNK), :] = out[:, DK:] + inside[i][:, DK:]
             moved = mm(state, change[i][:DK])
             state = last[i] * state - moved
             state = jnp.concatenate([state[:DK], state[DK:] + change[i][DK:]], 0)
             kept = kept * last[i]
             if j == chunks - 1:
                 part = kept.astype(bf16).astype(f32)
-                total_ref[mine, 0:DK, :] = (state[:DK] - kept * eye).astype(bf16)
-                total_ref[mine, DK : DK + DV, :] = state[DK:].astype(bf16)
-                total_ref[mine, DK + DV :, :] = jnp.concatenate(
+                total_ref[head, 0:DK, :] = (state[:DK] - kept * eye).astype(bf16)
+                total_ref[head, DK : DK + DV, :] = state[DK:].astype(bf16)
+                total_ref[head, DK + DV :, :] = jnp.concatenate(
                     [jnp.broadcast_to(part, (8, DK)), jnp.broadcast_to(kept - part, (8, DK))], 0
                 ).astype(bf16)
 
@@ -135,19 +169,14 @@
     return packed[:DK].astype(f32) + kept * eye, packed[DK : DK + DV].astype(f32)
 
 
-def group_kernel(place_ref, *refs):
-    part_refs, (prefix_ref, total_ref) = refs[:SIDE], refs[SIDE:]
-    zh = place_ref[3]
+def group_kernel(part_ref, prefix_ref, total_ref):
     row = lax.broadcasted_iota(jnp.int32, (DK + DV, DK), 0)
     col = lax.broadcasted_iota(jnp.int32, (DK + DV, DK), 1)
     state = jnp.where(row == col, 1.0, 0.0).astype(f32)
     eye = state[:DK]
     for j in range(SIDE):
         prefix_ref[j] = state
-        packed = part_refs[0][...]
-        for shift in range(1, SIDE):
-            packed = jnp.where(lax.rem(zh - shift + SIDE, SIDE) == j, part_refs[shift][...], packed)
-        step, added = widen_map(packed, eye)
+        step, added = widen_map(part_ref[j], eye)
         moved = mm_exact(state, step)
         state = jnp.concatenate([moved[:DK], moved[DK:] + added], 0)
     total_ref[...] = state
@@ -182,29 +211,14 @@
         state_ref[j] = (mm_exact(state, inner_ref[j, :DK]) + inner_ref[j, DK:]).astype(bf16)
 
 
-def read_kernel(place_ref, *refs):
-    state_refs, (reach_ref, own_ref, read_ref) = refs[:SIDE], refs[SIDE:]
-    at_y, zh = place_ref[2], place_ref[3]
-    for k in range(SIDE):
-        head = lax.rem(at_y - k + SIDE, SIDE)
-        state = state_refs[0][...]
-        for shift in range(1, SIDE):
-            state = jnp.where(lax.rem(zh - shift + SIDE, SIDE) == head, state_refs[shift][...], state)
-        read_ref[head] = (mm(reach_ref[k], state, 1, 1) + own_ref[k]).astype(bf16)
+def read_kernel(state_ref, reach_ref, own_ref, read_ref):
+    for head in range(SIDE):
+        read_ref[head] = (mm(reach_ref[head], state_ref[head], 1, 1) + own_ref[head]).astype(bf16)
 
 
 def shifted(x, axis, shift):
     size = lax.axis_size(axis)
     return lax.ppermute(x, axis, [(i, (i + shift) % size) for i in range(size)])
-
-
-def ring_gather(x, axis):
-    size, me = lax.axis_size(axis), lax.axis_index(axis)
-    out = jnp.zeros((size,) + x.shape, x.dtype)
-    for shift in range(size):
-        piece = shifted(x, axis, shift) if shift else x
-        out = lax.dynamic_update_index_in_dim(out, piece, lax.rem(me - shift + size, size), 0)
-    return out
 
 
 def shards(
@@ -223,31 +237,31 @@
         w = lax.dynamic_slice_in_dim(w, first, rows, 0).reshape(rows, SIDE, SIDE, DK)
         return lax.dynamic_index_in_dim(w, at_y, 2, False)
 
-    weights = jnp.concatenate([share(w_query), share(w_key), share(w_value)], -1).transpose(1, 0, 2)
+    def gate_share(w):
+        w = lax.dynamic_slice_in_dim(w, at_x * 2 * rows, 2 * rows, 0).reshape(2, rows, SIDE, SIDE)
+        return w.transpose(1, 2, 0, 3).reshape(rows, SIDE, 2 * SIDE)
+
+    weights = jnp.concatenate(
+        [
+            share(w_query),
+            share(w_key),
+            share(w_value),
+            gate_share(decay_proj),
+            gate_share(beta_proj),
+            jnp.zeros((rows, SIDE, 128 - 4 * SIDE), bf16),
+        ],
+        -1,
+    ).transpose(1, 0, 2)
+    weights = jnp.broadcast_to(weights[None], (SIDE,) + weights.shape)
+    weights = weights.reshape((SIDE * SIDE,) + weights.shape[2:])
     run = lax.all_gather(tokens, "zl", axis=0, tiled=True)
-    weights = lax.all_to_all(weights, "zl", split_axis=0, concat_axis=0, tiled=True)
-    weights = ring_gather(weights, "zh")
-    weights = ring_gather(weights, "tm_1")
-    gates = jnp.concatenate([decay_proj, beta_proj], 1)
-    gates = lax.all_gather(gates, "zl", axis=0, tiled=True)
-    gates = lax.all_gather(gates, "zh", axis=0, tiled=True)
-    heads = zl * SIDE + jnp.remainder(at_y - jnp.arange(SIDE), SIDE)
-    wanted = jnp.stack([heads, heads + HEADS], 1).reshape(2 * SIDE)
-    wanted = jnp.concatenate([wanted, jnp.full((128 - 2 * SIDE,), -1, wanted.dtype)])
-    pick = (jnp.arange(2 * HEADS)[:, None] == wanted[None, :]).astype(bf16)
-    gates = jnp.dot(gates, pick, preferred_element_type=f32).astype(bf16)
-    logits = jnp.dot(run, gates, preferred_element_type=f32)
-    both = jnp.concatenate([decay_rate, beta_bias])
-    levels = jnp.sum(jnp.where(pick > 0, both[:, None], 0.0), 0)[: 2 * SIDE]
-
-    raws = []
-    for k in range(SIDE):
-        own = shifted(weights, "tm_0", k) if k else weights
-        other = shifted(own, "tm_2", 1)
-        pair = jnp.stack([jnp.where(at_c == 0, own, other), jnp.where(at_c == 0, other, own)])
-        matrix = pair.transpose(2, 3, 1, 0, 4, 5).reshape(tokens.shape[1], 3 * DK)
-        raws.append(jnp.dot(run, matrix, preferred_element_type=f32))
-    run_rows = run.shape[0]
+    weights = lax.all_to_all(weights, STREAM, split_axis=0, concat_axis=0, tiled=True)
+    first = jnp.stack([weights] + [shifted(weights, "tm_1", k) for k in range(1, SIDE)])
+    narrow = first[..., : 3 * DK]
+    mine = [narrow] + [shifted(narrow, "tm_0", k) for k in range(1, SIDE)]
+    others = [shifted(a, "tm_2", 1) for a in mine]
+    place = jnp.stack([at_x * 2 + at_c, at_c, at_y, zh, zl, at_x]).astype(jnp.int32)
+    run_rows, features = run.shape
     reach, own, total = pl.pallas_call(
         chunk_kernel,
         out_shape=(
@@ -255,25 +269,26 @@
             jax.ShapeDtypeStruct((SIDE, run_rows, DV), f32),
             jax.ShapeDtypeStruct((SIDE, MAP_ROWS, DK), bf16),
         ),
-        in_specs=[smem] + [vmem] * 5,
+        in_specs=[smem] * 3 + [vmem] * (2 * SIDE + 1),
         out_specs=(vmem, vmem, vmem),
-        compiler_params=pltpu.CompilerParams(vmem_limit_bytes=48 * 2**20),
-    )(levels, *raws, logits)
-
-    place = jnp.stack([at_x * 2 + at_c, at_c, at_y, zh]).astype(jnp.int32)
-    parts = []
-    for shift in range(SIDE):
-        sent = lax.dynamic_index_in_dim(total, jnp.remainder(at_y - zh - shift, SIDE), 0, False)
-        parts.append(shifted(sent, "zh", shift) if shift else sent)
+        scratch_shapes=[
+            pltpu.VMEM((features, 3 * DK), bf16),
+            pltpu.VMEM((SIDE, run_rows, 3 * DK), f32),
+            pltpu.VMEM((run_rows, 128), f32),
+        ],
+        compiler_params=pltpu.CompilerParams(vmem_limit_bytes=56 * 2**20),
+    )(place, decay_rate, beta_bias, run, first, *mine[1:], *others)
+
+    parts = lax.all_to_all(total, "zh", split_axis=0, concat_axis=0, tiled=True)
     inner, block = pl.pallas_call(
         group_kernel,
         out_shape=(
             jax.ShapeDtypeStruct((SIDE, DK + DV, DK), f32),
             jax.ShapeDtypeStruct((DK + DV, DK), f32),
         ),
-        in_specs=[smem] + [vmem] * SIDE,
+        in_specs=[vmem],
         out_specs=(vmem, vmem),
-    )(place, *parts)
+    )(parts)
     mine = lax.all_gather(block, "tm_1", axis=0)
     other = lax.ppermute(mine, "tm_2", [(0, 1), (1, 0)])
     prefix, subtotal = pl.pallas_call(
@@ -289,17 +304,14 @@
         in_specs=[smem] + [vmem] * 3,
         out_specs=vmem,
     )(place, outer, prefix, inner)
-    arrived = []
-    for shift in range(SIDE):
-        sent = lax.dynamic_index_in_dim(states, jnp.remainder(zh + shift, SIDE), 0, False)
-        arrived.append(shifted(sent, "zh", shift) if shift else sent)
+    states = lax.all_to_all(states, "zh", split_axis=0, concat_axis=0, tiled=True)
     readout = pl.pallas_call(
         read_kernel,
         out_shape=jax.ShapeDtypeStruct((SIDE, run_rows, DV), bf16),
-        in_specs=[smem] + [vmem] * (SIDE + 2),
+        in_specs=[vmem] * 3,
         out_specs=vmem,
         compiler_params=pltpu.CompilerParams(vmem_limit_bytes=32 * 2**20),
-    )(place, *arrived, reach, own)
+    )(states, reach, own)
     returned = lax.all_to_all(
         readout.reshape(SIDE, SIDE, local_rows, DV), "zl", split_axis=1, concat_axis=0, tiled=True
     )

time: 297 us -> 246 us (0.83)
  the two profiles are of different devices: /device:TPU:2 before, /device:TPU:4 now
where the time goes in v3:
time: 246 us; the launch traced here: 245 us
  blocking collectives  133 us (54%)
  waiting for transfers between devices  31.1 us (13%)
  Pallas kernels  31.1 us (13%)
  starting transfers between devices  29.5 us (12%)
  between operations  13.7 us (6%)
  local copies, waits for them, and re-layouts  6.23 us (3%)
    all_to_all x1, blocking collectives, shards(): parts = lax.all_to_all(total, 'zh', split_axis=0, concat_axis=0, tiled=True)  37.3 us
    all_to_all x1, blocking collectives, shards(): lax.all_to_all(weights, STREAM, split_axis=0, concat_axis=0, tiled=True)  34.1 us
    ppermute x10, waiting for transfers between devices, shifted(): return lax.ppermute(x, axis, [(i, (i + shift) % size) for i in range(size)])  28.5 us
    ppermute x10, starting transfers between devices, shifted(): return lax.ppermute(x, axis, [(i, (i + shift) % size) for i in range(size)])  27.6 us
    pallas_call x1, Pallas kernels, shards(): pl.pallas_call(chunk_kernel, out_shape=(jax.ShapeDtypeStruct((SIDE, run_r...  20.1 us
    all_to_all x1, blocking collectives, shards(): lax.all_to_all(states, 'zh', split_axis=0, concat_axis=0, tiled=True)  18.9 us
    all_gather x1, blocking collectives, shards(): outer = lax.all_gather(subtotal, 'tm_0', axis=0)  14.5 us
    all_gather x1, blocking collectives, shards(): mine = lax.all_gather(block, 'tm_1', axis=0)  13.9 us
  transfers between devices with their start and end apart: 12, of which 6 were waited for; matrix products, arithmetic and copies ran while one was open for 2% of the time, Pallas kernels for 0%

profile of v3, /device:TPU:4, one launch (start us, length us, event | category | flops | bytes accessed | tf_op | source)
XLA Modules:
  0.0 245.0 jit_solution(13862081938276420234)
XLA Ops:
  6.5 0.7 all-gather.4.cloned.1.call-update
  7.3 0.8 constant_dynamic-slice_fusion
  8.1 0.1 reshape.50
  8.1 0.1 copy.27
  8.2 0.1 reshape.48
  8.3 0.1 copy.26
  8.6 0.9 constant_dynamic-slice_fusion.3
  9.7 0.1 concatenate.3
  9.8 34.1 %all_to_all.24 = bf16[16,16,512]{2,1,0:T(8,128)(2,1)S(1)} all-to-all(bf16[16,16,512]{2,1,0:T(8,128)(2,1)S(1)} %bitcast.55), channel_id=1, replica_groups=mesh['tm_0'=4,'tm_1'=4,'tm_2'=2,'zh'=4,'zl'=4] {'zh','zl'}, dimensions={0} | all-to-all | bytes 524288 | tf_op jit(solution)/shard_map/all_to_all | solution.py:258
  43.9 2.4 collective-permute-start.2
  46.3 4.7 %collective-permute-start.1 = (bf16[16,16,512]{2,1,0:T(8,128)(2,1)S(1)}, bf16[16,16,512]{2,1,0:T(8,128)(2,1)S(1)}, u32[]{:S(2)}, u32[]{:S(2)}) collective-permute-start(bf16[16,16,512]{2,1,0:T(8,128)(2,1)S(1)} %all_to_all.24), channel_id=1, source_target_pairs={{0,64},{32,96},{64,0},{96,32},{1,65},{33,97},{65,1},{97,33},{2,66}... | collective-permute-start | bytes 786440 | tf_op jit(solution)/shard_map/ppermute | solution.py:221
  51.0 1.9 collective-permute-start
  52.9 0.0 collective-permute-done.2
  52.9 3.1 %collective-permute-done.1 = bf16[16,16,512]{2,1,0:T(8,128)(2,1)S(1)} collective-permute-done((bf16[16,16,512]{2,1,0:T(8,128)(2,1)S(1)}, bf16[16,16,512]{2,1,0:T(8,128)(2,1)S(1)}, u32[]{:S(2)}, u32[]{:S(2)}) %collective-permute-start.1) | collective-permute-done | bytes 262176 | tf_op jit(solution)/shard_map/ppermute | solution.py:221
  56.0 3.2 %collective-permute-done = bf16[16,16,512]{2,1,0:T(8,128)(2,1)S(1)} collective-permute-done((bf16[16,16,512]{2,1,0:T(8,128)(2,1)S(1)}, bf16[16,16,512]{2,1,0:T(8,128)(2,1)S(1)}, u32[]{:S(2)}, u32[]{:S(2)}) %collective-permute-start) | collective-permute-done | bytes 262176 | tf_op jit(solution)/shard_map/ppermute | solution.py:221
  59.2 0.1 pad_maximum_fusion.refs_1_
  59.4 1.0 slice.4
  60.4 5.1 %collective-permute-start.5 = (bf16[4,16,16,384]{3,2,1,0:T(8,128)(2,1)}, bf16[4,16,16,384]{3,2,1,0:T(8,128)(2,1)S(1)}, u32[]{:S(2)}, u32[]{:S(2)}) collective-permute-start(bf16[4,16,16,384]{3,2,1,0:T(8,128)(2,1)} %slice.4), channel_id=1, source_target_pairs={{0,384},{128,0},{256,128},{384,256},{1,385},{129,1},{257,129},{385... | collective-permute-start | bytes 2359304 | tf_op jit(solution)/shard_map/ppermute | solution.py:221
  65.5 2.4 collective-permute-start.4
  67.9 2.9 %collective-permute-start.3 = (bf16[4,16,16,384]{3,2,1,0:T(8,128)(2,1)}, bf16[4,16,16,384]{3,2,1,0:T(8,128)(2,1)}, u32[]{:S(2)}, u32[]{:S(2)}) collective-permute-start(bf16[4,16,16,384]{3,2,1,0:T(8,128)(2,1)} %slice.4), channel_id=1, source_target_pairs={{0,128},{128,256},{256,384},{384,0},{1,129},{129,257},{257,385},{3... | collective-permute-start | bytes 2359304 | tf_op jit(solution)/shard_map/ppermute | solution.py:221
  70.8 1.9 collective-permute-start.6
  72.8 19.0 %collective-permute-done.5.refs_4_ = bf16[4,16,16,384]{3,2,1,0:T(8,128)(2,1)S(1)} collective-permute-done((bf16[4,16,16,384]{3,2,1,0:T(8,128)(2,1)}, bf16[4,16,16,384]{3,2,1,0:T(8,128)(2,1)S(1)}, u32[]{:S(2)}, u32[]{:S(2)}) %collective-permute-start.5) | collective-permute-done | bytes 786464 | tf_op jit(solution)/shard_map/ppermute | solution.py:221
  91.7 1.9 collective-permute-start.9
  93.7 2.4 collective-permute-start.8
  96.1 1.3 collective-permute-done.3.refs_2_
  97.4 1.9 collective-permute-start.7
  99.3 0.6 stack.42.place_ref
  99.9 0.0 collective-permute-done.6.refs_5_
  99.9 0.0 collective-permute-done.9.refs_8_
  99.9 0.0 collective-permute-done.8.refs_7_
  99.9 2.0 collective-permute-done.7.refs_6_
  101.9 20.1 %shard_map.91 = (bf16[4,512,128]{2,1,0:T(8,128)(2,1)}, f32[4,512,128]{2,1,0:T(8,128)}, bf16[4,272,128]{2,1,0:T(8,128)(2,1)}) custom-call(s32[6]{0:T(128)} %stack.42.place_ref, f32[16]{0:T(128)} %rate_ref.1, f32[16]{0:T(128)} %bias_ref.1, bf16[512,2048]{1,0:T(8,128)(2,1)} %all-gather.4.cloned.1.call-done.refs_0_, bf16[4,16,16,512]{3,2,1,0:T(8,128)(2,1)} %copy-done.3, ...), custom_call_target="tpu_custom_call" | custom-call | tf_op jit(solution)/shard_map/pallas_call | solution.py:265
  122.0 37.3 %all_to_all.25.part_ref = bf16[4,272,128]{2,1,0:T(8,128)(2,1)} all-to-all(bf16[4,272,128]{2,1,0:T(8,128)(2,1)} %get-tuple-element.12), channel_id=1, replica_groups=mesh['tm_0'=4,'tm_1'=4,'tm_2'=2,'zh'=4,'zl'=4] {'zh'}, dimensions={0} | all-to-all | bytes 557056 | tf_op jit(solution)/shard_map/all_to_all | solution.py:282
  159.3 2.9 %shard_map.92 = (f32[4,256,128]{2,1,0:T(8,128)}, f32[256,128]{1,0:T(8,128)}) custom-call(bf16[4,272,128]{2,1,0:T(8,128)(2,1)} %all_to_all.25.part_ref), custom_call_target="tpu_custom_call" | custom-call | tf_op jit(solution)/shard_map/pallas_call | solution.py:283
  162.2 13.9 %all-gather = f32[1024,128]{1,0:T(8,128)S(1)} all-gather(f32[256,128]{1,0:T(8,128)} %get-tuple-element.13), channel_id=2, replica_groups=mesh['tm_0'=4,'tm_1'=4,'tm_2'=2,'zh'=4,'zl'=4] {'tm_1'}, dimensions={0}, use_global_device_ids=true | all-gather | bytes 655360 | tf_op jit(solution)/shard_map/all_gather | solution.py:292
  176.1 1.9 collective-permute-start.10
  178.1 1.9 collective-permute-done.10.other_ref
  179.9 0.8 copy-done.7
  180.7 4.6 %shard_map.93 = (f32[256,128]{1,0:T(8,128)}, f32[256,128]{1,0:T(8,128)}) custom-call(s32[6]{0:T(128)} %stack.42.place_ref, f32[4,256,128]{2,1,0:T(8,128)} %bitcast.53, f32[4,256,128]{2,1,0:T(8,128)} %copy-done.7), custom_call_target="tpu_custom_call" | custom-call | tf_op jit(solution)/shard_map/pallas_call | solution.py:294
  185.4 14.5 %all-gather.1 = f32[1024,128]{1,0:T(8,128)} all-gather(f32[256,128]{1,0:T(8,128)} %get-tuple-element.14), channel_id=3, replica_groups=mesh['tm_0'=4,'tm_1'=4,'tm_2'=2,'zh'=4,'zl'=4] {'tm_0'}, dimensions={0}, use_global_device_ids=true | all-gather | bytes 655360 | tf_op jit(solution)/shard_map/all_gather | solution.py:300
  199.9 3.1 %shard_map.94 = bf16[4,128,128]{2,1,0:T(8,128)(2,1)} custom-call(s32[6]{0:T(128)} %stack.42.place_ref, f32[4,256,128]{2,1,0:T(8,128)} %bitcast.51, f32[256,128]{1,0:T(8,128)} %get-tuple-element.15.prefix_ref, f32[4,256,128]{2,1,0:T(8,128)} %get-tuple-element.16.inner_ref), custom_call_target="tpu_custom_call" | custom-call | tf_op jit(solution)/shard_map/pallas_call | solution.py:301
  203.0 18.9 %all_to_all.26.state_ref = bf16[4,128,128]{2,1,0:T(8,128)(2,1)S(1)} all-to-all(bf16[4,128,128]{2,1,0:T(8,128)(2,1)} %shard_map.94), channel_id=1, replica_groups=mesh['tm_0'=4,'tm_1'=4,'tm_2'=2,'zh'=4,'zl'=4] {'zh'}, dimensions={0} | all-to-all | bytes 262144 | tf_op jit(solution)/shard_map/all_to_all | solution.py:307
  222.0 0.3 shard_map.95
  222.3 13.8 %all_to_all.27 = bf16[4,4,128,128]{3,2,0,1:T(8,128)(2,1)S(1)} all-to-all(bf16[4,4,128,128]{3,2,0,1:T(8,128)(2,1)S(1)} %copy.28), channel_id=1, replica_groups=mesh['tm_0'=4,'tm_1'=4,'tm_2'=2,'zh'=4,'zl'=4] {'zl'}, dimensions={1} | all-to-all | bytes 1048576 | tf_op jit(solution)/shard_map/all_to_all | solution.py:315
  236.2 0.3 fusion
  236.5 0.3 fusion.2
  236.9 0.3 copy.29
  237.2 1.0 copy.30
  (36 shorter events, 0.4 us)
Async XLA Ops:
  6.5 1.9 copy-start
  6.5 95.3 %all-gather.4.cloned.1.call-start = ((), (), s32[]{:S(2)}) async-start(), calls=%async_computation.4 | async-start | bytes 2621440 | tf_op jit(solution)/shard_map/all_gather | solution.py:257
  43.9 9.0 %collective-permute-start.2 = (bf16[16,16,512]{2,1,0:T(8,128)(2,1)S(1)}, bf16[16,16,512]{2,1,0:T(8,128)(2,1)S(1)}, u32[]{:S(2)}, u32[]{:S(2)}) collective-permute-start(bf16[16,16,512]{2,1,0:T(8,128)(2,1)S(1)} %all_to_all.24), channel_id=1, source_target_pairs={{0,96},{32,0},{64,32},{96,64},{1,97},{33,1},{65,33},{97,65},{2,98}... | collective-permute-start | bytes 786440 | tf_op jit(solution)/shard_map/ppermute | solution.py:221
  46.3 9.8 %collective-permute-start.1 = (bf16[16,16,512]{2,1,0:T(8,128)(2,1)S(1)}, bf16[16,16,512]{2,1,0:T(8,128)(2,1)S(1)}, u32[]{:S(2)}, u32[]{:S(2)}) collective-permute-start(bf16[16,16,512]{2,1,0:T(8,128)(2,1)S(1)} %all_to_all.24), channel_id=1, source_target_pairs={{0,64},{32,96},{64,0},{96,32},{1,65},{33,97},{65,1},{97,33},{2,66}... | collective-permute-start | bytes 786440 | tf_op jit(solution)/shard_map/ppermute | solution.py:221
  51.0 8.3 %collective-permute-start = (bf16[16,16,512]{2,1,0:T(8,128)(2,1)S(1)}, bf16[16,16,512]{2,1,0:T(8,128)(2,1)S(1)}, u32[]{:S(2)}, u32[]{:S(2)}) collective-permute-start(bf16[16,16,512]{2,1,0:T(8,128)(2,1)S(1)} %all_to_all.24), channel_id=1, source_target_pairs={{0,32},{32,64},{64,96},{96,0},{1,33},{33,65},{65,97},{97,1},{2,34}... | collective-permute-start | bytes 786440 | tf_op jit(solution)/shard_map/ppermute | solution.py:221
  59.4 42.5 %copy-start.3 = (bf16[4,16,16,512]{3,2,1,0:T(8,128)(2,1)}, bf16[4,16,16,512]{3,2,1,0:T(8,128)(2,1)S(1)}, u32[]{:S(2)}) copy-start(bf16[4,16,16,512]{3,2,1,0:T(8,128)(2,1)S(1)} %pad_maximum_fusion.refs_1_) | copy-start | bytes 3145732
  60.4 31.3 %collective-permute-start.5 = (bf16[4,16,16,384]{3,2,1,0:T(8,128)(2,1)}, bf16[4,16,16,384]{3,2,1,0:T(8,128)(2,1)S(1)}, u32[]{:S(2)}, u32[]{:S(2)}) collective-permute-start(bf16[4,16,16,384]{3,2,1,0:T(8,128)(2,1)} %slice.4), channel_id=1, source_target_pairs={{0,384},{128,0},{256,128},{384,256},{1,385},{129,1},{257,129},{385... | collective-permute-start | bytes 2359304 | tf_op jit(solution)/shard_map/ppermute | solution.py:221
  65.5 28.2 %collective-permute-start.4 = (bf16[4,16,16,384]{3,2,1,0:T(8,128)(2,1)}, bf16[4,16,16,384]{3,2,1,0:T(8,128)(2,1)S(1)}, u32[]{:S(2)}, u32[]{:S(2)}) collective-permute-start(bf16[4,16,16,384]{3,2,1,0:T(8,128)(2,1)} %slice.4), channel_id=1, source_target_pairs={{0,256},{128,384},{256,0},{384,128},{1,257},{129,385},{257,1},{385... | collective-permute-start | bytes 2359304 | tf_op jit(solution)/shard_map/ppermute | solution.py:221
  67.9 29.4 %collective-permute-start.3 = (bf16[4,16,16,384]{3,2,1,0:T(8,128)(2,1)}, bf16[4,16,16,384]{3,2,1,0:T(8,128)(2,1)}, u32[]{:S(2)}, u32[]{:S(2)}) collective-permute-start(bf16[4,16,16,384]{3,2,1,0:T(8,128)(2,1)} %slice.4), channel_id=1, source_target_pairs={{0,128},{128,256},{256,384},{384,0},{1,129},{129,257},{257,385},{3... | collective-permute-start | bytes 2359304 | tf_op jit(solution)/shard_map/ppermute | solution.py:221
  70.8 29.0 %collective-permute-start.6 = (bf16[4,16,16,384]{3,2,1,0:T(8,128)(2,1)}, bf16[4,16,16,384]{3,2,1,0:T(8,128)(2,1)}, u32[]{:S(2)}, u32[]{:S(2)}) collective-permute-start(bf16[4,16,16,384]{3,2,1,0:T(8,128)(2,1)} %slice.4), channel_id=1, source_target_pairs={{0,16},{16,0},{1,17},{17,1},{2,18},{18,2},{3,19},{19,3},{4,20},{20... | collective-permute-start | bytes 2359304 | tf_op jit(solution)/shard_map/ppermute | solution.py:221
  91.7 10.1 %copy-start.5 = (bf16[4,16,16,384]{3,2,1,0:T(8,128)(2,1)}, bf16[4,16,16,384]{3,2,1,0:T(8,128)(2,1)S(1)}, u32[]{:S(2)}) copy-start(bf16[4,16,16,384]{3,2,1,0:T(8,128)(2,1)S(1)} %collective-permute-done.5.refs_4_) | copy-start | bytes 2359300
  91.7 8.2 %collective-permute-start.9 = (bf16[4,16,16,384]{3,2,1,0:T(8,128)(2,1)S(1)}, bf16[4,16,16,384]{3,2,1,0:T(8,128)(2,1)}, u32[]{:S(2)}, u32[]{:S(2)}) collective-permute-start(bf16[4,16,16,384]{3,2,1,0:T(8,128)(2,1)S(1)} %collective-permute-done.5.refs_4_), channel_id=1, source_target_pairs={{0,16},{16,0},{1,17},{17,1},{2,18},{18,2},{3,19},{19,3},{4,20},{20... | collective-permute-start | bytes 2359304 | tf_op jit(solution)/shard_map/ppermute | solution.py:221
  93.7 8.2 %copy-start.6 = (bf16[4,16,16,384]{3,2,1,0:T(8,128)(2,1)}, bf16[4,16,16,384]{3,2,1,0:T(8,128)(2,1)S(1)}, u32[]{:S(2)}) copy-start(bf16[4,16,16,384]{3,2,1,0:T(8,128)(2,1)S(1)} %collective-permute-done.4.refs_3_) | copy-start | bytes 2359300
  93.7 6.2 %collective-permute-start.8 = (bf16[4,16,16,384]{3,2,1,0:T(8,128)(2,1)S(1)}, bf16[4,16,16,384]{3,2,1,0:T(8,128)(2,1)}, u32[]{:S(2)}, u32[]{:S(2)}) collective-permute-start(bf16[4,16,16,384]{3,2,1,0:T(8,128)(2,1)S(1)} %collective-permute-done.4.refs_3_), channel_id=1, source_target_pairs={{0,16},{16,0},{1,17},{17,1},{2,18},{18,2},{3,19},{19,3},{4,20},{20... | collective-permute-start | bytes 2359304 | tf_op jit(solution)/shard_map/ppermute | solution.py:221
  97.4 4.5 %collective-permute-start.7 = (bf16[4,16,16,384]{3,2,1,0:T(8,128)(2,1)}, bf16[4,16,16,384]{3,2,1,0:T(8,128)(2,1)}, u32[]{:S(2)}, u32[]{:S(2)}) collective-permute-start(bf16[4,16,16,384]{3,2,1,0:T(8,128)(2,1)} %collective-permute-done.3.refs_2_), channel_id=1, source_target_pairs={{0,16},{16,0},{1,17},{17,1},{2,18},{18,2},{3,19},{19,3},{4,20},{20... | collective-permute-start | bytes 2359304 | tf_op jit(solution)/shard_map/ppermute | solution.py:221
  159.3 62.7 %copy-start.1 = (f32[4,512,128]{2,1,0:T(8,128)S(1)}, f32[4,512,128]{2,1,0:T(8,128)}, u32[]{:S(2)}) copy-start(f32[4,512,128]{2,1,0:T(8,128)} %get-tuple-element.18.own_ref) | copy-start | bytes 3145732
  159.3 62.7 %copy-start.2 = (bf16[4,512,128]{2,1,0:T(8,128)(2,1)S(1)}, bf16[4,512,128]{2,1,0:T(8,128)(2,1)}, u32[]{:S(2)}) copy-start(bf16[4,512,128]{2,1,0:T(8,128)(2,1)} %get-tuple-element.17.reach_ref) | copy-start | bytes 1572868
  176.1 3.8 %copy-start.4 = (f32[1024,128]{1,0:T(8,128)}, f32[1024,128]{1,0:T(8,128)S(1)}, u32[]{:S(2)}) copy-start(f32[1024,128]{1,0:T(8,128)S(1)} %all-gather) | copy-start | bytes 1572868
  176.1 3.8 %collective-permute-start.10 = (f32[4,256,128]{2,1,0:T(8,128)S(1)}, f32[4,256,128]{2,1,0:T(8,128)S(1)}, u32[]{:S(2)}, u32[]{:S(2)}) collective-permute-start(f32[4,256,128]{2,1,0:T(8,128)S(1)} %bitcast.52), channel_id=1, source_target_pairs={{0,16},{16,0},{1,17},{17,1},{2,18},{18,2},{3,19},{19,3},{4,20},{20... | collective-permute-start | bytes 1572872 | tf_op jit(solution)/shard_map/ppermute | solution.py:293
  179.9 0.8 copy-start.7
  222.0 14.6 %copy-start.8 = (f32[128]{0:T(128)S(1)}, f32[128]{0:T(128)}, u32[]{:S(2)}) copy-start(f32[128]{0:T(128)} %param.17) | copy-start | bytes 1540
Sparse Core Ops, SparseCore 0:
  9.5 63.8 all-gather.3

commit v4 on v1

--- a/solution.py
+++ b/solution.py
@@ -12,6 +12,8 @@
 CHUNK = 128
 GANG = 8
 WIDE = 512
+MAP_ROWS = 272
+PLANE = ("tm_0", "tm_1", "tm_2")
 TM_STREAM = ("tm_0", "tm_1", "tm_2", "stream")
 f32 = jnp.float32
 bf16 = jnp.bfloat16
@@ -23,21 +25,31 @@
     )
 
 
-def mm_exact(a, b, ca=1, cb=0):
-    return lax.dot_general(
-        a, b, (((ca,), (cb,)), ((), ())), precision=lax.Precision.HIGHEST, preferred_element_type=f32
-    )
-
-
-def chunk_kernel(gate_ref, raw_ref, reach_ref, own_ref, total_ref):
-    rate, bias = gate_ref[0], gate_ref[1]
+def chunk_kernel(
+    head_ref,
+    rate_ref,
+    bias_ref,
+    token_ref,
+    weight_ref,
+    reach_ref,
+    own_ref,
+    total_ref,
+    raw_ref,
+    state_ref,
+):
+    rate, bias = rate_ref[head_ref[0]], bias_ref[head_ref[0]]
+    raw_ref[...] = jnp.dot(token_ref[...], weight_ref[...], preferred_element_type=f32)
     row = lax.broadcasted_iota(jnp.int32, (CHUNK, CHUNK), 0)
     col = lax.broadcasted_iota(jnp.int32, (CHUNK, CHUNK), 1)
     strict, inclusive = row > col, row >= col
     eye = jnp.where(row == col, 1.0, 0.0).astype(f32)
     ones_below = jnp.where(inclusive, 1.0, 0.0).astype(bf16)
-    total_ref[0:DK, :] = eye
-    total_ref[DK:, :] = jnp.zeros((DV, DK), f32)
+
+    @pl.when(pl.program_id(0) == 0)
+    def _():
+        state_ref[0:DK, :] = eye
+        state_ref[DK : DK + DV, :] = jnp.zeros((DV, DK), f32)
+        state_ref[DK + DV :, :] = jnp.ones((8, DK), f32)
 
     def below(size):
         return (
@@ -105,7 +117,7 @@
         change = [mm(wu[i] * tail2[i], k[i], 0, 0) for i in each]
         inside = [mm(scores[i], wu[i]) for i in each]
         reach = [grow[i] * q[i].astype(f32) - inside[i][:, :DK] for i in each]
-        state = total_ref[...]
+        state, kept = state_ref[0 : DK + DV, :], state_ref[DK + DV :, :]
         for i in each:
             out = mm(reach[i], state, 1, 1)
             reach_ref[pl.ds(starts[i], CHUNK), :] = out[:, :DK].astype(bf16)
@@ -113,49 +125,30 @@
             moved = mm(state, change[i][:DK])
             state = last[i] * state - moved
             state = jnp.concatenate([state[:DK], state[DK:] + change[i][DK:]], 0)
-        total_ref[...] = state
+            kept = last[i] * kept
+        state_ref[0 : DK + DV, :] = state
+        state_ref[DK + DV :, :] = kept
         return carry
 
     lax.fori_loop(0, raw_ref.shape[0] // (CHUNK * GANG), gang, 0)
 
-
-def join_kernel(place_ref, mine_ref, other_ref, prefix_ref, total_ref):
-    place, core = place_ref[0], place_ref[1]
-    row = lax.broadcasted_iota(jnp.int32, (DK + DV, DK), 0)
-    col = lax.broadcasted_iota(jnp.int32, (DK + DV, DK), 1)
-    state = jnp.where(row == col, 1.0, 0.0).astype(f32)
-    prefix_ref[...] = state
-    for j in range(8):
-        piece = jnp.where(core == j % 2, mine_ref[j // 2], other_ref[j // 2])
-        moved = mm_exact(state, piece[:DK])
-        state = jnp.concatenate([moved[:DK], moved[DK:] + piece[DK:]], 0)
-
-        @pl.when(place == j + 1)
-        def _():
-            prefix_ref[...] = state
-
-    total_ref[...] = state
-
-
-def read_kernel(place_ref, outer_ref, prefix_ref, reach_ref, own_ref, read_ref):
-    place = place_ref[2]
-    state = jnp.zeros((DV, DK), f32)
-    for j in range(3):
-        moved = mm_exact(state, outer_ref[j, :DK]) + outer_ref[j, DK:]
-        state = jnp.where(j < place, moved, state)
-    state = mm_exact(state, prefix_ref[:DK]) + prefix_ref[DK:]
+    @pl.when(pl.program_id(0) == pl.num_programs(0) - 1)
+    def _():
+        kept = state_ref[DK + DV :, :]
+        part = kept.astype(bf16).astype(f32)
+        total_ref[0:DK, :] = (state_ref[0:DK, :] - kept[0:1] * eye).astype(bf16)
+        total_ref[DK : DK + DV, :] = state_ref[DK : DK + DV, :].astype(bf16)
+        total_ref[DK + DV :, :] = jnp.concatenate([part, kept - part], 0).astype(bf16)
+
+
+def read_kernel(place_ref, map_ref, reach_ref, own_ref, read_ref):
+    def one(j, state):
+        kept = map_ref[j, DK + DV : MAP_ROWS, :].astype(f32)
+        kept = kept[0:1] + kept[8:9]
+        return kept * state + mm(state, map_ref[j, 0:DK, :]) + map_ref[j, DK : DK + DV, :].astype(f32)
+
+    state = lax.fori_loop(0, place_ref[0], one, jnp.zeros((DV, DK), f32))
     read_ref[...] = (mm(reach_ref[...], state, 1, 1) + own_ref[...]).astype(bf16)
-
-
-def ring_gather(x, axis):
-    size, me = lax.axis_size(axis), lax.axis_index(axis)
-    out = jnp.zeros((size,) + x.shape, x.dtype)
-    for shift in range(size):
-        piece = x
-        if shift:
-            piece = lax.ppermute(x, axis, [(i, (i + shift) % size) for i in range(size)])
-        out = lax.dynamic_update_index_in_dim(out, piece, lax.rem(me - shift + size, size), 0)
-    return out
 
 
 def shards(
@@ -188,46 +181,50 @@
     ).transpose(1, 0, 2)
     all_tokens = lax.all_gather(tokens, "stream", axis=0, tiled=True)
     weights = lax.all_to_all(weights, "stream", split_axis=0, concat_axis=0, tiled=True)
-    weights = ring_gather(ring_gather(weights, "tm_1"), "tm_0")
-    weights = weights.transpose(2, 0, 1, 3, 4).reshape(streams * shares * rows, WIDE)
-
-    raw = jnp.dot(all_tokens, weights, preferred_element_type=f32)
-    block_rows = raw.shape[0]
-    gates = jnp.stack(
-        [
-            lax.dynamic_index_in_dim(decay_rate, head, 0, False),
-            lax.dynamic_index_in_dim(beta_bias, head, 0, False),
-        ]
-    )
+    weights = jnp.broadcast_to(weights[None], (shares,) + weights.shape)
+    weights = lax.all_to_all(weights, ("tm_0", "tm_1"), split_axis=0, concat_axis=0, tiled=True)
+    weights = weights.transpose(1, 0, 2, 3).reshape(streams * shares * rows, WIDE)
+
+    block_rows, features = all_tokens.shape
+    stretch = CHUNK * GANG
     reach, own, total = pl.pallas_call(
         chunk_kernel,
         out_shape=(
             jax.ShapeDtypeStruct((block_rows, DK), bf16),
             jax.ShapeDtypeStruct((block_rows, DV), f32),
-            jax.ShapeDtypeStruct((DK + DV, DK), f32),
+            jax.ShapeDtypeStruct((MAP_ROWS, DK), bf16),
         ),
-        in_specs=[smem, vmem],
-        out_specs=(vmem, vmem, vmem),
+        grid=(block_rows // stretch,),
+        in_specs=[
+            smem,
+            smem,
+            smem,
+            pl.BlockSpec((stretch, features), lambda i: (i, 0)),
+            pl.BlockSpec((features, WIDE), lambda i: (0, 0)),
+        ],
+        out_specs=(
+            pl.BlockSpec((stretch, DK), lambda i: (i, 0)),
+            pl.BlockSpec((stretch, DV), lambda i: (i, 0)),
+            pl.BlockSpec((MAP_ROWS, DK), lambda i: (0, 0)),
+        ),
+        scratch_shapes=[
+            pltpu.VMEM((stretch, WIDE), f32),
+            pltpu.VMEM((DK + DV + 8, DK), f32),
+        ],
         compiler_params=pltpu.CompilerParams(vmem_limit_bytes=48 * 2**20),
-    )(gates, raw)
-
-    place = jnp.stack([at_x * 2 + at_c, at_c, at_y]).astype(jnp.int32)
-    mine = lax.all_gather(total, "tm_1", axis=0)
-    other = lax.ppermute(mine, "tm_2", [(0, 1), (1, 0)])
-    prefix, subtotal = pl.pallas_call(
-        join_kernel,
-        out_shape=(jax.ShapeDtypeStruct((DK + DV, DK), f32),) * 2,
-        in_specs=[smem, vmem, vmem],
-        out_specs=(vmem, vmem),
-    )(place, mine, other)
-    outer = lax.all_gather(subtotal, "tm_0", axis=0)
+    )(head.reshape(1).astype(jnp.int32), decay_rate, beta_bias, all_tokens, weights)
+
+    runs = 32
+    maps = jnp.broadcast_to(total[None], (runs,) + total.shape)
+    maps = lax.all_to_all(maps, PLANE, split_axis=0, concat_axis=0, tiled=True)
+    place = ((at_y * 4 + at_x) * 2 + at_c).reshape(1).astype(jnp.int32)
     readout = pl.pallas_call(
         read_kernel,
         out_shape=jax.ShapeDtypeStruct((block_rows, DV), bf16),
-        in_specs=[smem, vmem, vmem, vmem, vmem],
+        in_specs=[smem, vmem, vmem, vmem],
         out_specs=vmem,
         compiler_params=pltpu.CompilerParams(vmem_limit_bytes=32 * 2**20),
-    )(place, outer, prefix, reach, own)
+    )(place, maps, reach, own)
     returned = lax.all_to_all(readout, "stream", split_axis=0, concat_axis=1, tiled=True)
     head_read = returned.reshape(local_rows, HEADS, DV).astype(f32)
     normed = (

time: 224 us -> 228 us (1.018)
  the two profiles are of different devices: /device:TPU:66 before, /device:TPU:48 now
where the time goes in v4:
time: 228 us; the launch traced here: 227 us
  waiting for transfers between devices  127 us (56%)
  blocking collectives  29.2 us (13%)
  starting transfers between devices  24.7 us (11%)
  Pallas kernels  20.1 us (9%)
  between operations  13.5 us (6%)
  local copies, waits for them, and re-layouts  10.8 us (5%)
    all_gather x1, waiting for transfers between devices, shards(): all_tokens = lax.all_gather(tokens, 'stream', axis=0, tiled=True)  42.7 us
    all_to_all x1, waiting for transfers between devices, shards(): lax.all_to_all(readout, 'stream', split_axis=0, concat_axis=1, tiled=True)  29.7 us
    all_to_all x1, blocking collectives, shards(): lax.all_to_all(weights, 'stream', split_axis=0, concat_axis=0, tiled=True)  29.2 us
    all_to_all x1, waiting for transfers between devices, shards(): maps = lax.all_to_all(maps, PLANE, split_axis=0, concat_axis=0, tiled=True)  29 us
    all_to_all x1, waiting for transfers between devices, shards(): lax.all_to_all(weights, ('tm_0', 'tm_1'), split_axis=0, concat_axis=0, ti...  25 us
    pallas_call x1, Pallas kernels, shards(): pl.pallas_call(chunk_kernel, out_shape=(jax.ShapeDtypeStruct((block_rows,...  16.8 us
    all_to_all x1, starting transfers between devices, shards(): lax.all_to_all(readout, 'stream', split_axis=0, concat_axis=1, tiled=True)  10 us
    all_to_all x1, starting transfers between devices, shards(): maps = lax.all_to_all(maps, PLANE, split_axis=0, concat_axis=0, tiled=True)  7.41 us
  transfers between devices with their start and end apart: 4, of which 4 were waited for; matrix products, arithmetic and copies ran while one was open for 2% of the time, Pallas kernels for 0%

profile of v4, /device:TPU:48, one launch (start us, length us, event | category | flops | bytes accessed | tf_op | source)
XLA Modules:
  0.0 227.0 jit_solution(7305706169200182635)
XLA Ops:
  6.5 0.0 copy-start
  6.5 0.0 all-gather.2.cloned.1.call-start
  6.5 0.7 all-gather.2.cloned.1.call-update
  7.3 0.8 constant_dynamic-slice_fusion
  8.1 0.1 copy.21
  8.1 0.1 copy.17
  8.3 0.1 copy.22
  8.4 0.1 copy.18
  8.5 0.0 copy-done
  8.6 0.8 dynamic-slice_bitcast_fusion
  9.4 0.1 concatenate.3
  9.5 29.2 %all_to_all.28 = bf16[16,8,512]{2,1,0:T(8,128)(2,1)S(1)} all-to-all(bf16[16,8,512]{2,1,0:T(8,128)(2,1)S(1)} %bitcast.34), channel_id=1, replica_groups=mesh['tm_0'=4,'tm_1'=4,'tm_2'=2,'stream'=16] {'stream'}, dimensions={0} | all-to-all | bytes 262144 | tf_op jit(solution)/shard_map/all_to_all | solution.py:183
  38.7 1.6 broadcast_in_dim.7
  40.3 7.3 %all-to-all-start.1 = ((bf16[16,16,8,512]{3,2,1,0:T(8,128)(2,1)}), bf16[16,16,8,512]{3,2,1,0:T(8,128)(2,1)S(1)}, u32[]{:S(2)}, u32[]{:S(2)}) async-start(bf16[16,16,8,512]{3,2,1,0:T(8,128)(2,1)} %broadcast_in_dim.7), calls=%async_computation.1 | async-start | bytes 4194304 | tf_op jit(solution)/shard_map/all_to_all | solution.py:185
  47.6 0.0 copy-start.3
  47.6 0.0 copy-start.4
  47.6 25.0 %all-to-all-done.1 = bf16[16,16,8,512]{3,2,1,0:T(8,128)(2,1)S(1)} async-done(((bf16[16,16,8,512]{3,2,1,0:T(8,128)(2,1)}), bf16[16,16,8,512]{3,2,1,0:T(8,128)(2,1)S(1)}, u32[]{:S(2)}, u32[]{:S(2)}) %all-to-all-start.1) | async-done | bytes 2097184 | tf_op jit(solution)/shard_map/all_to_all | solution.py:185
  72.6 0.0 copy-start.5
  72.6 1.4 copy-done.5
  74.0 1.8 copy.19
  75.8 42.7 %all-gather.2.cloned.1.call-done.token_ref = bf16[2048,2048]{1,0:T(8,128)(2,1)} async-done(((bf16[128,2048]{1,0:T(8,128)(2,1)}), bf16[2048,2048]{1,0:T(8,128)(2,1)}) %all-gather.2.cloned.1.call-update) | async-done | bytes 8388624 | tf_op jit(solution)/shard_map/all_gather | solution.py:182
  118.5 0.0 copy-done.3
  118.5 0.0 copy-done.4
  118.5 16.8 %shard_map.91 = (bf16[2048,128]{1,0:T(8,128)(2,1)S(1)}, f32[2048,128]{1,0:T(8,128)S(1)}, bf16[272,128]{1,0:T(8,128)(2,1)S(1)}) custom-call(s32[1]{0:T(128)} %bitcast.1.head_ref, f32[16]{0:T(128)S(1)} %copy-done.3, f32[16]{0:T(128)S(1)} %copy-done.4, bf16[2048,2048]{1,0:T(8,128)(2,1)} %all-gather.2.cloned.1.call-done.token_ref, bf16[2048,512]{1,0:T(8,128)(2,1)S(1)} %bitcast.32), custom_call_target="tpu_custom_call" | custom-call | tf_op jit(solution)/shard_map/pallas_call | solution.py:190
  135.3 0.0 copy-start.1
  135.3 1.0 copy-done.1
  136.3 1.7 broadcast_in_dim.8
  137.9 7.4 %all-to-all-start.2 = ((bf16[32,272,128]{2,1,0:T(8,128)(2,1)}), bf16[32,272,128]{2,1,0:T(8,128)(2,1)S(1)}, u32[]{:S(2)}, u32[]{:S(2)}) async-start(bf16[32,272,128]{2,1,0:T(8,128)(2,1)} %broadcast_in_dim.8), calls=%async_computation.2 | async-start | bytes 4456448 | tf_op jit(solution)/shard_map/all_to_all | solution.py:219
  145.4 29.0 %all-to-all-done.2.map_ref = bf16[32,272,128]{2,1,0:T(8,128)(2,1)S(1)} async-done(((bf16[32,272,128]{2,1,0:T(8,128)(2,1)}), bf16[32,272,128]{2,1,0:T(8,128)(2,1)S(1)}, u32[]{:S(2)}, u32[]{:S(2)}) %all-to-all-start.2) | async-done | bytes 2228256 | tf_op jit(solution)/shard_map/all_to_all | solution.py:219
  174.4 0.0 copy-start.2
  174.4 1.2 copy-done.2
  175.6 0.0 copy-start.6
  175.6 3.3 %shard_map.92 = bf16[2048,128]{1,0:T(8,128)(2,1)} custom-call(s32[1]{0:T(128)} %bitcast.place_ref, bf16[32,272,128]{2,1,0:T(8,128)(2,1)S(1)} %all-to-all-done.2.map_ref, bf16[2048,128]{1,0:T(8,128)(2,1)S(1)} %get-tuple-element.9.reach_ref, f32[2048,128]{1,0:T(8,128)S(1)} %copy-done.2), custom_call_target="tpu_custom_call" | custom-call | tf_op jit(solution)/shard_map/pallas_call | solution.py:221
  179.0 10.0 %all-to-all-start.3 = ((bf16[16,128,128]{2,1,0:T(8,128)(2,1)}), bf16[16,128,128]{2,1,0:T(8,128)(2,1)S(1)}, u32[]{:S(2)}, u32[]{:S(2)}) async-start(bf16[16,128,128]{2,1,0:T(8,128)(2,1)} %bitcast.10), calls=%async_computation.3 | async-start | bytes 1048576 | tf_op jit(solution)/shard_map/all_to_all | solution.py:228
  189.0 0.0 copy-done.6
  189.0 29.7 %all-to-all-done.3 = bf16[16,128,128]{2,1,0:T(8,128)(2,1)S(1)} async-done(((bf16[16,128,128]{2,1,0:T(8,128)(2,1)}), bf16[16,128,128]{2,1,0:T(8,128)(2,1)S(1)}, u32[]{:S(2)}, u32[]{:S(2)}) %all-to-all-start.3) | async-done | bytes 524320 | tf_op jit(solution)/shard_map/all_to_all | solution.py:228
  218.7 0.3 fusion.2
  219.1 1.1 fusion.3
  (4 shorter events, 0.0 us)
Async XLA Ops:
  6.5 2.0 copy-start
  6.5 112.0 %all-gather.2.cloned.1.call-start = ((), (), s32[]{:S(2)}) async-start(), calls=%async_computation.4 | async-start | bytes 8912896 | tf_op jit(solution)/shard_map/all_gather | solution.py:182
  40.3 32.4 %all-to-all-start.1 = ((bf16[16,16,8,512]{3,2,1,0:T(8,128)(2,1)}), bf16[16,16,8,512]{3,2,1,0:T(8,128)(2,1)S(1)}, u32[]{:S(2)}, u32[]{:S(2)}) async-start(bf16[16,16,8,512]{3,2,1,0:T(8,128)(2,1)} %broadcast_in_dim.7), calls=%async_computation.1 | async-start | bytes 4194304 | tf_op jit(solution)/shard_map/all_to_all | solution.py:185
  47.6 71.0 %copy-start.3 = (f32[16]{0:T(128)S(1)}, f32[16]{0:T(128)}, u32[]{:S(2)}) copy-start(f32[16]{0:T(128)} %rate_ref.1) | copy-start | bytes 196
  47.6 71.0 %copy-start.4 = (f32[16]{0:T(128)S(1)}, f32[16]{0:T(128)}, u32[]{:S(2)}) copy-start(f32[16]{0:T(128)} %bias_ref.1) | copy-start | bytes 196
  72.6 1.4 copy-start.5
  135.3 1.0 copy-start.1
  137.9 36.4 %all-to-all-start.2 = ((bf16[32,272,128]{2,1,0:T(8,128)(2,1)}), bf16[32,272,128]{2,1,0:T(8,128)(2,1)S(1)}, u32[]{:S(2)}, u32[]{:S(2)}) async-start(bf16[32,272,128]{2,1,0:T(8,128)(2,1)} %broadcast_in_dim.8), calls=%async_computation.2 | async-start | bytes 4456448 | tf_op jit(solution)/shard_map/all_to_all | solution.py:219
  174.4 1.2 copy-start.2
  175.6 13.4 %copy-start.6 = (f32[128]{0:T(128)S(1)}, f32[128]{0:T(128)}, u32[]{:S(2)}) copy-start(f32[128]{0:T(128)} %param.17) | copy-start | bytes 1540
  179.0 39.7 %all-to-all-start.3 = ((bf16[16,128,128]{2,1,0:T(8,128)(2,1)}), bf16[16,128,128]{2,1,0:T(8,128)(2,1)S(1)}, u32[]{:S(2)}, u32[]{:S(2)}) async-start(bf16[16,128,128]{2,1,0:T(8,128)(2,1)} %bitcast.10), calls=%async_computation.3 | async-start | bytes 1048576 | tf_op jit(solution)/shard_map/all_to_all | solution.py:228
Sparse Core Ops, SparseCore 0:
  9.4 109.0 all-gather.1

commit v5 on v4

--- a/solution.py
+++ b/solution.py
@@ -13,7 +13,6 @@
 GANG = 8
 WIDE = 512
 MAP_ROWS = 272
-PLANE = ("tm_0", "tm_1", "tm_2")
 TM_STREAM = ("tm_0", "tm_1", "tm_2", "stream")
 f32 = jnp.float32
 bf16 = jnp.bfloat16
@@ -141,13 +140,45 @@
         total_ref[DK + DV :, :] = jnp.concatenate([part, kept - part], 0).astype(bf16)
 
 
-def read_kernel(place_ref, map_ref, reach_ref, own_ref, read_ref):
+def opened(map_ref, *at):
+    kept = map_ref[(*at, slice(DK + DV, MAP_ROWS))].astype(f32)
+    change, shift = map_ref[(*at, slice(0, DK))], map_ref[(*at, slice(DK, DK + DV))]
+    return change, shift.astype(f32), kept[0:1] + kept[8:9]
+
+
+def join_kernel(core_ref, mine_ref, other_ref, copies_ref):
+    def write(first_ref, second_ref):
+        change, shift, kept = opened(first_ref)
+        next_change, next_shift, next_kept = opened(second_ref)
+        joined = kept * next_change.astype(f32) + next_kept * change.astype(f32)
+        joined = (joined + mm(change, next_change)).astype(bf16)
+        shift = (next_kept * shift + mm(shift, next_change) + next_shift).astype(bf16)
+        kept = jnp.broadcast_to(kept * next_kept, (8, DK))
+        part = kept.astype(bf16).astype(f32)
+        kept = jnp.concatenate([part, kept - part], 0).astype(bf16)
+        for i in range(copies_ref.shape[0]):
+            copies_ref[i, 0:DK, :] = joined
+            copies_ref[i, DK : DK + DV, :] = shift
+            copies_ref[i, DK + DV : MAP_ROWS, :] = kept
+
+    @pl.when(core_ref[0] == 0)
+    def _():
+        write(mine_ref, other_ref)
+
+    @pl.when(core_ref[0] == 1)
+    def _():
+        write(other_ref, mine_ref)
+
+
+def read_kernel(place_ref, map_ref, other_ref, reach_ref, own_ref, read_ref):
+    def after(state, change, shift, kept):
+        return kept * state + mm(state, change) + shift
+
     def one(j, state):
-        kept = map_ref[j, DK + DV : MAP_ROWS, :].astype(f32)
-        kept = kept[0:1] + kept[8:9]
-        return kept * state + mm(state, map_ref[j, 0:DK, :]) + map_ref[j, DK : DK + DV, :].astype(f32)
+        return after(state, *opened(map_ref, j))
 
     state = lax.fori_loop(0, place_ref[0], one, jnp.zeros((DV, DK), f32))
+    state = jnp.where(place_ref[1] == 1, after(state, *opened(other_ref)), state)
     read_ref[...] = (mm(reach_ref[...], state, 1, 1) + own_ref[...]).astype(bf16)
 
 
@@ -214,17 +245,23 @@
         compiler_params=pltpu.CompilerParams(vmem_limit_bytes=48 * 2**20),
     )(head.reshape(1).astype(jnp.int32), decay_rate, beta_bias, all_tokens, weights)
 
-    runs = 32
-    maps = jnp.broadcast_to(total[None], (runs,) + total.shape)
-    maps = lax.all_to_all(maps, PLANE, split_axis=0, concat_axis=0, tiled=True)
-    place = ((at_y * 4 + at_x) * 2 + at_c).reshape(1).astype(jnp.int32)
+    core = at_c.reshape(1).astype(jnp.int32)
+    other = lax.ppermute(total, "tm_2", [(0, 1), (1, 0)])
+    maps = pl.pallas_call(
+        join_kernel,
+        out_shape=jax.ShapeDtypeStruct((shares, MAP_ROWS, DK), bf16),
+        in_specs=[smem, vmem, vmem],
+        out_specs=vmem,
+    )(core, total, other)
+    maps = lax.all_to_all(maps, ("tm_0", "tm_1"), split_axis=0, concat_axis=0, tiled=True)
+    place = jnp.stack([at_y * 4 + at_x, at_c]).astype(jnp.int32)
     readout = pl.pallas_call(
         read_kernel,
         out_shape=jax.ShapeDtypeStruct((block_rows, DV), bf16),
-        in_specs=[smem, vmem, vmem, vmem],
+        in_specs=[smem, vmem, vmem, vmem, vmem],
         out_specs=vmem,
         compiler_params=pltpu.CompilerParams(vmem_limit_bytes=32 * 2**20),
-    )(place, maps, reach, own)
+    )(place, maps, other, reach, own)
     returned = lax.all_to_all(readout, "stream", split_axis=0, concat_axis=1, tiled=True)
     head_read = returned.reshape(local_rows, HEADS, DV).astype(f32)
     normed = (

time: 228 us -> 216 us (0.947)
  the two profiles are of different devices: /device:TPU:48 before, /device:TPU:32 now
where the time goes in v5:
time: 216 us; the launch traced here: 215 us
  waiting for transfers between devices  117 us (54%)
  blocking collectives  29.2 us (14%)
  starting transfers between devices  26.4 us (12%)
  Pallas kernels  20.7 us (10%)
  between operations  13.5 us (6%)
  local copies, waits for them, and re-layouts  7.16 us (3%)
    all_gather x1, waiting for transfers between devices, shards(): all_tokens = lax.all_gather(tokens, 'stream', axis=0, tiled=True)  41.6 us
    all_to_all x1, blocking collectives, shards(): lax.all_to_all(weights, 'stream', split_axis=0, concat_axis=0, tiled=True)  29.2 us
    all_to_all x1, waiting for transfers between devices, shards(): lax.all_to_all(weights, ('tm_0', 'tm_1'), split_axis=0, concat_axis=0, ti...  27.7 us
    all_to_all x1, waiting for transfers between devices, shards(): lax.all_to_all(readout, 'stream', split_axis=0, concat_axis=1, tiled=True)  27.1 us
    all_to_all x1, waiting for transfers between devices, shards(): lax.all_to_all(maps, ('tm_0', 'tm_1'), split_axis=0, concat_axis=0, tiled...  18.6 us
    pallas_call x1, Pallas kernels, shards(): pl.pallas_call(chunk_kernel, out_shape=(jax.ShapeDtypeStruct((block_rows,...  16.7 us
    all_to_all x1, starting transfers between devices, shards(): lax.all_to_all(readout, 'stream', split_axis=0, concat_axis=1, tiled=True)  10 us
    all_to_all x1, starting transfers between devices, shards(): lax.all_to_all(maps, ('tm_0', 'tm_1'), split_axis=0, concat_axis=0, tiled...  7.15 us
  transfers between devices with their start and end apart: 5, of which 5 were waited for; matrix products, arithmetic and copies ran while one was open for 3% of the time, Pallas kernels for 0%

profile of v5, /device:TPU:32, one launch (start us, length us, event | category | flops | bytes accessed | tf_op | source)
XLA Modules:
  0.0 215.4 jit_solution(7833184902515408174)
XLA Ops:
  6.5 0.0 copy-start
  6.5 0.0 all-gather.2.cloned.1.call-start
  6.5 0.7 all-gather.2.cloned.1.call-update
  7.3 0.8 constant_dynamic-slice_fusion
  8.1 0.1 copy.21
  8.1 0.1 copy.17
  8.3 0.1 copy.22
  8.4 0.1 copy.18
  8.5 0.0 copy-done
  8.6 0.8 dynamic-slice_bitcast_fusion
  9.4 0.1 concatenate.3
  9.5 29.2 %all_to_all.28 = bf16[16,8,512]{2,1,0:T(8,128)(2,1)S(1)} all-to-all(bf16[16,8,512]{2,1,0:T(8,128)(2,1)S(1)} %bitcast.34), channel_id=1, replica_groups=mesh['tm_0'=4,'tm_1'=4,'tm_2'=2,'stream'=16] {'stream'}, dimensions={0} | all-to-all | bytes 262144 | tf_op jit(solution)/shard_map/all_to_all | solution.py:214
  38.7 1.5 broadcast_in_dim.5
  40.2 7.1 %all-to-all-start.1 = ((bf16[16,16,8,512]{3,2,1,0:T(8,128)(2,1)}), bf16[16,16,8,512]{3,2,1,0:T(8,128)(2,1)}, u32[]{:S(2)}, u32[]{:S(2)}) async-start(bf16[16,16,8,512]{3,2,1,0:T(8,128)(2,1)} %broadcast_in_dim.5), calls=%async_computation.1 | async-start | bytes 4194304 | tf_op jit(solution)/shard_map/all_to_all | solution.py:216
  47.3 27.7 %all-to-all-done.1 = bf16[16,16,8,512]{3,2,1,0:T(8,128)(2,1)} async-done(((bf16[16,16,8,512]{3,2,1,0:T(8,128)(2,1)}), bf16[16,16,8,512]{3,2,1,0:T(8,128)(2,1)}, u32[]{:S(2)}, u32[]{:S(2)}) %all-to-all-start.1) | async-done | bytes 2097184 | tf_op jit(solution)/shard_map/all_to_all | solution.py:216
  75.0 0.0 copy-start.6
  75.0 0.0 copy-start.7
  75.0 1.8 copy.19
  76.9 41.6 %all-gather.2.cloned.1.call-done.token_ref = bf16[2048,2048]{1,0:T(8,128)(2,1)} async-done(((bf16[128,2048]{1,0:T(8,128)(2,1)}), bf16[2048,2048]{1,0:T(8,128)(2,1)}) %all-gather.2.cloned.1.call-update) | async-done | bytes 8388624 | tf_op jit(solution)/shard_map/all_gather | solution.py:213
  118.5 0.0 copy-done.6
  118.5 0.0 copy-done.7
  118.5 16.7 %shard_map.91 = (bf16[2048,128]{1,0:T(8,128)(2,1)S(1)}, f32[2048,128]{1,0:T(8,128)S(1)}, bf16[272,128]{1,0:T(8,128)(2,1)S(1)}) custom-call(s32[1]{0:T(128)} %bitcast.2.head_ref, f32[16]{0:T(128)S(1)} %copy-done.6, f32[16]{0:T(128)S(1)} %copy-done.7, bf16[2048,2048]{1,0:T(8,128)(2,1)} %all-gather.2.cloned.1.call-done.token_ref, bf16[2048,512]{1,0:T(8,128)(2,1)S(1)} %bitcast.33), custom_call_target="tpu_custom_call" | custom-call | tf_op jit(solution)/shard_map/pallas_call | solution.py:221
  135.3 0.0 copy-start.1
  135.3 1.0 copy-done.1
  136.3 0.0 copy-start.5
  136.3 0.0 copy-start.2
  136.3 2.1 collective-permute-start
  138.4 1.2 collective-permute-done.other_ref
  139.5 0.0 copy-start.3
  139.5 0.0 copy-done.5
  139.5 0.6 copy-done.3
  140.2 2.1 shard_map.92
  142.3 0.0 copy-start.4
  142.3 7.1 %all-to-all-start.2 = ((bf16[16,272,128]{2,1,0:T(8,128)(2,1)}), bf16[16,272,128]{2,1,0:T(8,128)(2,1)S(1)}, u32[]{:S(2)}, u32[]{:S(2)}) async-start(bf16[16,272,128]{2,1,0:T(8,128)(2,1)} %shard_map.92), calls=%async_computation.2 | async-start | bytes 2228224 | tf_op jit(solution)/shard_map/all_to_all | solution.py:256
  149.5 0.1 pad_add_fusion.place_ref
  149.5 18.6 %all-to-all-done.2.map_ref = bf16[16,272,128]{2,1,0:T(8,128)(2,1)S(1)} async-done(((bf16[16,272,128]{2,1,0:T(8,128)(2,1)}), bf16[16,272,128]{2,1,0:T(8,128)(2,1)S(1)}, u32[]{:S(2)}, u32[]{:S(2)}) %all-to-all-start.2) | async-done | bytes 1114144 | tf_op jit(solution)/shard_map/all_to_all | solution.py:256
  168.1 0.0 copy-done.2
  168.1 0.0 copy-done.4
  168.1 0.0 copy-start.8
  168.1 1.8 shard_map.93
  169.9 10.0 %all-to-all-start.3 = ((bf16[16,128,128]{2,1,0:T(8,128)(2,1)}), bf16[16,128,128]{2,1,0:T(8,128)(2,1)S(1)}, u32[]{:S(2)}, u32[]{:S(2)}) async-start(bf16[16,128,128]{2,1,0:T(8,128)(2,1)} %bitcast.11), calls=%async_computation.3 | async-start | bytes 1048576 | tf_op jit(solution)/shard_map/all_to_all | solution.py:265
  180.0 0.0 copy-done.8
  180.0 27.1 %all-to-all-done.3 = bf16[16,128,128]{2,1,0:T(8,128)(2,1)S(1)} async-done(((bf16[16,128,128]{2,1,0:T(8,128)(2,1)}), bf16[16,128,128]{2,1,0:T(8,128)(2,1)S(1)}, u32[]{:S(2)}, u32[]{:S(2)}) %all-to-all-start.3) | async-done | bytes 524320 | tf_op jit(solution)/shard_map/all_to_all | solution.py:265
  207.1 0.3 fusion.2
  207.5 1.1 fusion.3
  (4 shorter events, 0.0 us)
Async XLA Ops:
  6.5 2.0 copy-start
  6.5 112.0 %all-gather.2.cloned.1.call-start = ((), (), s32[]{:S(2)}) async-start(), calls=%async_computation.4 | async-start | bytes 8912896 | tf_op jit(solution)/shard_map/all_gather | solution.py:213
  40.2 34.8 %all-to-all-start.1 = ((bf16[16,16,8,512]{3,2,1,0:T(8,128)(2,1)}), bf16[16,16,8,512]{3,2,1,0:T(8,128)(2,1)}, u32[]{:S(2)}, u32[]{:S(2)}) async-start(bf16[16,16,8,512]{3,2,1,0:T(8,128)(2,1)} %broadcast_in_dim.5), calls=%async_computation.1 | async-start | bytes 4194304 | tf_op jit(solution)/shard_map/all_to_all | solution.py:216
  75.0 43.5 %copy-start.6 = (f32[16]{0:T(128)S(1)}, f32[16]{0:T(128)}, u32[]{:S(2)}) copy-start(f32[16]{0:T(128)} %rate_ref.1) | copy-start | bytes 196
  75.0 43.5 %copy-start.7 = (f32[16]{0:T(128)S(1)}, f32[16]{0:T(128)}, u32[]{:S(2)}) copy-start(f32[16]{0:T(128)} %bias_ref.1) | copy-start | bytes 196
  135.3 1.0 copy-start.1
  136.3 3.3 %copy-start.5 = (bf16[272,128]{1,0:T(8,128)(2,1)}, bf16[272,128]{1,0:T(8,128)(2,1)S(1)}, u32[]{:S(2)}) copy-start(bf16[272,128]{1,0:T(8,128)(2,1)S(1)} %get-tuple-element.8.mine_ref) | copy-start | bytes 208900
  136.3 31.9 %copy-start.2 = (f32[2048,128]{1,0:T(8,128)S(1)}, f32[2048,128]{1,0:T(8,128)}, u32[]{:S(2)}) copy-start(f32[2048,128]{1,0:T(8,128)} %copy-done.1) | copy-start | bytes 3145732
  136.3 3.3 %collective-permute-start = (bf16[272,128]{1,0:T(8,128)(2,1)S(1)}, bf16[272,128]{1,0:T(8,128)(2,1)S(1)}, u32[]{:S(2)}, u32[]{:S(2)}) collective-permute-start(bf16[272,128]{1,0:T(8,128)(2,1)S(1)} %get-tuple-element.8.mine_ref), channel_id=1, source_target_pairs={{0,16},{16,0},{1,17},{17,1},{2,18},{18,2},{3,19},{19,3},{4,20},{20... | collective-permute-start | bytes 208904 | tf_op jit(solution)/shard_map/ppermute | solution.py:249
  139.5 0.6 copy-start.3
  142.3 25.8 %copy-start.4 = (bf16[272,128]{1,0:T(8,128)(2,1)S(1)}, bf16[272,128]{1,0:T(8,128)(2,1)}, u32[]{:S(2)}) copy-start(bf16[272,128]{1,0:T(8,128)(2,1)} %copy-done.3) | copy-start | bytes 208900
  142.3 25.8 %all-to-all-start.2 = ((bf16[16,272,128]{2,1,0:T(8,128)(2,1)}), bf16[16,272,128]{2,1,0:T(8,128)(2,1)S(1)}, u32[]{:S(2)}, u32[]{:S(2)}) async-start(bf16[16,272,128]{2,1,0:T(8,128)(2,1)} %shard_map.92), calls=%async_computation.2 | async-start | bytes 2228224 | tf_op jit(solution)/shard_map/all_to_all | solution.py:256
  168.1 11.8 %copy-start.8 = (f32[128]{0:T(128)S(1)}, f32[128]{0:T(128)}, u32[]{:S(2)}) copy-start(f32[128]{0:T(128)} %param.17) | copy-start | bytes 1540
  169.9 37.2 %all-to-all-start.3 = ((bf16[16,128,128]{2,1,0:T(8,128)(2,1)}), bf16[16,128,128]{2,1,0:T(8,128)(2,1)S(1)}, u32[]{:S(2)}, u32[]{:S(2)}) async-start(bf16[16,128,128]{2,1,0:T(8,128)(2,1)} %bitcast.11), calls=%async_computation.3 | async-start | bytes 1048576 | tf_op jit(solution)/shard_map/all_to_all | solution.py:265
Sparse Core Ops, SparseCore 0:
  9.4 109.0 all-gather.1

commit v6 on v5

--- a/solution.py
+++ b/solution.py
@@ -10,7 +10,8 @@
 DK = 128
 DV = 128
 CHUNK = 128
-GANG = 8
+GANG = 16
+APART = 8
 WIDE = 512
 MAP_ROWS = 272
 TM_STREAM = ("tm_0", "tm_1", "tm_2", "stream")
@@ -29,26 +30,33 @@
     rate_ref,
     bias_ref,
     token_ref,
+    apart_ref,
     weight_ref,
     reach_ref,
     own_ref,
     total_ref,
     raw_ref,
-    state_ref,
+    raw_apart_ref,
 ):
+    step, steps = pl.program_id(0), pl.num_programs(0)
     rate, bias = rate_ref[head_ref[0]], bias_ref[head_ref[0]]
-    raw_ref[...] = jnp.dot(token_ref[...], weight_ref[...], preferred_element_type=f32)
+    for part_ref, part_raw_ref in ((token_ref, raw_ref), (apart_ref, raw_apart_ref)):
+        size = part_ref.shape[0]
+        part_raw_ref[pl.ds(pl.multiple_of(step * size, 8), size), :] = jnp.dot(
+            part_ref[...], weight_ref[...], preferred_element_type=f32
+        )
+
+    @pl.when(step == steps - 1)
+    def _():
+        delta_rule(rate, bias, raw_ref, raw_apart_ref, reach_ref, own_ref, total_ref)
+
+
+def delta_rule(rate, bias, raw_ref, raw_apart_ref, reach_ref, own_ref, total_ref):
     row = lax.broadcasted_iota(jnp.int32, (CHUNK, CHUNK), 0)
     col = lax.broadcasted_iota(jnp.int32, (CHUNK, CHUNK), 1)
     strict, inclusive = row > col, row >= col
     eye = jnp.where(row == col, 1.0, 0.0).astype(f32)
     ones_below = jnp.where(inclusive, 1.0, 0.0).astype(bf16)
-
-    @pl.when(pl.program_id(0) == 0)
-    def _():
-        state_ref[0:DK, :] = eye
-        state_ref[DK : DK + DV, :] = jnp.zeros((DV, DK), f32)
-        state_ref[DK + DV :, :] = jnp.ones((8, DK), f32)
 
     def below(size):
         return (
@@ -57,15 +65,25 @@
             & ((col // size) % 2 == 0)
         )
 
-    def gang(step, carry):
-        starts = [pl.multiple_of((step * GANG + i) * CHUNK, CHUNK) for i in range(GANG)]
+    state = jnp.concatenate([eye, jnp.zeros((DV, DK), f32)], 0)
+    kept = jnp.ones((8, DK), f32)
+    most = CHUNK - APART
+    for first in range(0, raw_ref.shape[0] // most, GANG):
+        starts = [(first + i) * CHUNK for i in range(GANG)]
         each = range(GANG)
         q, k, v, beta, grow, scale_row, beta_row, tail, last, decay = ([] for _ in range(10))
         for i in each:
-            raw_q = raw_ref[pl.ds(starts[i], CHUNK), 0:128]
-            raw_k = raw_ref[pl.ds(starts[i], CHUNK), 128:256]
-            raw_v = raw_ref[pl.ds(starts[i], CHUNK), 256:384]
-            logits = raw_ref[pl.ds(starts[i], CHUNK), 384:512]
+            raw = jnp.concatenate(
+                [
+                    raw_ref[pl.ds((first + i) * most, most), :],
+                    raw_apart_ref[pl.ds((first + i) * APART, APART), :],
+                ],
+                0,
+            )
+            raw_q = raw[:, 0:128]
+            raw_k = raw[:, 128:256]
+            raw_v = raw[:, 256:384]
+            logits = raw[:, 384:512]
             q.append(
                 (
                     raw_q
@@ -103,11 +121,7 @@
             inverse = [inverse[i] - mm(inverse[i], inner[i]) for i in each]
         rounded = [inverse[i].astype(bf16) for i in each]
         high = [lower[i].astype(bf16) for i in each]
-        low = [(lower[i] - high[i].astype(f32)).astype(bf16) for i in each]
-        rest = [
-            eye - rounded[i].astype(f32) - mm(high[i], rounded[i]) - mm(low[i], rounded[i])
-            for i in each
-        ]
+        rest = [eye - rounded[i].astype(f32) - mm(high[i], rounded[i]) for i in each]
         inverse = [rounded[i].astype(f32) + mm(rounded[i], rest[i]) for i in each]
         w = [mm(inverse[i] * scale_row[i], k[i]) for i in each]
         u = [mm(inverse[i] * beta_row[i], v[i]) for i in each]
@@ -116,7 +130,6 @@
         change = [mm(wu[i] * tail2[i], k[i], 0, 0) for i in each]
         inside = [mm(scores[i], wu[i]) for i in each]
         reach = [grow[i] * q[i].astype(f32) - inside[i][:, :DK] for i in each]
-        state, kept = state_ref[0 : DK + DV, :], state_ref[DK + DV :, :]
         for i in each:
             out = mm(reach[i], state, 1, 1)
             reach_ref[pl.ds(starts[i], CHUNK), :] = out[:, :DK].astype(bf16)
@@ -125,19 +138,10 @@
             state = last[i] * state - moved
             state = jnp.concatenate([state[:DK], state[DK:] + change[i][DK:]], 0)
             kept = last[i] * kept
-        state_ref[0 : DK + DV, :] = state
-        state_ref[DK + DV :, :] = kept
-        return carry
-
-    lax.fori_loop(0, raw_ref.shape[0] // (CHUNK * GANG), gang, 0)
-
-    @pl.when(pl.program_id(0) == pl.num_programs(0) - 1)
-    def _():
-        kept = state_ref[DK + DV :, :]
-        part = kept.astype(bf16).astype(f32)
-        total_ref[0:DK, :] = (state_ref[0:DK, :] - kept[0:1] * eye).astype(bf16)
-        total_ref[DK : DK + DV, :] = state_ref[DK : DK + DV, :].astype(bf16)
-        total_ref[DK + DV :, :] = jnp.concatenate([part, kept - part], 0).astype(bf16)
+    part = kept.astype(bf16).astype(f32)
+    total_ref[0:DK, :] = (state[:DK] - kept[0:1] * eye).astype(bf16)
+    total_ref[DK : DK + DV, :] = state[DK:].astype(bf16)
+    total_ref[DK + DV :, :] = jnp.concatenate([part, kept - part], 0).astype(bf16)
 
 
 def opened(map_ref, *at):
@@ -210,14 +214,17 @@
         ],
         -1,
     ).transpose(1, 0, 2)
-    all_tokens = lax.all_gather(tokens, "stream", axis=0, tiled=True)
+    most = local_rows - APART
+    all_tokens = lax.all_gather(tokens[:most], "stream", axis=0, tiled=True)
+    apart = lax.all_gather(tokens[most:], "stream", axis=0, tiled=True)
     weights = lax.all_to_all(weights, "stream", split_axis=0, concat_axis=0, tiled=True)
     weights = jnp.broadcast_to(weights[None], (shares,) + weights.shape)
     weights = lax.all_to_all(weights, ("tm_0", "tm_1"), split_axis=0, concat_axis=0, tiled=True)
     weights = weights.transpose(1, 0, 2, 3).reshape(streams * shares * rows, WIDE)
 
-    block_rows, features = all_tokens.shape
-    stretch = CHUNK * GANG
+    features = all_tokens.shape[1]
+    block_rows = streams * local_rows
+    steps = 2
     reach, own, total = pl.pallas_call(
         chunk_kernel,
         out_shape=(
@@ -225,25 +232,26 @@
             jax.ShapeDtypeStruct((block_rows, DV), f32),
             jax.ShapeDtypeStruct((MAP_ROWS, DK), bf16),
         ),
-        grid=(block_rows // stretch,),
+        grid=(steps,),
         in_specs=[
             smem,
             smem,
             smem,
-            pl.BlockSpec((stretch, features), lambda i: (i, 0)),
+            pl.BlockSpec((streams * most // steps, features), lambda i: (i, 0)),
+            pl.BlockSpec((streams * APART // steps, features), lambda i: (i, 0)),
             pl.BlockSpec((features, WIDE), lambda i: (0, 0)),
         ],
         out_specs=(
-            pl.BlockSpec((stretch, DK), lambda i: (i, 0)),
-            pl.BlockSpec((stretch, DV), lambda i: (i, 0)),
+            pl.BlockSpec((block_rows, DK), lambda i: (0, 0)),
+            pl.BlockSpec((block_rows, DV), lambda i: (0, 0)),
             pl.BlockSpec((MAP_ROWS, DK), lambda i: (0, 0)),
         ),
         scratch_shapes=[
-            pltpu.VMEM((stretch, WIDE), f32),
-            pltpu.VMEM((DK + DV + 8, DK), f32),
+            pltpu.VMEM((streams * most, WIDE), f32),
+            pltpu.VMEM((streams * APART, WIDE), f32),
         ],
         compiler_params=pltpu.CompilerParams(vmem_limit_bytes=48 * 2**20),
-    )(head.reshape(1).astype(jnp.int32), decay_rate, beta_bias, all_tokens, weights)
+    )(head.reshape(1).astype(jnp.int32), decay_rate, beta_bias, all_tokens, apart, weights)
 
     core = at_c.reshape(1).astype(jnp.int32)
     other = lax.ppermute(total, "tm_2", [(0, 1), (1, 0)])

time: 216 us -> 215 us (level)
  waiting for transfers between devices: 117 us -> 80.4 us
  blocking collectives: 29.2 us -> 64.2 us
  Pallas kernels: 20.7 us -> 17.8 us
  local copies, waits for them, and re-layouts: 7.16 us -> 9.8 us
    all_gather x0 -> x1, blocking collectives: none -> 35 us  [shards(): apart = lax.all_gather(tokens[most:], 'stream', axis=0, tiled=True)]
    all_to_all x1, waiting for transfers between devices: 27.7 us -> 0.01 us  [shards(): lax.all_to_all(weights, ('tm_0', 'tm_1'), split_axis=0, concat_axis=0, ti...]
    all_gather x1, waiting for transfers between devices: 41.6 us -> 33.5 us  [shards(): all_tokens = lax.all_gather(tokens[:most], 'stream', axis=0, tiled=True)]
    pallas_call x1, Pallas kernels: 16.7 us -> 13.9 us  [shards(): pl.pallas_call(chunk_kernel, out_shape=(jax.ShapeDtypeStruct((block_rows,...]
  transfers between devices with their start and end apart: 5 -> 5, of which waited for: 5 -> 4; matrix products, arithmetic and copies ran while one was open for 3% -> 3% of each run, Pallas kernels for 0% -> 0%
where the time goes in v6:
time: 215 us
  waiting for transfers between devices  80.4 us (37%)
  blocking collectives  64.2 us (30%)
  starting transfers between devices  27.3 us (13%)
  Pallas kernels  17.8 us (8%)
  between operations  13.5 us (6%)
  local copies, waits for them, and re-layouts  9.8 us (5%)
    all_gather x1, blocking collectives, shards(): apart = lax.all_gather(tokens[most:], 'stream', axis=0, tiled=True)  35 us
    all_gather x1, waiting for transfers between devices, shards(): all_tokens = lax.all_gather(tokens[:most], 'stream', axis=0, tiled=True)  33.5 us
    all_to_all x1, blocking collectives, shards(): lax.all_to_all(weights, 'stream', split_axis=0, concat_axis=0, tiled=True)  29.2 us
    all_to_all x1, waiting for transfers between devices, shards(): lax.all_to_all(readout, 'stream', split_axis=0, concat_axis=1, tiled=True)  27.1 us
    all_to_all x1, waiting for transfers between devices, shards(): lax.all_to_all(maps, ('tm_0', 'tm_1'), split_axis=0, concat_axis=0, tiled...  18.6 us
    pallas_call x1, Pallas kernels, shards(): pl.pallas_call(chunk_kernel, out_shape=(jax.ShapeDtypeStruct((block_rows,...  13.9 us
    all_to_all x1, starting transfers between devices, shards(): lax.all_to_all(readout, 'stream', split_axis=0, concat_axis=1, tiled=True)  10.7 us
    all_to_all x1, starting transfers between devices, shards(): lax.all_to_all(weights, ('tm_0', 'tm_1'), split_axis=0, concat_axis=0, ti...  7.28 us
  transfers between devices with their start and end apart: 5, of which 4 were waited for; matrix products, arithmetic and copies ran while one was open for 3% of the time, Pallas kernels for 0%

profile of v6, /device:TPU:32, one launch (start us, length us, event | category | flops | bytes accessed | tf_op | source)
XLA Modules:
  0.0 214.7 jit_solution(13020712614280468732)
XLA Ops:
  6.5 0.0 copy-start
  6.5 0.0 all-gather.2.cloned.1.call-start
  6.5 1.9 slice.6
  8.4 0.0 all-gather.2.cloned.1.call-update
  8.5 0.8 constant_dynamic-slice_fusion
  9.3 0.1 copy.21
  9.4 0.1 copy.17
  9.5 0.1 copy.22
  9.6 0.1 copy.18
  9.7 0.0 copy-done
  9.8 0.8 dynamic-slice_bitcast_fusion
  10.6 0.1 concatenate.3
  10.7 29.2 %all_to_all.28 = bf16[16,8,512]{2,1,0:T(8,128)(2,1)S(1)} all-to-all(bf16[16,8,512]{2,1,0:T(8,128)(2,1)S(1)} %bitcast.34), channel_id=1, replica_groups=mesh['tm_0'=4,'tm_1'=4,'tm_2'=2,'stream'=16] {'stream'}, dimensions={0} | all-to-all | bytes 262144 | tf_op jit(solution)/shard_map/all_to_all | solution.py:220
  39.9 1.5 broadcast_in_dim.5
  41.4 0.0 slice-start
  41.4 7.3 %all-to-all-start.1 = ((bf16[16,16,8,512]{3,2,1,0:T(8,128)(2,1)}), bf16[16,16,8,512]{3,2,1,0:T(8,128)(2,1)}, u32[]{:S(2)}, u32[]{:S(2)}) async-start(bf16[16,16,8,512]{3,2,1,0:T(8,128)(2,1)} %broadcast_in_dim.5), calls=%async_computation.1 | async-start | bytes 4194304 | tf_op jit(solution)/shard_map/all_to_all | solution.py:222
  48.7 0.0 slice-done
  48.7 35.0 %all_gather.7.apart_ref = bf16[128,2048]{1,0:T(8,128)(2,1)S(1)} all-gather(bf16[8,2048]{1,0:T(8,128)(2,1)S(1)} %slice-done), channel_id=1, replica_groups=mesh['tm_0'=4,'tm_1'=4,'tm_2'=2,'stream'=16] {'stream'}, dimensions={0}, use_global_device_ids=true | all-gather | bytes 557056 | tf_op jit(solution)/shard_map/all_gather | solution.py:219
  83.7 0.0 all-to-all-done.1
  83.7 0.0 copy-start.8
  83.7 0.0 copy-start.9
  83.7 1.8 copy.19
  85.6 33.5 %all-gather.2.cloned.1.call-done.token_ref = bf16[1920,2048]{1,0:T(8,128)(2,1)} async-done(((bf16[120,2048]{1,0:T(8,128)(2,1)}), bf16[1920,2048]{1,0:T(8,128)(2,1)}) %all-gather.2.cloned.1.call-update) | async-done | bytes 7864336 | tf_op jit(solution)/shard_map/all_gather | solution.py:218
  119.1 0.0 copy-done.8
  119.1 0.0 copy-done.9
  119.1 13.9 %shard_map.91 = (bf16[2048,128]{1,0:T(8,128)(2,1)S(1)}, f32[2048,128]{1,0:T(8,128)S(1)}, bf16[272,128]{1,0:T(8,128)(2,1)S(1)}) custom-call(s32[1]{0:T(128)} %bitcast.2.head_ref, f32[16]{0:T(128)S(1)} %copy-done.8, f32[16]{0:T(128)S(1)} %copy-done.9, bf16[1920,2048]{1,0:T(8,128)(2,1)} %all-gather.2.cloned.1.call-done.token_ref, ...), custom_call_target="tpu_custom_call" | custom-call | tf_op jit(solution)/shard_map/pallas_call | solution.py:228
  133.0 0.0 copy-start.1
  133.0 0.9 copy-done.1
  133.9 0.0 copy-start.3
  133.9 0.8 copy-done.3
  134.7 2.1 collective-permute-start
  136.8 1.2 collective-permute-done.other_ref
  138.0 0.0 copy-done.7
  138.0 0.6 copy-done.5
  138.6 2.2 %shard_map.92 = bf16[16,272,128]{2,1,0:T(8,128)(2,1)} custom-call(s32[1]{0:T(128)} %bitcast.1.core_ref, bf16[272,128]{1,0:T(8,128)(2,1)} %copy-done.7, bf16[272,128]{1,0:T(8,128)(2,1)} %copy-done.5), custom_call_target="tpu_custom_call" | custom-call | tf_op jit(solution)/shard_map/pallas_call | solution.py:258
  140.8 7.2 %all-to-all-start.2 = ((bf16[16,272,128]{2,1,0:T(8,128)(2,1)}), bf16[16,272,128]{2,1,0:T(8,128)(2,1)S(1)}, u32[]{:S(2)}, u32[]{:S(2)}) async-start(bf16[16,272,128]{2,1,0:T(8,128)(2,1)} %shard_map.92), calls=%async_computation.2 | async-start | bytes 2228224 | tf_op jit(solution)/shard_map/all_to_all | solution.py:264
  148.0 0.1 pad_add_fusion.place_ref
  148.0 18.6 %all-to-all-done.2.map_ref = bf16[16,272,128]{2,1,0:T(8,128)(2,1)S(1)} async-done(((bf16[16,272,128]{2,1,0:T(8,128)(2,1)}), bf16[16,272,128]{2,1,0:T(8,128)(2,1)S(1)}, u32[]{:S(2)}, u32[]{:S(2)}) %all-to-all-start.2) | async-done | bytes 1114144 | tf_op jit(solution)/shard_map/all_to_all | solution.py:264
  166.6 0.0 copy-done.2
  166.6 0.0 copy-done.4
  166.6 0.0 copy-done.6
  166.6 0.0 copy-start.10
  166.7 1.8 shard_map.93
  168.4 10.7 %all-to-all-start.3 = ((bf16[16,128,128]{2,1,0:T(8,128)(2,1)}), bf16[16,128,128]{2,1,0:T(8,128)(2,1)S(1)}, u32[]{:S(2)}, u32[]{:S(2)}) async-start(bf16[16,128,128]{2,1,0:T(8,128)(2,1)} %bitcast.11), calls=%async_computation.3 | async-start | bytes 1048576 | tf_op jit(solution)/shard_map/all_to_all | solution.py:273
  179.2 0.0 copy-done.10
  179.2 27.1 %all-to-all-done.3 = bf16[16,128,128]{2,1,0:T(8,128)(2,1)S(1)} async-done(((bf16[16,128,128]{2,1,0:T(8,128)(2,1)}), bf16[16,128,128]{2,1,0:T(8,128)(2,1)S(1)}, u32[]{:S(2)}, u32[]{:S(2)}) %all-to-all-start.3) | async-done | bytes 524320 | tf_op jit(solution)/shard_map/all_to_all | solution.py:273
  206.3 0.3 fusion.2
  206.7 1.1 fusion.3
  (9 shorter events, 0.0 us)
Async XLA Ops:
  6.5 3.2 %copy-start = (bf16[128,2048]{1,0:T(8,128)(2,1)S(1)}, bf16[128,2048]{1,0:T(8,128)(2,1)}, u32[]{:S(2)}) copy-start(bf16[128,2048]{1,0:T(8,128)(2,1)} %param.10) | copy-start | bytes 1572868
  6.5 112.5 %all-gather.2.cloned.1.call-start = ((), (), s32[]{:S(2)}) async-start(), calls=%async_computation.4 | async-start | bytes 8355840 | tf_op jit(solution)/shard_map/all_gather | solution.py:218
  41.4 7.3 %slice-start = ((bf16[128,2048]{1,0:T(8,128)(2,1)}), bf16[8,2048]{1,0:T(8,128)(2,1)S(1)}, s32[]{:S(2)}) async-start(bf16[128,2048]{1,0:T(8,128)(2,1)} %param.9), calls=%async_computation.5 | async-start | bytes 65536 | tf_op jit(solution)/shard_map/slice | solution.py:219
  41.4 42.3 %all-to-all-start.1 = ((bf16[16,16,8,512]{3,2,1,0:T(8,128)(2,1)}), bf16[16,16,8,512]{3,2,1,0:T(8,128)(2,1)}, u32[]{:S(2)}, u32[]{:S(2)}) async-start(bf16[16,16,8,512]{3,2,1,0:T(8,128)(2,1)} %broadcast_in_dim.5), calls=%async_computation.1 | async-start | bytes 4194304 | tf_op jit(solution)/shard_map/all_to_all | solution.py:222
  83.7 35.3 %copy-start.8 = (f32[16]{0:T(128)S(1)}, f32[16]{0:T(128)}, u32[]{:S(2)}) copy-start(f32[16]{0:T(128)} %rate_ref.1) | copy-start | bytes 196
  83.7 35.3 %copy-start.9 = (f32[16]{0:T(128)S(1)}, f32[16]{0:T(128)}, u32[]{:S(2)}) copy-start(f32[16]{0:T(128)} %bias_ref.1) | copy-start | bytes 196
  133.0 0.9 copy-start.1
  133.9 0.8 copy-start.3
  134.7 3.3 %copy-start.7 = (bf16[272,128]{1,0:T(8,128)(2,1)}, bf16[272,128]{1,0:T(8,128)(2,1)S(1)}, u32[]{:S(2)}) copy-start(bf16[272,128]{1,0:T(8,128)(2,1)S(1)} %get-tuple-element.8.mine_ref) | copy-start | bytes 208900
  134.7 31.9 %copy-start.2 = (f32[2048,128]{1,0:T(8,128)S(1)}, f32[2048,128]{1,0:T(8,128)}, u32[]{:S(2)}) copy-start(f32[2048,128]{1,0:T(8,128)} %copy-done.1) | copy-start | bytes 3145732
  134.7 31.9 %copy-start.4 = (bf16[2048,128]{1,0:T(8,128)(2,1)S(1)}, bf16[2048,128]{1,0:T(8,128)(2,1)}, u32[]{:S(2)}) copy-start(bf16[2048,128]{1,0:T(8,128)(2,1)} %copy-done.3) | copy-start | bytes 1572868
  134.7 3.3 %collective-permute-start = (bf16[272,128]{1,0:T(8,128)(2,1)S(1)}, bf16[272,128]{1,0:T(8,128)(2,1)S(1)}, u32[]{:S(2)}, u32[]{:S(2)}) collective-permute-start(bf16[272,128]{1,0:T(8,128)(2,1)S(1)} %get-tuple-element.8.mine_ref), channel_id=1, source_target_pairs={{0,16},{16,0},{1,17},{17,1},{2,18},{18,2},{3,19},{19,3},{4,20},{20... | collective-permute-start | bytes 208904 | tf_op jit(solution)/shard_map/ppermute | solution.py:257
  138.0 0.6 copy-start.5
  140.8 25.9 %copy-start.6 = (bf16[272,128]{1,0:T(8,128)(2,1)S(1)}, bf16[272,128]{1,0:T(8,128)(2,1)}, u32[]{:S(2)}) copy-start(bf16[272,128]{1,0:T(8,128)(2,1)} %copy-done.5) | copy-start | bytes 208900
  140.8 25.9 %all-to-all-start.2 = ((bf16[16,272,128]{2,1,0:T(8,128)(2,1)}), bf16[16,272,128]{2,1,0:T(8,128)(2,1)S(1)}, u32[]{:S(2)}, u32[]{:S(2)}) async-start(bf16[16,272,128]{2,1,0:T(8,128)(2,1)} %shard_map.92), calls=%async_computation.2 | async-start | bytes 2228224 | tf_op jit(solution)/shard_map/all_to_all | solution.py:264
  166.6 12.5 %copy-start.10 = (f32[128]{0:T(128)S(1)}, f32[128]{0:T(128)}, u32[]{:S(2)}) copy-start(f32[128]{0:T(128)} %param.17) | copy-start | bytes 1540
  168.4 37.9 %all-to-all-start.3 = ((bf16[16,128,128]{2,1,0:T(8,128)(2,1)}), bf16[16,128,128]{2,1,0:T(8,128)(2,1)S(1)}, u32[]{:S(2)}, u32[]{:S(2)}) async-start(bf16[16,128,128]{2,1,0:T(8,128)(2,1)} %bitcast.11), calls=%async_computation.3 | async-start | bytes 1048576 | tf_op jit(solution)/shard_map/all_to_all | solution.py:273
Sparse Core Ops, SparseCore 0:
  9.4 109.5 all-gather.1

commit v7 on v6

--- a/solution.py
+++ b/solution.py
@@ -11,7 +11,6 @@
 DV = 128
 CHUNK = 128
 GANG = 16
-APART = 8
 WIDE = 512
 MAP_ROWS = 272
 TM_STREAM = ("tm_0", "tm_1", "tm_2", "stream")
@@ -30,28 +29,30 @@
     rate_ref,
     bias_ref,
     token_ref,
-    apart_ref,
-    weight_ref,
+    mine_ref,
+    other_ref,
     reach_ref,
     own_ref,
     total_ref,
     raw_ref,
-    raw_apart_ref,
 ):
     step, steps = pl.program_id(0), pl.num_programs(0)
     rate, bias = rate_ref[head_ref[0]], bias_ref[head_ref[0]]
-    for part_ref, part_raw_ref in ((token_ref, raw_ref), (apart_ref, raw_apart_ref)):
-        size = part_ref.shape[0]
-        part_raw_ref[pl.ds(pl.multiple_of(step * size, 8), size), :] = jnp.dot(
-            part_ref[...], weight_ref[...], preferred_element_type=f32
+    size = token_ref.shape[0]
+    rows = pl.ds(pl.multiple_of(step * size, size), size)
+    half = mine_ref.shape[1]
+    for c in range(2):
+        weights = jnp.where(head_ref[1] == c, mine_ref[...], other_ref[...])
+        raw_ref[rows, c * half : (c + 1) * half] = jnp.dot(
+            token_ref[...], weights, preferred_element_type=f32
         )
 
     @pl.when(step == steps - 1)
     def _():
-        delta_rule(rate, bias, raw_ref, raw_apart_ref, reach_ref, own_ref, total_ref)
-
-
-def delta_rule(rate, bias, raw_ref, raw_apart_ref, reach_ref, own_ref, total_ref):
+        delta_rule(rate, bias, raw_ref, reach_ref, own_ref, total_ref)
+
+
+def delta_rule(rate, bias, raw_ref, reach_ref, own_ref, total_ref):
     row = lax.broadcasted_iota(jnp.int32, (CHUNK, CHUNK), 0)
     col = lax.broadcasted_iota(jnp.int32, (CHUNK, CHUNK), 1)
     strict, inclusive = row > col, row >= col
@@ -67,19 +68,12 @@
 
     state = jnp.concatenate([eye, jnp.zeros((DV, DK), f32)], 0)
     kept = jnp.ones((8, DK), f32)
-    most = CHUNK - APART
-    for first in range(0, raw_ref.shape[0] // most, GANG):
+    for first in range(0, raw_ref.shape[0] // CHUNK, GANG):
         starts = [(first + i) * CHUNK for i in range(GANG)]
         each = range(GANG)
         q, k, v, beta, grow, scale_row, beta_row, tail, last, decay = ([] for _ in range(10))
         for i in each:
-            raw = jnp.concatenate(
-                [
-                    raw_ref[pl.ds((first + i) * most, most), :],
-                    raw_apart_ref[pl.ds((first + i) * APART, APART), :],
-                ],
-                0,
-            )
+            raw = raw_ref[pl.ds(starts[i], CHUNK), :]
             raw_q = raw[:, 0:128]
             raw_k = raw[:, 128:256]
             raw_v = raw[:, 256:384]
@@ -203,27 +197,20 @@
     def share(w, width):
         return lax.dynamic_slice_in_dim(w, first, rows, 0).reshape(rows, HEADS, width)
 
-    weights = jnp.concatenate(
-        [
-            share(w_query, DK),
-            share(w_key, DK),
-            share(w_value, DV),
-            share(decay_proj, 1),
-            share(beta_proj, 1),
-            jnp.zeros((rows, HEADS, WIDE - 386), bf16),
-        ],
-        -1,
-    ).transpose(1, 0, 2)
-    most = local_rows - APART
-    all_tokens = lax.all_gather(tokens[:most], "stream", axis=0, tiled=True)
-    apart = lax.all_gather(tokens[most:], "stream", axis=0, tiled=True)
+    pads = jnp.zeros((rows, HEADS, WIDE - 386), bf16)
+    left = jnp.concatenate([share(w_query, DK), share(w_key, DK)], -1)
+    right = jnp.concatenate(
+        [share(w_value, DV), share(decay_proj, 1), share(beta_proj, 1), pads], -1
+    )
+    weights = jnp.where(at_c == 0, left, right).transpose(1, 0, 2)
+    all_tokens = lax.all_gather(tokens, "stream", axis=0, tiled=True)
     weights = lax.all_to_all(weights, "stream", split_axis=0, concat_axis=0, tiled=True)
     weights = jnp.broadcast_to(weights[None], (shares,) + weights.shape)
     weights = lax.all_to_all(weights, ("tm_0", "tm_1"), split_axis=0, concat_axis=0, tiled=True)
-    weights = weights.transpose(1, 0, 2, 3).reshape(streams * shares * rows, WIDE)
-
-    features = all_tokens.shape[1]
-    block_rows = streams * local_rows
+    weights = weights.transpose(1, 0, 2, 3).reshape(streams * shares * rows, WIDE // 2)
+    swapped = lax.ppermute(weights, "tm_2", [(0, 1), (1, 0)])
+
+    block_rows, features = all_tokens.shape
     steps = 2
     reach, own, total = pl.pallas_call(
         chunk_kernel,
@@ -237,9 +224,9 @@
             smem,
             smem,
             smem,
-            pl.BlockSpec((streams * most // steps, features), lambda i: (i, 0)),
-            pl.BlockSpec((streams * APART // steps, features), lambda i: (i, 0)),
-            pl.BlockSpec((features, WIDE), lambda i: (0, 0)),
+            pl.BlockSpec((block_rows // steps, features), lambda i: (i, 0)),
+            pl.BlockSpec((features, WIDE // 2), lambda i: (0, 0)),
+            pl.BlockSpec((features, WIDE // 2), lambda i: (0, 0)),
         ],
         out_specs=(
             pl.BlockSpec((block_rows, DK), lambda i: (0, 0)),
@@ -247,11 +234,17 @@
             pl.BlockSpec((MAP_ROWS, DK), lambda i: (0, 0)),
         ),
         scratch_shapes=[
-            pltpu.VMEM((streams * most, WIDE), f32),
-            pltpu.VMEM((streams * APART, WIDE), f32),
+            pltpu.VMEM((block_rows, WIDE), f32),
         ],
         compiler_params=pltpu.CompilerParams(vmem_limit_bytes=48 * 2**20),
-    )(head.reshape(1).astype(jnp.int32), decay_rate, beta_bias, all_tokens, apart, weights)
+    )(
+        jnp.stack([head, at_c]).astype(jnp.int32),
+        decay_rate,
+        beta_bias,
+        all_tokens,
+        weights,
+        swapped,
+    )
 
     core = at_c.reshape(1).astype(jnp.int32)
     other = lax.ppermute(total, "tm_2", [(0, 1), (1, 0)])

time: 215 us -> 213 us (level)
  the two profiles are of different devices: /device:TPU:32 before, /device:TPU:64 now
where the time goes in v7:
time: 213 us
  waiting for transfers between devices  104 us (49%)
  blocking collectives  48.7 us (23%)
  starting transfers between devices  21.9 us (10%)
  Pallas kernels  17.6 us (8%)
  between operations  13.5 us (6%)
  local copies, waits for them, and re-layouts  5.23 us (2%)
    all_gather x1, waiting for transfers between devices, shards(): all_tokens = lax.all_gather(tokens, 'stream', axis=0, tiled=True)  53.1 us
    all_to_all x1, waiting for transfers between devices, shards(): lax.all_to_all(readout, 'stream', split_axis=0, concat_axis=1, tiled=True)  27.6 us
    all_to_all x1, blocking collectives, shards(): lax.all_to_all(weights, 'stream', split_axis=0, concat_axis=0, tiled=True)  25.6 us
    all_to_all x1, blocking collectives, shards(): lax.all_to_all(weights, ('tm_0', 'tm_1'), split_axis=0, concat_axis=0, ti...  23.1 us
    all_to_all x1, waiting for transfers between devices, shards(): lax.all_to_all(maps, ('tm_0', 'tm_1'), split_axis=0, concat_axis=0, tiled...  18.6 us
    pallas_call x1, Pallas kernels, shards(): pl.pallas_call(chunk_kernel, out_shape=(jax.ShapeDtypeStruct((block_rows,...  13.6 us
    all_to_all x1, starting transfers between devices, shards(): lax.all_to_all(readout, 'stream', split_axis=0, concat_axis=1, tiled=True)  11 us
    all_to_all x1, starting transfers between devices, shards(): lax.all_to_all(maps, ('tm_0', 'tm_1'), split_axis=0, concat_axis=0, tiled...  7.05 us
  transfers between devices with their start and end apart: 5, of which 5 were waited for; matrix products, arithmetic and copies ran while one was open for 1% of the time, Pallas kernels for 0%

profile of v7, /device:TPU:64, one launch (start us, length us, event | category | flops | bytes accessed | tf_op | source)
XLA Modules:
  0.0 212.5 jit_solution(3415589117646526332)
XLA Ops:
  6.5 0.0 copy-start
  6.5 0.0 all-gather.2.cloned.1.call-start
  6.5 0.7 all-gather.2.cloned.1.call-update
  7.3 0.8 constant_dynamic-slice_fusion
  8.1 0.1 copy.21
  8.1 0.1 copy.17
  8.3 0.1 copy.22
  8.4 0.1 copy.18
  8.5 0.1 pad.3.clone
  8.6 0.0 copy-done
  8.6 0.8 dynamic-slice_bitcast_fusion
  9.4 0.1 fusion.4
  9.5 25.6 %all_to_all.28 = bf16[16,8,256]{2,1,0:T(8,128)(2,1)S(1)} all-to-all(bf16[16,8,256]{2,1,0:T(8,128)(2,1)S(1)} %fusion.4), channel_id=1, replica_groups=mesh['tm_0'=4,'tm_1'=4,'tm_2'=2,'stream'=16] {'stream'}, dimensions={0} | all-to-all | bytes 131072 | tf_op jit(solution)/shard_map/all_to_all | solution.py:207
  35.1 0.1 broadcast_in_dim.5
  35.2 23.1 %all_to_all.29 = bf16[16,16,8,256]{3,2,1,0:T(8,128)(2,1)S(1)} all-to-all(bf16[16,16,8,256]{3,2,1,0:T(8,128)(2,1)S(1)} %broadcast_in_dim.5), channel_id=1, replica_groups=mesh['tm_0'=4,'tm_1'=4,'tm_2'=2,'stream'=16] {'tm_0','tm_1'}, dimensions={0} | all-to-all | bytes 2097152 | tf_op jit(solution)/shard_map/all_to_all | solution.py:209
  58.3 0.0 copy-start.6
  58.3 0.0 copy-start.7
  58.3 0.1 copy.19
  58.4 1.9 collective-permute-start
  60.4 0.1 pad_add_fusion.1.head_ref
  60.5 2.5 %collective-permute-done.other_ref = bf16[2048,256]{1,0:T(8,128)(2,1)S(1)} collective-permute-done((bf16[2048,256]{1,0:T(8,128)(2,1)S(1)}, bf16[2048,256]{1,0:T(8,128)(2,1)S(1)}, u32[]{:S(2)}, u32[]{:S(2)}) %collective-permute-start) | collective-permute-done | bytes 1048608 | tf_op jit(solution)/shard_map/ppermute | solution.py:211
  63.0 0.0 copy-start.1
  63.0 1.0 copy-done.1
  64.0 53.1 %all-gather.2.cloned.1.call-done.token_ref = bf16[2048,2048]{1,0:T(8,128)(2,1)} async-done(((bf16[128,2048]{1,0:T(8,128)(2,1)}), bf16[2048,2048]{1,0:T(8,128)(2,1)}) %all-gather.2.cloned.1.call-update) | async-done | bytes 8388624 | tf_op jit(solution)/shard_map/all_gather | solution.py:206
  117.2 0.0 copy-done.6
  117.2 0.0 copy-done.7
  117.2 0.0 copy-start.2
  117.2 1.2 copy-done.2
  118.4 13.6 %shard_map.91 = (bf16[2048,128]{1,0:T(8,128)(2,1)S(1)}, f32[2048,128]{1,0:T(8,128)S(1)}, bf16[272,128]{1,0:T(8,128)(2,1)S(1)}) custom-call(s32[2]{0:T(128)S(1)} %pad_add_fusion.1.head_ref, f32[16]{0:T(128)S(1)} %copy-done.6, f32[16]{0:T(128)S(1)} %copy-done.7, bf16[2048,2048]{1,0:T(8,128)(2,1)} %all-gather.2.cloned.1.call-done.token_ref, ...), custom_call_target="tpu_custom_call" | custom-call | tf_op jit(solution)/shard_map/pallas_call | solution.py:215
  132.0 0.0 copy-start.5
  132.1 1.9 collective-permute-start.1
  134.0 1.2 collective-permute-done.1.other_ref
  135.2 0.0 copy-done.5
  135.2 0.0 copy-start.3
  135.2 0.6 copy-done.3
  135.8 2.1 %shard_map.92 = bf16[16,272,128]{2,1,0:T(8,128)(2,1)} custom-call(s32[1]{0:T(128)} %bitcast.1.core_ref, bf16[272,128]{1,0:T(8,128)(2,1)} %copy-done.5, bf16[272,128]{1,0:T(8,128)(2,1)} %copy-done.3), custom_call_target="tpu_custom_call" | custom-call | tf_op jit(solution)/shard_map/pallas_call | solution.py:251
  138.0 0.0 copy-start.4
  138.0 7.1 %all-to-all-start.2 = ((bf16[16,272,128]{2,1,0:T(8,128)(2,1)}), bf16[16,272,128]{2,1,0:T(8,128)(2,1)S(1)}, u32[]{:S(2)}, u32[]{:S(2)}) async-start(bf16[16,272,128]{2,1,0:T(8,128)(2,1)} %shard_map.92), calls=%async_computation.2 | async-start | bytes 2228224 | tf_op jit(solution)/shard_map/all_to_all | solution.py:257
  145.0 0.1 pad_add_fusion.place_ref
  145.1 18.6 %all-to-all-done.2.map_ref = bf16[16,272,128]{2,1,0:T(8,128)(2,1)S(1)} async-done(((bf16[16,272,128]{2,1,0:T(8,128)(2,1)}), bf16[16,272,128]{2,1,0:T(8,128)(2,1)S(1)}, u32[]{:S(2)}, u32[]{:S(2)}) %all-to-all-start.2) | async-done | bytes 1114144 | tf_op jit(solution)/shard_map/all_to_all | solution.py:257
  163.7 0.0 copy-done.4
  163.7 0.0 copy-start.8
  163.7 1.8 shard_map.93
  165.5 11.0 %all-to-all-start.3 = ((bf16[16,128,128]{2,1,0:T(8,128)(2,1)}), bf16[16,128,128]{2,1,0:T(8,128)(2,1)S(1)}, u32[]{:S(2)}, u32[]{:S(2)}) async-start(bf16[16,128,128]{2,1,0:T(8,128)(2,1)} %bitcast.11), calls=%async_computation.3 | async-start | bytes 1048576 | tf_op jit(solution)/shard_map/all_to_all | solution.py:266
  176.6 0.0 copy-done.8
  176.6 27.6 %all-to-all-done.3 = bf16[16,128,128]{2,1,0:T(8,128)(2,1)S(1)} async-done(((bf16[16,128,128]{2,1,0:T(8,128)(2,1)}), bf16[16,128,128]{2,1,0:T(8,128)(2,1)S(1)}, u32[]{:S(2)}, u32[]{:S(2)}) %all-to-all-start.3) | async-done | bytes 524320 | tf_op jit(solution)/shard_map/all_to_all | solution.py:266
  204.2 0.3 fusion.2
  204.5 1.1 fusion.3
  (4 shorter events, 0.0 us)
Async XLA Ops:
  6.5 2.1 copy-start
  6.5 110.6 %all-gather.2.cloned.1.call-start = ((), (), s32[]{:S(2)}) async-start(), calls=%async_computation.4 | async-start | bytes 8912896 | tf_op jit(solution)/shard_map/all_gather | solution.py:206
  58.3 58.8 %copy-start.6 = (f32[16]{0:T(128)S(1)}, f32[16]{0:T(128)}, u32[]{:S(2)}) copy-start(f32[16]{0:T(128)} %rate_ref.1) | copy-start | bytes 196
  58.3 58.8 %copy-start.7 = (f32[16]{0:T(128)S(1)}, f32[16]{0:T(128)}, u32[]{:S(2)}) copy-start(f32[16]{0:T(128)} %bias_ref.1) | copy-start | bytes 196
  58.4 4.6 %collective-permute-start = (bf16[2048,256]{1,0:T(8,128)(2,1)S(1)}, bf16[2048,256]{1,0:T(8,128)(2,1)S(1)}, u32[]{:S(2)}, u32[]{:S(2)}) collective-permute-start(bf16[2048,256]{1,0:T(8,128)(2,1)S(1)} %bitcast.34), channel_id=1, source_target_pairs={{0,16},{16,0},{1,17},{17,1},{2,18},{18,2},{3,19},{19,3},{4,20},{20... | collective-permute-start | bytes 3145736 | tf_op jit(solution)/shard_map/ppermute | solution.py:211
  63.0 1.0 copy-start.1
  117.2 1.2 copy-start.2
  132.0 3.2 %copy-start.5 = (bf16[272,128]{1,0:T(8,128)(2,1)}, bf16[272,128]{1,0:T(8,128)(2,1)S(1)}, u32[]{:S(2)}) copy-start(bf16[272,128]{1,0:T(8,128)(2,1)S(1)} %get-tuple-element.8.mine_ref) | copy-start | bytes 208900
  132.1 3.2 %collective-permute-start.1 = (bf16[272,128]{1,0:T(8,128)(2,1)S(1)}, bf16[272,128]{1,0:T(8,128)(2,1)S(1)}, u32[]{:S(2)}, u32[]{:S(2)}) collective-permute-start(bf16[272,128]{1,0:T(8,128)(2,1)S(1)} %get-tuple-element.8.mine_ref), channel_id=1, source_target_pairs={{0,16},{16,0},{1,17},{17,1},{2,18},{18,2},{3,19},{19,3},{4,20},{20... | collective-permute-start | bytes 208904 | tf_op jit(solution)/shard_map/ppermute | solution.py:250
  135.2 0.6 copy-start.3
  138.0 25.7 %copy-start.4 = (bf16[272,128]{1,0:T(8,128)(2,1)S(1)}, bf16[272,128]{1,0:T(8,128)(2,1)}, u32[]{:S(2)}) copy-start(bf16[272,128]{1,0:T(8,128)(2,1)} %copy-done.3) | copy-start | bytes 208900
  138.0 25.7 %all-to-all-start.2 = ((bf16[16,272,128]{2,1,0:T(8,128)(2,1)}), bf16[16,272,128]{2,1,0:T(8,128)(2,1)S(1)}, u32[]{:S(2)}, u32[]{:S(2)}) async-start(bf16[16,272,128]{2,1,0:T(8,128)(2,1)} %shard_map.92), calls=%async_computation.2 | async-start | bytes 2228224 | tf_op jit(solution)/shard_map/all_to_all | solution.py:257
  163.7 12.8 %copy-start.8 = (f32[128]{0:T(128)S(1)}, f32[128]{0:T(128)}, u32[]{:S(2)}) copy-start(f32[128]{0:T(128)} %param.17) | copy-start | bytes 1540
  165.5 38.7 %all-to-all-start.3 = ((bf16[16,128,128]{2,1,0:T(8,128)(2,1)}), bf16[16,128,128]{2,1,0:T(8,128)(2,1)S(1)}, u32[]{:S(2)}, u32[]{:S(2)}) async-start(bf16[16,128,128]{2,1,0:T(8,128)(2,1)} %bitcast.11), calls=%async_computation.3 | async-start | bytes 1048576 | tf_op jit(solution)/shard_map/all_to_all | solution.py:266
Sparse Core Ops, SparseCore 0:
  9.4 107.6 all-gather.1

commit v8 on v7

--- a/solution.py
+++ b/solution.py
@@ -31,9 +31,12 @@
     token_ref,
     mine_ref,
     other_ref,
-    reach_ref,
-    own_ref,
     total_ref,
+    query_ref,
+    key_ref,
+    level_ref,
+    solved_ref,
+    state_ref,
     raw_ref,
 ):
     step, steps = pl.program_id(0), pl.num_programs(0)
@@ -49,10 +52,12 @@
 
     @pl.when(step == steps - 1)
     def _():
-        delta_rule(rate, bias, raw_ref, reach_ref, own_ref, total_ref)
-
-
-def delta_rule(rate, bias, raw_ref, reach_ref, own_ref, total_ref):
+        for start in range(0, raw_ref.shape[0], CHUNK):
+            query_ref[start : start + CHUNK, :] = raw_ref[start : start + CHUNK, 0:128]
+        run_map(rate, bias, raw_ref, total_ref, key_ref, level_ref, solved_ref, state_ref)
+
+
+def run_map(rate, bias, raw_ref, total_ref, key_ref, level_ref, solved_ref, state_ref):
     row = lax.broadcasted_iota(jnp.int32, (CHUNK, CHUNK), 0)
     col = lax.broadcasted_iota(jnp.int32, (CHUNK, CHUNK), 1)
     strict, inclusive = row > col, row >= col
@@ -71,24 +76,17 @@
     for first in range(0, raw_ref.shape[0] // CHUNK, GANG):
         starts = [(first + i) * CHUNK for i in range(GANG)]
         each = range(GANG)
-        q, k, v, beta, grow, scale_row, beta_row, tail, last, decay = ([] for _ in range(10))
+        k, v, beta, scale_row, beta_row, tail, last, decay = ([] for _ in range(8))
         for i in each:
             raw = raw_ref[pl.ds(starts[i], CHUNK), :]
-            raw_q = raw[:, 0:128]
             raw_k = raw[:, 128:256]
             raw_v = raw[:, 256:384]
             logits = raw[:, 384:512]
-            q.append(
-                (
-                    raw_q
-                    * lax.rsqrt(jnp.sum(raw_q * raw_q, -1, keepdims=True) + 1e-06)
-                    * DK ** (-0.5)
-                ).astype(bf16)
-            )
             k.append(
                 (raw_k * lax.rsqrt(jnp.sum(raw_k * raw_k, -1, keepdims=True) + 1e-06)).astype(bf16)
             )
             v.append(raw_v.astype(bf16))
+            key_ref[pl.ds(starts[i], CHUNK), :] = k[i]
             x = logits[:, 0:1]
             softplus = jnp.maximum(x, 0.0) + jnp.log1p(jnp.exp(-jnp.abs(x)))
             log_decay = (-rate * softplus).astype(bf16)
@@ -99,15 +97,14 @@
             g_row, b_row = turned[0:1, :], turned[64:65, :]
             g_last = g_row[:, CHUNK - 1 : CHUNK]
             beta.append(b)
-            grow.append(jnp.exp(g))
+            level_ref[pl.ds(starts[i], CHUNK), :] = g
             beta_row.append(b_row)
             scale_row.append(b_row * jnp.exp(g_row))
             tail.append(jnp.exp(g_last - g))
             last.append(jnp.exp(g_last))
             decay.append(jnp.exp(jnp.where(inclusive, g - g_row, 0.0)))
-        both = [mm(jnp.concatenate([q[i], k[i]], 0), k[i], 1, 1) for i in each]
-        scores = [jnp.where(inclusive, both[i][:CHUNK] * decay[i], 0.0) for i in each]
-        lower = [jnp.where(strict, beta[i] * decay[i] * both[i][CHUNK:], 0.0) for i in each]
+        products = [mm(k[i], k[i], 1, 1) for i in each]
+        lower = [jnp.where(strict, beta[i] * decay[i] * products[i], 0.0) for i in each]
         inverse = [eye - jnp.where(below(1), lower[i], 0.0) for i in each]
         for size in (2, 4, 8, 16, 32, 64):
             mask = below(size)
@@ -122,12 +119,9 @@
         wu = [jnp.concatenate([w[i], u[i]], 1) for i in each]
         tail2 = [jnp.concatenate([tail[i], tail[i]], 1) for i in each]
         change = [mm(wu[i] * tail2[i], k[i], 0, 0) for i in each]
-        inside = [mm(scores[i], wu[i]) for i in each]
-        reach = [grow[i] * q[i].astype(f32) - inside[i][:, :DK] for i in each]
-        for i in each:
-            out = mm(reach[i], state, 1, 1)
-            reach_ref[pl.ds(starts[i], CHUNK), :] = out[:, :DK].astype(bf16)
-            own_ref[pl.ds(starts[i], CHUNK), :] = out[:, DK:] + inside[i][:, DK:]
+        for i in each:
+            solved_ref[pl.ds(starts[i], CHUNK), :] = wu[i].astype(bf16)
+            state_ref[first + i] = state.astype(bf16)
             moved = mm(state, change[i][:DK])
             state = last[i] * state - moved
             state = jnp.concatenate([state[:DK], state[DK:] + change[i][DK:]], 0)
@@ -136,6 +130,39 @@
     total_ref[0:DK, :] = (state[:DK] - kept[0:1] * eye).astype(bf16)
     total_ref[DK : DK + DV, :] = state[DK:].astype(bf16)
     total_ref[DK + DV :, :] = jnp.concatenate([part, kept - part], 0).astype(bf16)
+
+
+def reach_kernel(query_ref, key_ref, level_ref, solved_ref, state_ref, reach_ref, own_ref):
+    row = lax.broadcasted_iota(jnp.int32, (CHUNK, CHUNK), 0)
+    col = lax.broadcasted_iota(jnp.int32, (CHUNK, CHUNK), 1)
+    inclusive = row >= col
+
+    gang = 8
+
+    def some(step, carry):
+        each = range(gang)
+        spans = [pl.ds(pl.multiple_of((step * gang + i) * CHUNK, CHUNK), CHUNK) for i in each]
+        q, scores, reach = [], [], []
+        for i in each:
+            raw_q = query_ref[spans[i], :]
+            scale = lax.rsqrt(jnp.sum(raw_q * raw_q, -1, keepdims=True) + 1e-06)
+            q.append((raw_q * scale * DK ** (-0.5)).astype(bf16))
+        products = [mm(q[i], key_ref[spans[i], :], 1, 1) for i in each]
+        for i in each:
+            g = level_ref[spans[i], :]
+            decay = jnp.exp(jnp.where(inclusive, g - g.T, 0.0))
+            scores.append(jnp.where(inclusive, products[i] * decay, 0.0))
+        inside = [mm(scores[i], solved_ref[spans[i], :]) for i in each]
+        for i in each:
+            grown = jnp.exp(level_ref[spans[i], :]) * q[i].astype(f32)
+            reach.append(grown - inside[i][:, :DK])
+        out = [mm(reach[i], state_ref[step * gang + i], 1, 1) for i in each]
+        for i in each:
+            reach_ref[spans[i], :] = out[i][:, :DK].astype(bf16)
+            own_ref[spans[i], :] = out[i][:, DK:] + inside[i][:, DK:]
+        return carry
+
+    lax.fori_loop(0, state_ref.shape[0] // gang, some, 0)
 
 
 def opened(map_ref, *at):
@@ -212,12 +239,15 @@
 
     block_rows, features = all_tokens.shape
     steps = 2
-    reach, own, total = pl.pallas_call(
+    total, *kept = pl.pallas_call(
         chunk_kernel,
         out_shape=(
+            jax.ShapeDtypeStruct((MAP_ROWS, DK), bf16),
+            jax.ShapeDtypeStruct((block_rows, DK), f32),
             jax.ShapeDtypeStruct((block_rows, DK), bf16),
-            jax.ShapeDtypeStruct((block_rows, DV), f32),
-            jax.ShapeDtypeStruct((MAP_ROWS, DK), bf16),
+            jax.ShapeDtypeStruct((block_rows, CHUNK), f32),
+            jax.ShapeDtypeStruct((block_rows, DK + DV), bf16),
+            jax.ShapeDtypeStruct((block_rows // CHUNK, DK + DV, DK), bf16),
         ),
         grid=(steps,),
         in_specs=[
@@ -229,14 +259,17 @@
             pl.BlockSpec((features, WIDE // 2), lambda i: (0, 0)),
         ],
         out_specs=(
+            pl.BlockSpec((MAP_ROWS, DK), lambda i: (0, 0)),
             pl.BlockSpec((block_rows, DK), lambda i: (0, 0)),
-            pl.BlockSpec((block_rows, DV), lambda i: (0, 0)),
-            pl.BlockSpec((MAP_ROWS, DK), lambda i: (0, 0)),
+            pl.BlockSpec((block_rows, DK), lambda i: (0, 0)),
+            pl.BlockSpec((block_rows, CHUNK), lambda i: (0, 0)),
+            pl.BlockSpec((block_rows, DK + DV), lambda i: (0, 0)),
+            pl.BlockSpec((block_rows // CHUNK, DK + DV, DK), lambda i: (0, 0, 0)),
         ),
         scratch_shapes=[
             pltpu.VMEM((block_rows, WIDE), f32),
         ],
-        compiler_params=pltpu.CompilerParams(vmem_limit_bytes=48 * 2**20),
+        compiler_params=pltpu.CompilerParams(vmem_limit_bytes=36 * 2**20),
     )(
         jnp.stack([head, at_c]).astype(jnp.int32),
         decay_rate,
@@ -246,6 +279,19 @@
         swapped,
     )
 
+    reach, own = pl.pallas_call(
+        reach_kernel,
+        out_shape=(
+            jax.ShapeDtypeStruct((block_rows, DK), bf16),
+            jax.ShapeDtypeStruct((block_rows, DV), f32),
+        ),
+        in_specs=[vmem] * 5,
+        out_specs=(vmem, vmem),
+        compiler_params=pltpu.CompilerParams(vmem_limit_bytes=20 * 2**20),
+        cost_estimate=pl.CostEstimate(
+            flops=10 * block_rows * CHUNK * DK, bytes_accessed=6 * 2**20, transcendentals=0
+        ),
+    )(*kept)
     core = at_c.reshape(1).astype(jnp.int32)
     other = lax.ppermute(total, "tm_2", [(0, 1), (1, 0)])
     maps = pl.pallas_call(
@@ -261,7 +307,7 @@
         out_shape=jax.ShapeDtypeStruct((block_rows, DV), bf16),
         in_specs=[smem, vmem, vmem, vmem, vmem],
         out_specs=vmem,
-        compiler_params=pltpu.CompilerParams(vmem_limit_bytes=32 * 2**20),
+        compiler_params=pltpu.CompilerParams(vmem_limit_bytes=12 * 2**20),
     )(place, maps, other, reach, own)
     returned = lax.all_to_all(readout, "stream", split_axis=0, concat_axis=1, tiled=True)
     head_read = returned.reshape(local_rows, HEADS, DV).astype(f32)

time: 213 us -> 220 us (1.033)
  local copies, waits for them, and re-layouts: 5.23 us -> 19.2 us
  waiting for transfers between devices: 104 us -> 97 us
    unnamed x20 -> x42, local copies, waits for them, and re-layouts: 3.09 us -> 17.1 us
    all_to_all x1, waiting for transfers between devices: 18.6 us -> 11.8 us  [shards(): lax.all_to_all(maps, ('tm_0', 'tm_1'), split_axis=0, concat_axis=0, tiled...]
    pallas_call x1 -> x2, Pallas kernels: 13.6 us -> 13 us  [the longest x1 11.6 us: shards(): pl.pallas_call(chunk_kernel, out_shape=(jax.ShapeDtypeStruct((MAP_ROWS, D...]
  transfers between devices with their start and end apart: 5 -> 5, of which waited for: 5 -> 5; matrix products, arithmetic and copies ran while one was open for 1% -> 1% of each run, Pallas kernels for 0% -> 1%
where the time goes in v8:
time: 220 us; the launch traced here: 219 us
  waiting for transfers between devices  97 us (44%)
  blocking collectives  48.7 us (22%)
  starting transfers between devices  21.8 us (10%)
  local copies, waits for them, and re-layouts  19.2 us (9%)
  Pallas kernels  16.9 us (8%)
  between operations  13.6 us (6%)
    all_gather x1, waiting for transfers between devices, shards(): all_tokens = lax.all_gather(tokens, 'stream', axis=0, tiled=True)  53.1 us
    all_to_all x1, waiting for transfers between devices, shards(): lax.all_to_all(readout, 'stream', split_axis=0, concat_axis=1, tiled=True)  27.6 us
    all_to_all x1, blocking collectives, shards(): lax.all_to_all(weights, 'stream', split_axis=0, concat_axis=0, tiled=True)  25.6 us
    all_to_all x1, blocking collectives, shards(): lax.all_to_all(weights, ('tm_0', 'tm_1'), split_axis=0, concat_axis=0, ti...  23.1 us
    unnamed x42, local copies, waits for them, and re-layouts  17.1 us
    all_to_all x1, waiting for transfers between devices, shards(): lax.all_to_all(maps, ('tm_0', 'tm_1'), split_axis=0, concat_axis=0, tiled...  11.8 us
    pallas_call x1, Pallas kernels, shards(): pl.pallas_call(chunk_kernel, out_shape=(jax.ShapeDtypeStruct((MAP_ROWS, D...  11.6 us
    all_to_all x1, starting transfers between devices, shards(): lax.all_to_all(readout, 'stream', split_axis=0, concat_axis=1, tiled=True)  11 us
  transfers between devices with their start and end apart: 5, of which 5 were waited for; matrix products, arithmetic and copies ran while one was open for 1% of the time, Pallas kernels for 1%

profile of v8, /device:TPU:64, one launch (start us, length us, event | category | flops | bytes accessed | tf_op | source)
XLA Modules:
  0.0 219.0 jit_solution(13881135282134106392)
XLA Ops:
  6.5 0.0 copy-start
  6.5 0.7 all-gather.2.cloned.1.call-update
  7.3 0.8 constant_dynamic-slice_fusion
  8.1 0.1 copy.21
  8.1 0.1 copy.17
  8.3 0.1 copy.22
  8.4 0.1 copy.18
  8.5 0.1 pad.3.clone
  8.6 0.8 dynamic-slice_bitcast_fusion
  9.4 0.1 fusion.4
  9.5 25.6 %all_to_all.28 = bf16[16,8,256]{2,1,0:T(8,128)(2,1)S(1)} all-to-all(bf16[16,8,256]{2,1,0:T(8,128)(2,1)S(1)} %fusion.4), channel_id=1, replica_groups=mesh['tm_0'=4,'tm_1'=4,'tm_2'=2,'stream'=16] {'stream'}, dimensions={0} | all-to-all | bytes 131072 | tf_op jit(solution)/shard_map/all_to_all | solution.py:234
  35.1 0.1 broadcast_in_dim.5
  35.2 23.1 %all_to_all.29 = bf16[16,16,8,256]{3,2,1,0:T(8,128)(2,1)S(1)} all-to-all(bf16[16,16,8,256]{3,2,1,0:T(8,128)(2,1)S(1)} %broadcast_in_dim.5), channel_id=1, replica_groups=mesh['tm_0'=4,'tm_1'=4,'tm_2'=2,'stream'=16] {'tm_0','tm_1'}, dimensions={0} | all-to-all | bytes 2097152 | tf_op jit(solution)/shard_map/all_to_all | solution.py:236
  58.3 0.1 copy.19
  58.4 1.9 collective-permute-start
  60.4 0.1 pad_add_fusion.1.head_ref
  60.5 2.5 %collective-permute-done.other_ref = bf16[2048,256]{1,0:T(8,128)(2,1)S(1)} collective-permute-done((bf16[2048,256]{1,0:T(8,128)(2,1)S(1)}, bf16[2048,256]{1,0:T(8,128)(2,1)S(1)}, u32[]{:S(2)}, u32[]{:S(2)}) %collective-permute-start) | collective-permute-done | bytes 1048608 | tf_op jit(solution)/shard_map/ppermute | solution.py:238
  63.0 1.0 copy-done.10
  64.0 53.1 %all-gather.2.cloned.1.call-done.token_ref = bf16[2048,2048]{1,0:T(8,128)(2,1)} async-done(((bf16[128,2048]{1,0:T(8,128)(2,1)}), bf16[2048,2048]{1,0:T(8,128)(2,1)}) %all-gather.2.cloned.1.call-update) | async-done | bytes 8388624 | tf_op jit(solution)/shard_map/all_gather | solution.py:233
  117.2 0.0 copy-done.18
  117.2 3.4 %copy-done.1 = bf16[2048,2048]{1,0:T(8,128)(2,1)S(1)} copy-done((bf16[2048,2048]{1,0:T(8,128)(2,1)S(1)}, bf16[2048,2048]{1,0:T(8,128)(2,1)}, u32[]{:S(2)}) %copy-start.1) | copy-done | bytes 8388632
  120.6 1.2 copy-done.11
  121.8 11.6 %shard_map.91 = (bf16[272,128]{1,0:T(8,128)(2,1)S(1)}, f32[2048,128]{1,0:T(8,128)S(1)}, bf16[2048,128]{1,0:T(8,128)(2,1)S(1)}, f32[2048,128]{1,0:T(8,128)S(1)}, ...) custom-call(s32[2]{0:T(128)S(1)} %pad_add_fusion.1.head_ref, f32[16]{0:T(128)S(1)} %copy-done.17, ...), custom_call_target="tpu_custom_call" | custom-call | tf_op jit(solution)/shard_map/pallas_call | solution.py:242
  133.4 0.0 copy-start.2
  133.4 1.0 copy-done.2
  134.4 1.0 copy-done.4
  135.4 1.0 copy-done.6
  136.4 1.9 collective-permute-start.1
  138.3 1.2 collective-permute-done.1.other_ref
  139.5 0.0 copy-done.16
  139.5 0.6 copy-done.14
  140.2 2.2 shard_map.92
  142.3 6.9 %all-to-all-start.2 = ((bf16[16,272,128]{2,1,0:T(8,128)(2,1)}), bf16[16,272,128]{2,1,0:T(8,128)(2,1)S(1)}, u32[]{:S(2)}, u32[]{:S(2)}) async-start(bf16[16,272,128]{2,1,0:T(8,128)(2,1)} %shard_map.92), calls=%async_computation.2 | async-start | bytes 2228224 | tf_op jit(solution)/shard_map/all_to_all | solution.py:303
  149.2 0.1 pad_add_fusion.place_ref
  149.3 1.2 copy-done.3
  150.5 1.2 copy-done.5
  151.8 1.2 copy-done.7
  153.0 1.3 shard_map.93
  154.3 1.0 copy-done.8
  155.3 0.8 copy-done.12
  156.1 11.8 %all-to-all-done.2.map_ref = bf16[16,272,128]{2,1,0:T(8,128)(2,1)S(1)} async-done(((bf16[16,272,128]{2,1,0:T(8,128)(2,1)}), bf16[16,272,128]{2,1,0:T(8,128)(2,1)S(1)}, u32[]{:S(2)}, u32[]{:S(2)}) %all-to-all-start.2) | async-done | bytes 1114144 | tf_op jit(solution)/shard_map/all_to_all | solution.py:303
  167.9 1.2 copy-done.9
  169.2 1.0 copy-done.13
  170.2 1.8 shard_map.94
  172.0 11.0 %all-to-all-start.3 = ((bf16[16,128,128]{2,1,0:T(8,128)(2,1)}), bf16[16,128,128]{2,1,0:T(8,128)(2,1)S(1)}, u32[]{:S(2)}, u32[]{:S(2)}) async-start(bf16[16,128,128]{2,1,0:T(8,128)(2,1)} %bitcast.11), calls=%async_computation.3 | async-start | bytes 1048576 | tf_op jit(solution)/shard_map/all_to_all | solution.py:312
  183.0 27.6 %all-to-all-done.3 = bf16[16,128,128]{2,1,0:T(8,128)(2,1)S(1)} async-done(((bf16[16,128,128]{2,1,0:T(8,128)(2,1)}), bf16[16,128,128]{2,1,0:T(8,128)(2,1)S(1)}, u32[]{:S(2)}, u32[]{:S(2)}) %all-to-all-start.3) | async-done | bytes 524320 | tf_op jit(solution)/shard_map/all_to_all | solution.py:312
  210.6 0.3 fusion.2
  211.0 1.1 fusion.3
  (27 shorter events, 0.1 us)
Async XLA Ops:
  6.5 2.1 copy-start
  6.5 110.6 %all-gather.2.cloned.1.call-start = ((), (), s32[]{:S(2)}) async-start(), calls=%async_computation.4 | async-start | bytes 8912896 | tf_op jit(solution)/shard_map/all_gather | solution.py:233
  58.3 58.8 %copy-start.17 = (f32[16]{0:T(128)S(1)}, f32[16]{0:T(128)}, u32[]{:S(2)}) copy-start(f32[16]{0:T(128)} %rate_ref.1) | copy-start | bytes 196
  58.3 58.8 %copy-start.18 = (f32[16]{0:T(128)S(1)}, f32[16]{0:T(128)}, u32[]{:S(2)}) copy-start(f32[16]{0:T(128)} %bias_ref.1) | copy-start | bytes 196
  58.4 4.6 %collective-permute-start = (bf16[2048,256]{1,0:T(8,128)(2,1)S(1)}, bf16[2048,256]{1,0:T(8,128)(2,1)S(1)}, u32[]{:S(2)}, u32[]{:S(2)}) collective-permute-start(bf16[2048,256]{1,0:T(8,128)(2,1)S(1)} %bitcast.34), channel_id=1, source_target_pairs={{0,16},{16,0},{1,17},{17,1},{2,18},{18,2},{3,19},{19,3},{4,20},{20... | collective-permute-start | bytes 3145736 | tf_op jit(solution)/shard_map/ppermute | solution.py:238
  63.0 1.0 copy-start.10
  117.2 3.4 %copy-start.1 = (bf16[2048,2048]{1,0:T(8,128)(2,1)S(1)}, bf16[2048,2048]{1,0:T(8,128)(2,1)}, u32[]{:S(2)}) copy-start(bf16[2048,2048]{1,0:T(8,128)(2,1)} %all-gather.2.cloned.1.call-done.token_ref) | copy-start | bytes 25165828
  120.6 1.2 copy-start.11
  133.4 1.0 copy-start.2
  134.4 1.0 copy-start.4
  135.4 1.0 copy-start.6
  136.4 3.1 %copy-start.16 = (bf16[272,128]{1,0:T(8,128)(2,1)}, bf16[272,128]{1,0:T(8,128)(2,1)S(1)}, u32[]{:S(2)}) copy-start(bf16[272,128]{1,0:T(8,128)(2,1)S(1)} %get-tuple-element.13.mine_ref) | copy-start | bytes 208900
  136.4 3.1 %collective-permute-start.1 = (bf16[272,128]{1,0:T(8,128)(2,1)S(1)}, bf16[272,128]{1,0:T(8,128)(2,1)S(1)}, u32[]{:S(2)}, u32[]{:S(2)}) collective-permute-start(bf16[272,128]{1,0:T(8,128)(2,1)S(1)} %get-tuple-element.13.mine_ref), channel_id=1, source_target_pairs={{0,16},{16,0},{1,17},{17,1},{2,18},{18,2},{3,19},{19,3},{4,20},{20... | collective-permute-start | bytes 208904 | tf_op jit(solution)/shard_map/ppermute | solution.py:296
  139.5 0.6 copy-start.14
  142.3 25.6 %all-to-all-start.2 = ((bf16[16,272,128]{2,1,0:T(8,128)(2,1)}), bf16[16,272,128]{2,1,0:T(8,128)(2,1)S(1)}, u32[]{:S(2)}, u32[]{:S(2)}) async-start(bf16[16,272,128]{2,1,0:T(8,128)(2,1)} %shard_map.92), calls=%async_computation.2 | async-start | bytes 2228224 | tf_op jit(solution)/shard_map/all_to_all | solution.py:303
  149.3 1.2 copy-start.3
  150.5 1.2 copy-start.5
  151.8 1.2 copy-start.7
  153.0 14.9 %copy-start.15 = (bf16[272,128]{1,0:T(8,128)(2,1)S(1)}, bf16[272,128]{1,0:T(8,128)(2,1)}, u32[]{:S(2)}) copy-start(bf16[272,128]{1,0:T(8,128)(2,1)} %copy-done.14) | copy-start | bytes 208900
  154.3 1.0 copy-start.8
  155.3 0.8 copy-start.12
  167.9 1.2 copy-start.9
  169.1 1.0 copy-start.13
  170.2 12.8 %copy-start.19 = (f32[128]{0:T(128)S(1)}, f32[128]{0:T(128)}, u32[]{:S(2)}) copy-start(f32[128]{0:T(128)} %param.17) | copy-start | bytes 1540
  172.0 38.7 %all-to-all-start.3 = ((bf16[16,128,128]{2,1,0:T(8,128)(2,1)}), bf16[16,128,128]{2,1,0:T(8,128)(2,1)S(1)}, u32[]{:S(2)}, u32[]{:S(2)}) async-start(bf16[16,128,128]{2,1,0:T(8,128)(2,1)} %bitcast.11), calls=%async_computation.3 | async-start | bytes 1048576 | tf_op jit(solution)/shard_map/all_to_all | solution.py:312
Sparse Core Ops, SparseCore 0:
  9.4 107.6 all-gather.1

commit v9 on v7

--- a/solution.py
+++ b/solution.py
@@ -144,39 +144,40 @@
     return change, shift.astype(f32), kept[0:1] + kept[8:9]
 
 
-def join_kernel(core_ref, mine_ref, other_ref, copies_ref):
-    def write(first_ref, second_ref):
-        change, shift, kept = opened(first_ref)
-        next_change, next_shift, next_kept = opened(second_ref)
-        joined = kept * next_change.astype(f32) + next_kept * change.astype(f32)
-        joined = (joined + mm(change, next_change)).astype(bf16)
-        shift = (next_kept * shift + mm(shift, next_change) + next_shift).astype(bf16)
-        kept = jnp.broadcast_to(kept * next_kept, (8, DK))
-        part = kept.astype(bf16).astype(f32)
-        kept = jnp.concatenate([part, kept - part], 0).astype(bf16)
-        for i in range(copies_ref.shape[0]):
-            copies_ref[i, 0:DK, :] = joined
-            copies_ref[i, DK : DK + DV, :] = shift
-            copies_ref[i, DK + DV : MAP_ROWS, :] = kept
-
-    @pl.when(core_ref[0] == 0)
-    def _():
-        write(mine_ref, other_ref)
-
-    @pl.when(core_ref[0] == 1)
-    def _():
-        write(other_ref, mine_ref)
-
-
-def read_kernel(place_ref, map_ref, other_ref, reach_ref, own_ref, read_ref):
-    def after(state, change, shift, kept):
-        return kept * state + mm(state, change) + shift
-
+def after(state, change, shift, kept):
+    return kept * state + mm(state, change) + shift
+
+
+def join_kernel(place_ref, map_ref, before_ref, kept_ref, copies_ref):
+    row = lax.broadcasted_iota(jnp.int32, (DK + DV, DK), 0)
+    col = lax.broadcasted_iota(jnp.int32, (DK + DV, DK), 1)
+    eye = jnp.where(row == col, 1.0, 0.0).astype(f32)
+    state, decay = eye, jnp.ones((1, DK), f32)
+    for j in range(map_ref.shape[0]):
+
+        @pl.when(place_ref[1] == j)
+        def _():
+            before_ref[...] = state - decay * eye
+            kept_ref[...] = jnp.broadcast_to(decay, (8, DK))
+
+        change, shift, kept = opened(map_ref, j)
+        state = after(state, change, jnp.concatenate([jnp.zeros((DK, DK), f32), shift], 0), kept)
+        decay = kept * decay
+    state = (state - decay * eye).astype(bf16)
+    decay = jnp.broadcast_to(decay, (8, DK))
+    part = decay.astype(bf16).astype(f32)
+    decay = jnp.concatenate([part, decay - part], 0).astype(bf16)
+    for i in range(copies_ref.shape[0]):
+        copies_ref[i, 0 : DK + DV, :] = state
+        copies_ref[i, DK + DV : MAP_ROWS, :] = decay
+
+
+def read_kernel(place_ref, map_ref, before_ref, kept_ref, reach_ref, own_ref, read_ref):
     def one(j, state):
         return after(state, *opened(map_ref, j))
 
     state = lax.fori_loop(0, place_ref[0], one, jnp.zeros((DV, DK), f32))
-    state = jnp.where(place_ref[1] == 1, after(state, *opened(other_ref)), state)
+    state = after(state, before_ref[0:DK, :], before_ref[DK:, :], kept_ref[0:1, :])
     read_ref[...] = (mm(reach_ref[...], state, 1, 1) + own_ref[...]).astype(bf16)
 
 
@@ -246,23 +247,26 @@
         swapped,
     )
 
-    core = at_c.reshape(1).astype(jnp.int32)
-    other = lax.ppermute(total, "tm_2", [(0, 1), (1, 0)])
-    maps = pl.pallas_call(
+    place = jnp.stack([at_y, at_x * 2 + at_c]).astype(jnp.int32)
+    maps = lax.all_gather(total, ("tm_1", "tm_2"), axis=0)
+    before, kept, maps = pl.pallas_call(
         join_kernel,
-        out_shape=jax.ShapeDtypeStruct((shares, MAP_ROWS, DK), bf16),
-        in_specs=[smem, vmem, vmem],
-        out_specs=vmem,
-    )(core, total, other)
-    maps = lax.all_to_all(maps, ("tm_0", "tm_1"), split_axis=0, concat_axis=0, tiled=True)
-    place = jnp.stack([at_y * 4 + at_x, at_c]).astype(jnp.int32)
+        out_shape=(
+            jax.ShapeDtypeStruct((DK + DV, DK), f32),
+            jax.ShapeDtypeStruct((8, DK), f32),
+            jax.ShapeDtypeStruct((4, MAP_ROWS, DK), bf16),
+        ),
+        in_specs=[smem, vmem],
+        out_specs=(vmem, vmem, vmem),
+    )(place, maps)
+    maps = lax.all_to_all(maps, "tm_0", split_axis=0, concat_axis=0, tiled=True)
     readout = pl.pallas_call(
         read_kernel,
         out_shape=jax.ShapeDtypeStruct((block_rows, DV), bf16),
-        in_specs=[smem, vmem, vmem, vmem, vmem],
+        in_specs=[smem] + [vmem] * 5,
         out_specs=vmem,
         compiler_params=pltpu.CompilerParams(vmem_limit_bytes=32 * 2**20),
-    )(place, maps, other, reach, own)
+    )(place, maps, before, kept, reach, own)
     returned = lax.all_to_all(readout, "stream", split_axis=0, concat_axis=1, tiled=True)
     head_read = returned.reshape(local_rows, HEADS, DV).astype(f32)
     normed = (

time: 213 us -> 214 us (level)
  the two profiles are of different devices: /device:TPU:64 before, /device:TPU:32 now
where the time goes in v9:
time: 214 us
  waiting for transfers between devices  83.1 us (39%)
  blocking collectives  76.1 us (36%)
  Pallas kernels  18.5 us (9%)
  between operations  13.5 us (6%)
  starting transfers between devices  12.9 us (6%)
  local copies, waits for them, and re-layouts  7.49 us (4%)
  other arithmetic  2.29 us (1%)
    all_gather x1, waiting for transfers between devices, shards(): all_tokens = lax.all_gather(tokens, 'stream', axis=0, tiled=True)  52.5 us
    all_to_all x1, waiting for transfers between devices, shards(): lax.all_to_all(readout, 'stream', split_axis=0, concat_axis=1, tiled=True)  27.9 us
    all_to_all x1, blocking collectives, shards(): lax.all_to_all(weights, 'stream', split_axis=0, concat_axis=0, tiled=True)  26.6 us
    all_to_all x1, blocking collectives, shards(): lax.all_to_all(weights, ('tm_0', 'tm_1'), split_axis=0, concat_axis=0, ti...  23.2 us
    all_gather x1, blocking collectives, shards(): maps = lax.all_gather(total, ('tm_1', 'tm_2'), axis=0)  14.6 us
    pallas_call x1, Pallas kernels, shards(): pl.pallas_call(chunk_kernel, out_shape=(jax.ShapeDtypeStruct((block_rows,...  13.6 us
    all_to_all x1, blocking collectives, shards(): maps = lax.all_to_all(maps, 'tm_0', split_axis=0, concat_axis=0, tiled=True)  11.8 us
    all_to_all x1, starting transfers between devices, shards(): lax.all_to_all(readout, 'stream', split_axis=0, concat_axis=1, tiled=True)  11 us
  transfers between devices with their start and end apart: 3, of which 3 were waited for; matrix products, arithmetic and copies ran while one was open for 1% of the time, Pallas kernels for 0%

profile of v9, /device:TPU:32, one launch (start us, length us, event | category | flops | bytes accessed | tf_op | source)
XLA Modules:
  0.0 213.9 jit_solution(7375571567834739776)
XLA Ops:
  6.5 0.0 copy-start
  6.5 0.0 all-gather.3.cloned.1.call-start
  6.5 0.7 all-gather.3.cloned.1.call-update
  7.3 0.8 constant_dynamic-slice_fusion
  8.1 0.1 copy.21
  8.1 0.1 copy.17
  8.3 0.1 copy.22
  8.4 0.1 copy.18
  8.5 0.1 pad.3.clone
  8.6 0.0 copy-done
  8.6 0.8 dynamic-slice_bitcast_fusion
  9.4 0.1 fusion.4
  9.5 26.6 %all_to_all.28 = bf16[16,8,256]{2,1,0:T(8,128)(2,1)S(1)} all-to-all(bf16[16,8,256]{2,1,0:T(8,128)(2,1)S(1)} %fusion.4), channel_id=1, replica_groups=mesh['tm_0'=4,'tm_1'=4,'tm_2'=2,'stream'=16] {'stream'}, dimensions={0} | all-to-all | bytes 131072 | tf_op jit(solution)/shard_map/all_to_all | solution.py:208
  36.1 0.1 broadcast_in_dim.5
  36.2 23.2 %all_to_all.29 = bf16[16,16,8,256]{3,2,1,0:T(8,128)(2,1)S(1)} all-to-all(bf16[16,16,8,256]{3,2,1,0:T(8,128)(2,1)S(1)} %broadcast_in_dim.5), channel_id=1, replica_groups=mesh['tm_0'=4,'tm_1'=4,'tm_2'=2,'stream'=16] {'tm_0','tm_1'}, dimensions={0} | all-to-all | bytes 2097152 | tf_op jit(solution)/shard_map/all_to_all | solution.py:210
  59.4 0.1 copy.19
  59.5 0.0 copy-start.8
  59.5 1.9 collective-permute-start
  61.4 0.1 pad_add_fusion.1.head_ref
  61.5 0.6 pad_add_fusion.place_ref
  62.1 1.9 collective-permute-done.other_ref
  64.0 0.0 copy-start.1
  64.0 1.1 copy-done.1
  65.1 52.5 %all-gather.3.cloned.1.call-done.token_ref = bf16[2048,2048]{1,0:T(8,128)(2,1)} async-done(((bf16[128,2048]{1,0:T(8,128)(2,1)}), bf16[2048,2048]{1,0:T(8,128)(2,1)}) %all-gather.3.cloned.1.call-update) | async-done | bytes 8388624 | tf_op jit(solution)/shard_map/all_gather | solution.py:207
  117.6 0.0 copy-start.2
  117.6 1.2 copy-done.2
  118.9 0.0 copy-start.6
  118.9 0.7 copy-done.6
  119.5 0.0 copy-start.7
  119.5 0.7 copy-done.7
  120.2 0.0 copy-start.5
  120.2 13.6 %shard_map.91 = (bf16[2048,128]{1,0:T(8,128)(2,1)S(1)}, f32[2048,128]{1,0:T(8,128)S(1)}, bf16[272,128]{1,0:T(8,128)(2,1)S(1)}) custom-call(s32[2]{0:T(128)S(1)} %pad_add_fusion.1.head_ref, f32[16]{0:T(128)S(1)} %copy-done.6, f32[16]{0:T(128)S(1)} %copy-done.7, bf16[2048,2048]{1,0:T(8,128)(2,1)} %all-gather.3.cloned.1.call-done.token_ref, ...), custom_call_target="tpu_custom_call" | custom-call | tf_op jit(solution)/shard_map/pallas_call | solution.py:216
  133.8 14.6 %all-gather = bf16[2176,128]{1,0:T(8,128)(2,1)} all-gather(bf16[272,128]{1,0:T(8,128)(2,1)S(1)} %get-tuple-element.11), channel_id=2, replica_groups=mesh['tm_0'=4,'tm_1'=4,'tm_2'=2,'stream'=16] {'tm_1','tm_2'}, dimensions={0}, use_global_device_ids=true | all-gather | bytes 626688 | tf_op jit(solution)/shard_map/all_gather | solution.py:251
  148.4 3.1 %shard_map.92 = (f32[256,128]{1,0:T(8,128)}, f32[8,128]{1,0:T(8,128)}, bf16[4,272,128]{2,1,0:T(8,128)(2,1)}) custom-call(s32[2]{0:T(128)} %pad_add_fusion.place_ref, bf16[8,272,128]{2,1,0:T(8,128)(2,1)} %bitcast.39), custom_call_target="tpu_custom_call" | custom-call | tf_op jit(solution)/shard_map/pallas_call | solution.py:252
  151.5 11.8 %all_to_all.30.map_ref = bf16[4,272,128]{2,1,0:T(8,128)(2,1)S(1)} all-to-all(bf16[4,272,128]{2,1,0:T(8,128)(2,1)} %get-tuple-element.12), channel_id=1, replica_groups=mesh['tm_0'=4,'tm_1'=4,'tm_2'=2,'stream'=16] {'tm_0'}, dimensions={0} | all-to-all | bytes 557056 | tf_op jit(solution)/shard_map/all_to_all | solution.py:262
  163.3 0.0 copy-done.5
  163.3 0.0 copy-start.3
  163.3 0.9 copy-done.3
  164.2 0.0 copy-start.4
  164.2 0.7 copy-done.4
  164.8 1.8 shard_map.93
  166.6 11.0 %all-to-all-start.3 = ((bf16[16,128,128]{2,1,0:T(8,128)(2,1)}), bf16[16,128,128]{2,1,0:T(8,128)(2,1)S(1)}, u32[]{:S(2)}, u32[]{:S(2)}) async-start(bf16[16,128,128]{2,1,0:T(8,128)(2,1)} %bitcast.13), calls=%async_computation.3 | async-start | bytes 1048576 | tf_op jit(solution)/shard_map/all_to_all | solution.py:270
  177.6 0.0 copy-done.8
  177.6 27.9 %all-to-all-done.3 = bf16[16,128,128]{2,1,0:T(8,128)(2,1)S(1)} async-done(((bf16[16,128,128]{2,1,0:T(8,128)(2,1)}), bf16[16,128,128]{2,1,0:T(8,128)(2,1)S(1)}, u32[]{:S(2)}, u32[]{:S(2)}) %all-to-all-start.3) | async-done | bytes 524320 | tf_op jit(solution)/shard_map/all_to_all | solution.py:270
  205.5 0.3 fusion.2
  205.9 1.1 fusion.3
  (4 shorter events, 0.0 us)
Async XLA Ops:
  6.5 2.1 copy-start
  6.5 111.1 %all-gather.3.cloned.1.call-start = ((), (), s32[]{:S(2)}) async-start(), calls=%async_computation.4 | async-start | bytes 8912896 | tf_op jit(solution)/shard_map/all_gather | solution.py:207
  59.5 118.1 %copy-start.8 = (f32[128]{0:T(128)S(1)}, f32[128]{0:T(128)}, u32[]{:S(2)}) copy-start(f32[128]{0:T(128)} %param.17) | copy-start | bytes 1540
  59.5 4.6 %collective-permute-start = (bf16[2048,256]{1,0:T(8,128)(2,1)S(1)}, bf16[2048,256]{1,0:T(8,128)(2,1)S(1)}, u32[]{:S(2)}, u32[]{:S(2)}) collective-permute-start(bf16[2048,256]{1,0:T(8,128)(2,1)S(1)} %bitcast.36), channel_id=1, source_target_pairs={{0,16},{16,0},{1,17},{17,1},{2,18},{18,2},{3,19},{19,3},{4,20},{20... | collective-permute-start | bytes 3145736 | tf_op jit(solution)/shard_map/ppermute | solution.py:212
  64.0 1.1 copy-start.1
  117.6 1.2 copy-start.2
  118.9 0.7 copy-start.6
  119.5 0.7 copy-start.7
  120.2 43.1 %copy-start.5 = (s32[2]{0:T(128)S(1)}, s32[2]{0:T(128)}, u32[]{:S(2)}) copy-start(s32[2]{0:T(128)} %pad_add_fusion.place_ref) | copy-start | bytes 28
  163.3 0.9 copy-start.3
  164.2 0.7 copy-start.4
  166.6 38.9 %all-to-all-start.3 = ((bf16[16,128,128]{2,1,0:T(8,128)(2,1)}), bf16[16,128,128]{2,1,0:T(8,128)(2,1)S(1)}, u32[]{:S(2)}, u32[]{:S(2)}) async-start(bf16[16,128,128]{2,1,0:T(8,128)(2,1)} %bitcast.13), calls=%async_computation.3 | async-start | bytes 1048576 | tf_op jit(solution)/shard_map/all_to_all | solution.py:270
Sparse Core Ops, SparseCore 0:
  9.4 108.1 all-gather.2

commit v10 on v9

--- a/solution.py
+++ b/solution.py
@@ -29,8 +29,7 @@
     rate_ref,
     bias_ref,
     token_ref,
-    mine_ref,
-    other_ref,
+    weight_ref,
     reach_ref,
     own_ref,
     total_ref,
@@ -39,13 +38,9 @@
     step, steps = pl.program_id(0), pl.num_programs(0)
     rate, bias = rate_ref[head_ref[0]], bias_ref[head_ref[0]]
     size = token_ref.shape[0]
-    rows = pl.ds(pl.multiple_of(step * size, size), size)
-    half = mine_ref.shape[1]
-    for c in range(2):
-        weights = jnp.where(head_ref[1] == c, mine_ref[...], other_ref[...])
-        raw_ref[rows, c * half : (c + 1) * half] = jnp.dot(
-            token_ref[...], weights, preferred_element_type=f32
-        )
+    raw_ref[pl.ds(pl.multiple_of(step * size, size), size), :] = jnp.dot(
+        token_ref[...], weight_ref[...], preferred_element_type=f32
+    )
 
     @pl.when(step == steps - 1)
     def _():
@@ -155,7 +150,7 @@
     state, decay = eye, jnp.ones((1, DK), f32)
     for j in range(map_ref.shape[0]):
 
-        @pl.when(place_ref[1] == j)
+        @pl.when(place_ref[2] == j)
         def _():
             before_ref[...] = state - decay * eye
             kept_ref[...] = jnp.broadcast_to(decay, (8, DK))
@@ -176,7 +171,7 @@
     def one(j, state):
         return after(state, *opened(map_ref, j))
 
-    state = lax.fori_loop(0, place_ref[0], one, jnp.zeros((DV, DK), f32))
+    state = lax.fori_loop(0, place_ref[1], one, jnp.zeros((DV, DK), f32))
     state = after(state, before_ref[0:DK, :], before_ref[DK:, :], kept_ref[0:1, :])
     read_ref[...] = (mm(reach_ref[...], state, 1, 1) + own_ref[...]).astype(bf16)
 
@@ -208,8 +203,14 @@
     weights = lax.all_to_all(weights, "stream", split_axis=0, concat_axis=0, tiled=True)
     weights = jnp.broadcast_to(weights[None], (shares,) + weights.shape)
     weights = lax.all_to_all(weights, ("tm_0", "tm_1"), split_axis=0, concat_axis=0, tiled=True)
-    weights = weights.transpose(1, 0, 2, 3).reshape(streams * shares * rows, WIDE // 2)
     swapped = lax.ppermute(weights, "tm_2", [(0, 1), (1, 0)])
+    halves = [
+        jnp.where(at_c == 0, weights, swapped),
+        jnp.where(at_c == 0, swapped, weights),
+    ]
+    weights = jnp.concatenate(halves, -1)
+    weights = weights.transpose(1, 0, 2, 3).reshape(streams * shares * rows, WIDE)
+    place = jnp.stack([head, at_y, at_x * 2 + at_c]).astype(jnp.int32)
 
     block_rows, features = all_tokens.shape
     steps = 2
@@ -226,8 +227,7 @@
             smem,
             smem,
             pl.BlockSpec((block_rows // steps, features), lambda i: (i, 0)),
-            pl.BlockSpec((features, WIDE // 2), lambda i: (0, 0)),
-            pl.BlockSpec((features, WIDE // 2), lambda i: (0, 0)),
+            pl.BlockSpec((features, WIDE), lambda i: (0, 0)),
         ],
         out_specs=(
             pl.BlockSpec((block_rows, DK), lambda i: (0, 0)),
@@ -239,15 +239,13 @@
         ],
         compiler_params=pltpu.CompilerParams(vmem_limit_bytes=48 * 2**20),
     )(
-        jnp.stack([head, at_c]).astype(jnp.int32),
+        place,
         decay_rate,
         beta_bias,
         all_tokens,
         weights,
-        swapped,
-    )
-
-    place = jnp.stack([at_y, at_x * 2 + at_c]).astype(jnp.int32)
+    )
+
     maps = lax.all_gather(total, ("tm_1", "tm_2"), axis=0)
     before, kept, maps = pl.pallas_call(
         join_kernel,
@@ -265,7 +263,7 @@
         out_shape=jax.ShapeDtypeStruct((block_rows, DV), bf16),
         in_specs=[smem] + [vmem] * 5,
         out_specs=vmem,
-        compiler_params=pltpu.CompilerParams(vmem_limit_bytes=32 * 2**20),
+        compiler_params=pltpu.CompilerParams(vmem_limit_bytes=16 * 2**20),
     )(place, maps, before, kept, reach, own)
     returned = lax.all_to_all(readout, "stream", split_axis=0, concat_axis=1, tiled=True)
     head_read = returned.reshape(local_rows, HEADS, DV).astype(f32)

time: 214 us -> 214 us (level)
    unnamed x20 -> x22, local copies, waits for them, and re-layouts: 5.35 us -> 3.35 us
  transfers between devices with their start and end apart: 3 -> 3, of which waited for: 3 -> 3; matrix products, arithmetic and copies ran while one was open for 1% -> 2% of each run, Pallas kernels for 0% -> 0%
where the time goes in v10:
time: 214 us; the launch traced here: 213 us
  waiting for transfers between devices  83.1 us (39%)
  blocking collectives  76.3 us (36%)
  Pallas kernels  18.5 us (9%)
  between operations  13.5 us (6%)
  starting transfers between devices  12.9 us (6%)
  local copies, waits for them, and re-layouts  5.59 us (3%)
  other arithmetic  3.22 us (2%)
    all_gather x1, waiting for transfers between devices, shards(): all_tokens = lax.all_gather(tokens, 'stream', axis=0, tiled=True)  51.8 us
    all_to_all x1, waiting for transfers between devices, shards(): lax.all_to_all(readout, 'stream', split_axis=0, concat_axis=1, tiled=True)  27.9 us
    all_to_all x1, blocking collectives, shards(): lax.all_to_all(weights, 'stream', split_axis=0, concat_axis=0, tiled=True)  26.6 us
    all_to_all x1, blocking collectives, shards(): lax.all_to_all(weights, ('tm_0', 'tm_1'), split_axis=0, concat_axis=0, ti...  23.2 us
    all_gather x1, blocking collectives, shards(): maps = lax.all_gather(total, ('tm_1', 'tm_2'), axis=0)  14.7 us
    pallas_call x1, Pallas kernels, shards(): pl.pallas_call(chunk_kernel, out_shape=(jax.ShapeDtypeStruct((block_rows,...  13.6 us
    all_to_all x1, blocking collectives, shards(): maps = lax.all_to_all(maps, 'tm_0', split_axis=0, concat_axis=0, tiled=True)  11.9 us
    all_to_all x1, starting transfers between devices, shards(): lax.all_to_all(readout, 'stream', split_axis=0, concat_axis=1, tiled=True)  11 us
  transfers between devices with their start and end apart: 3, of which 3 were waited for; matrix products, arithmetic and copies ran while one was open for 2% of the time, Pallas kernels for 0%

profile of v10, /device:TPU:32, one launch (start us, length us, event | category | flops | bytes accessed | tf_op | source)
XLA Modules:
  0.0 213.2 jit_solution(12873822214491377073)
XLA Ops:
  6.5 0.0 copy-start
  6.5 0.0 all-gather.3.cloned.1.call-start
  6.5 0.7 all-gather.3.cloned.1.call-update
  7.3 0.8 constant_dynamic-slice_fusion
  8.1 0.1 copy.21
  8.1 0.1 copy.17
  8.3 0.1 copy.22
  8.4 0.1 copy.18
  8.5 0.1 pad.5.clone
  8.6 0.0 copy-done
  8.6 0.8 dynamic-slice_bitcast_fusion
  9.4 0.1 fusion.4
  9.5 26.6 %all_to_all.28 = bf16[16,8,256]{2,1,0:T(8,128)(2,1)S(1)} all-to-all(bf16[16,8,256]{2,1,0:T(8,128)(2,1)S(1)} %fusion.4), channel_id=1, replica_groups=mesh['tm_0'=4,'tm_1'=4,'tm_2'=2,'stream'=16] {'stream'}, dimensions={0} | all-to-all | bytes 131072 | tf_op jit(solution)/shard_map/all_to_all | solution.py:203
  36.1 0.1 broadcast_in_dim.5
  36.2 23.2 %all_to_all.29 = bf16[16,16,8,256]{3,2,1,0:T(8,128)(2,1)S(1)} all-to-all(bf16[16,16,8,256]{3,2,1,0:T(8,128)(2,1)S(1)} %broadcast_in_dim.5), channel_id=1, replica_groups=mesh['tm_0'=4,'tm_1'=4,'tm_2'=2,'stream'=16] {'tm_0','tm_1'}, dimensions={0} | all-to-all | bytes 2097152 | tf_op jit(solution)/shard_map/all_to_all | solution.py:205
  59.4 1.9 collective-permute-start
  61.3 0.1 pad_add_fusion.head_ref.place_ref
  61.4 0.0 copy-start.4
  61.4 2.7 %collective-permute-done = bf16[16,16,8,256]{3,2,1,0:T(8,128)(2,1)} collective-permute-done((bf16[16,16,8,256]{3,2,1,0:T(8,128)(2,1)S(1)}, bf16[16,16,8,256]{3,2,1,0:T(8,128)(2,1)}, u32[]{:S(2)}, u32[]{:S(2)}) %collective-permute-start) | collective-permute-done | bytes 1048608 | tf_op jit(solution)/shard_map/ppermute | solution.py:206
  64.0 1.4 broadcast_select_fusion.1
  65.4 0.2 maximum_bitcast_fusion
  65.6 0.0 copy-start.7
  65.6 0.0 copy-start.8
  65.7 0.2 copy.19
  65.9 51.8 %all-gather.3.cloned.1.call-done.token_ref = bf16[2048,2048]{1,0:T(8,128)(2,1)} async-done(((bf16[128,2048]{1,0:T(8,128)(2,1)}), bf16[2048,2048]{1,0:T(8,128)(2,1)}) %all-gather.3.cloned.1.call-update) | async-done | bytes 8388624 | tf_op jit(solution)/shard_map/all_gather | solution.py:202
  117.6 0.0 copy-done.4
  117.6 0.0 copy-done.7
  117.6 0.0 copy-done.8
  117.7 13.6 %shard_map.91 = (bf16[2048,128]{1,0:T(8,128)(2,1)S(1)}, f32[2048,128]{1,0:T(8,128)S(1)}, bf16[272,128]{1,0:T(8,128)(2,1)S(1)}) custom-call(s32[3]{0:T(128)S(1)} %pad_add_fusion.head_ref.place_ref, f32[16]{0:T(128)S(1)} %copy-done.7, f32[16]{0:T(128)S(1)} %copy-done.8, bf16[2048,2048]{1,0:T(8,128)(2,1)} %all-gather.3.cloned.1.call-done.token_ref, ...), custom_call_target="tpu_custom_call" | custom-call | tf_op jit(solution)/shard_map/pallas_call | solution.py:217
  131.3 0.0 copy-start.1
  131.3 1.0 copy-done.1
  132.3 14.7 %all-gather = bf16[2176,128]{1,0:T(8,128)(2,1)} all-gather(bf16[272,128]{1,0:T(8,128)(2,1)S(1)} %get-tuple-element.11), channel_id=2, replica_groups=mesh['tm_0'=4,'tm_1'=4,'tm_2'=2,'stream'=16] {'tm_1','tm_2'}, dimensions={0}, use_global_device_ids=true | all-gather | bytes 626688 | tf_op jit(solution)/shard_map/all_gather | solution.py:249
  146.9 3.1 %shard_map.92 = (f32[256,128]{1,0:T(8,128)}, f32[8,128]{1,0:T(8,128)}, bf16[4,272,128]{2,1,0:T(8,128)(2,1)}) custom-call(s32[3]{0:T(128)} %copy-done.4, bf16[8,272,128]{2,1,0:T(8,128)(2,1)} %bitcast.37), custom_call_target="tpu_custom_call" | custom-call | tf_op jit(solution)/shard_map/pallas_call | solution.py:250
  150.0 0.0 copy-start.9
  150.0 11.9 %all_to_all.30.map_ref = bf16[4,272,128]{2,1,0:T(8,128)(2,1)S(1)} all-to-all(bf16[4,272,128]{2,1,0:T(8,128)(2,1)} %get-tuple-element.12), channel_id=1, replica_groups=mesh['tm_0'=4,'tm_1'=4,'tm_2'=2,'stream'=16] {'tm_0'}, dimensions={0} | all-to-all | bytes 557056 | tf_op jit(solution)/shard_map/all_to_all | solution.py:260
  161.9 0.0 copy-done.2
  161.9 0.0 copy-start.3
  161.9 0.9 copy-done.3
  162.8 0.0 copy-start.5
  162.8 0.6 copy-done.5
  163.5 0.0 copy-start.6
  163.5 0.7 copy-done.6
  164.1 1.8 shard_map.93
  165.9 11.0 %all-to-all-start.3 = ((bf16[16,128,128]{2,1,0:T(8,128)(2,1)}), bf16[16,128,128]{2,1,0:T(8,128)(2,1)S(1)}, u32[]{:S(2)}, u32[]{:S(2)}) async-start(bf16[16,128,128]{2,1,0:T(8,128)(2,1)} %bitcast.12), calls=%async_computation.3 | async-start | bytes 1048576 | tf_op jit(solution)/shard_map/all_to_all | solution.py:268
  176.9 0.0 copy-done.9
  176.9 27.9 %all-to-all-done.3 = bf16[16,128,128]{2,1,0:T(8,128)(2,1)S(1)} async-done(((bf16[16,128,128]{2,1,0:T(8,128)(2,1)}), bf16[16,128,128]{2,1,0:T(8,128)(2,1)S(1)}, u32[]{:S(2)}, u32[]{:S(2)}) %all-to-all-start.3) | async-done | bytes 524320 | tf_op jit(solution)/shard_map/all_to_all | solution.py:268
  204.8 0.3 fusion.2
  205.2 1.1 fusion.3
  (5 shorter events, 0.0 us)
Async XLA Ops:
  6.5 2.1 copy-start
  6.5 111.1 %all-gather.3.cloned.1.call-start = ((), (), s32[]{:S(2)}) async-start(), calls=%async_computation.4 | async-start | bytes 8912896 | tf_op jit(solution)/shard_map/all_gather | solution.py:202
  59.4 4.7 %collective-permute-start = (bf16[16,16,8,256]{3,2,1,0:T(8,128)(2,1)S(1)}, bf16[16,16,8,256]{3,2,1,0:T(8,128)(2,1)}, u32[]{:S(2)}, u32[]{:S(2)}) collective-permute-start(bf16[16,16,8,256]{3,2,1,0:T(8,128)(2,1)S(1)} %all_to_all.29), channel_id=1, source_target_pairs={{0,16},{16,0},{1,17},{17,1},{2,18},{18,2},{3,19},{19,3},{4,20},{20... | collective-permute-start | bytes 3145736 | tf_op jit(solution)/shard_map/ppermute | solution.py:206
  61.4 56.3 %copy-start.4 = (s32[3]{0:T(128)}, s32[3]{0:T(128)S(1)}, u32[]{:S(2)}) copy-start(s32[3]{0:T(128)S(1)} %pad_add_fusion.head_ref.place_ref) | copy-start | bytes 40
  65.6 52.0 %copy-start.7 = (f32[16]{0:T(128)S(1)}, f32[16]{0:T(128)}, u32[]{:S(2)}) copy-start(f32[16]{0:T(128)} %rate_ref.1) | copy-start | bytes 196
  65.6 52.0 %copy-start.8 = (f32[16]{0:T(128)S(1)}, f32[16]{0:T(128)}, u32[]{:S(2)}) copy-start(f32[16]{0:T(128)} %bias_ref.1) | copy-start | bytes 196
  131.3 1.0 copy-start.1
  132.3 29.7 %copy-start.2 = (f32[2048,128]{1,0:T(8,128)S(1)}, f32[2048,128]{1,0:T(8,128)}, u32[]{:S(2)}) copy-start(f32[2048,128]{1,0:T(8,128)} %copy-done.1) | copy-start | bytes 3145732
  150.0 26.9 %copy-start.9 = (f32[128]{0:T(128)S(1)}, f32[128]{0:T(128)}, u32[]{:S(2)}) copy-start(f32[128]{0:T(128)} %param.17) | copy-start | bytes 1540
  161.9 0.9 copy-start.3
  162.8 0.6 copy-start.5
  163.5 0.7 copy-start.6
  165.9 38.9 %all-to-all-start.3 = ((bf16[16,128,128]{2,1,0:T(8,128)(2,1)}), bf16[16,128,128]{2,1,0:T(8,128)(2,1)S(1)}, u32[]{:S(2)}, u32[]{:S(2)}) async-start(bf16[16,128,128]{2,1,0:T(8,128)(2,1)} %bitcast.12), calls=%async_computation.3 | async-start | bytes 1048576 | tf_op jit(solution)/shard_map/all_to_all | solution.py:268
Sparse Core Ops, SparseCore 0:
  9.4 108.1 all-gather.2

commit v11 on v7

--- a/solution.py
+++ b/solution.py
@@ -29,8 +29,7 @@
     rate_ref,
     bias_ref,
     token_ref,
-    mine_ref,
-    other_ref,
+    weight_ref,
     reach_ref,
     own_ref,
     total_ref,
@@ -39,13 +38,9 @@
     step, steps = pl.program_id(0), pl.num_programs(0)
     rate, bias = rate_ref[head_ref[0]], bias_ref[head_ref[0]]
     size = token_ref.shape[0]
-    rows = pl.ds(pl.multiple_of(step * size, size), size)
-    half = mine_ref.shape[1]
-    for c in range(2):
-        weights = jnp.where(head_ref[1] == c, mine_ref[...], other_ref[...])
-        raw_ref[rows, c * half : (c + 1) * half] = jnp.dot(
-            token_ref[...], weights, preferred_element_type=f32
-        )
+    raw_ref[pl.ds(pl.multiple_of(step * size, size), size), :] = jnp.dot(
+        token_ref[...], weight_ref[...], preferred_element_type=f32
+    )
 
     @pl.when(step == steps - 1)
     def _():
@@ -144,7 +139,7 @@
     return change, shift.astype(f32), kept[0:1] + kept[8:9]
 
 
-def join_kernel(core_ref, mine_ref, other_ref, copies_ref):
+def join_kernel(place_ref, mine_ref, other_ref, copies_ref):
     def write(first_ref, second_ref):
         change, shift, kept = opened(first_ref)
         next_change, next_shift, next_kept = opened(second_ref)
@@ -159,11 +154,11 @@
             copies_ref[i, DK : DK + DV, :] = shift
             copies_ref[i, DK + DV : MAP_ROWS, :] = kept
 
-    @pl.when(core_ref[0] == 0)
+    @pl.when(place_ref[2] == 0)
     def _():
         write(mine_ref, other_ref)
 
-    @pl.when(core_ref[0] == 1)
+    @pl.when(place_ref[2] == 1)
     def _():
         write(other_ref, mine_ref)
 
@@ -175,8 +170,8 @@
     def one(j, state):
         return after(state, *opened(map_ref, j))
 
-    state = lax.fori_loop(0, place_ref[0], one, jnp.zeros((DV, DK), f32))
-    state = jnp.where(place_ref[1] == 1, after(state, *opened(other_ref)), state)
+    state = lax.fori_loop(0, place_ref[1], one, jnp.zeros((DV, DK), f32))
+    state = jnp.where(place_ref[2] == 1, after(state, *opened(other_ref)), state)
     read_ref[...] = (mm(reach_ref[...], state, 1, 1) + own_ref[...]).astype(bf16)
 
 
@@ -207,8 +202,14 @@
     weights = lax.all_to_all(weights, "stream", split_axis=0, concat_axis=0, tiled=True)
     weights = jnp.broadcast_to(weights[None], (shares,) + weights.shape)
     weights = lax.all_to_all(weights, ("tm_0", "tm_1"), split_axis=0, concat_axis=0, tiled=True)
-    weights = weights.transpose(1, 0, 2, 3).reshape(streams * shares * rows, WIDE // 2)
     swapped = lax.ppermute(weights, "tm_2", [(0, 1), (1, 0)])
+    halves = [
+        jnp.where(at_c == 0, weights, swapped),
+        jnp.where(at_c == 0, swapped, weights),
+    ]
+    weights = jnp.concatenate(halves, -1)
+    weights = weights.transpose(1, 0, 2, 3).reshape(streams * shares * rows, WIDE)
+    place = jnp.stack([head, at_y * 4 + at_x, at_c]).astype(jnp.int32)
 
     block_rows, features = all_tokens.shape
     steps = 2
@@ -225,8 +226,7 @@
             smem,
             smem,
             pl.BlockSpec((block_rows // steps, features), lambda i: (i, 0)),
-            pl.BlockSpec((features, WIDE // 2), lambda i: (0, 0)),
-            pl.BlockSpec((features, WIDE // 2), lambda i: (0, 0)),
+            pl.BlockSpec((features, WIDE), lambda i: (0, 0)),
         ],
         out_specs=(
             pl.BlockSpec((block_rows, DK), lambda i: (0, 0)),
@@ -238,24 +238,21 @@
         ],
         compiler_params=pltpu.CompilerParams(vmem_limit_bytes=48 * 2**20),
     )(
-        jnp.stack([head, at_c]).astype(jnp.int32),
+        place,
         decay_rate,
         beta_bias,
         all_tokens,
         weights,
-        swapped,
-    )
-
-    core = at_c.reshape(1).astype(jnp.int32)
+    )
+
     other = lax.ppermute(total, "tm_2", [(0, 1), (1, 0)])
     maps = pl.pallas_call(
         join_kernel,
         out_shape=jax.ShapeDtypeStruct((shares, MAP_ROWS, DK), bf16),
         in_specs=[smem, vmem, vmem],
         out_specs=vmem,
-    )(core, total, other)
+    )(place, total, other)
     maps = lax.all_to_all(maps, ("tm_0", "tm_1"), split_axis=0, concat_axis=0, tiled=True)
-    place = jnp.stack([at_y * 4 + at_x, at_c]).astype(jnp.int32)
     readout = pl.pallas_call(
         read_kernel,
         out_shape=jax.ShapeDtypeStruct((block_rows, DV), bf16),

time: 213 us -> 213 us (level)
  the two profiles are of different devices: /device:TPU:64 before, /device:TPU:32 now
where the time goes in v11:
time: 213 us; the launch traced here: 212 us
  waiting for transfers between devices  83.8 us (39%)
  blocking collectives  75.1 us (35%)
  Pallas kernels  17.6 us (8%)
  starting transfers between devices  14.9 us (7%)
  between operations  13.6 us (6%)
  local copies, waits for them, and re-layouts  4.03 us (2%)
  other arithmetic  3.22 us (2%)
    all_gather x1, waiting for transfers between devices, shards(): all_tokens = lax.all_gather(tokens, 'stream', axis=0, tiled=True)  51.8 us
    all_to_all x1, waiting for transfers between devices, shards(): lax.all_to_all(readout, 'stream', split_axis=0, concat_axis=1, tiled=True)  27.5 us
    all_to_all x1, blocking collectives, shards(): lax.all_to_all(weights, 'stream', split_axis=0, concat_axis=0, tiled=True)  26.6 us
    all_to_all x1, blocking collectives, shards(): lax.all_to_all(maps, ('tm_0', 'tm_1'), split_axis=0, concat_axis=0, tiled...  25.3 us
    all_to_all x1, blocking collectives, shards(): lax.all_to_all(weights, ('tm_0', 'tm_1'), split_axis=0, concat_axis=0, ti...  23.2 us
    pallas_call x1, Pallas kernels, shards(): pl.pallas_call(chunk_kernel, out_shape=(jax.ShapeDtypeStruct((block_rows,...  13.6 us
    all_to_all x1, starting transfers between devices, shards(): lax.all_to_all(readout, 'stream', split_axis=0, concat_axis=1, tiled=True)  11 us
  transfers between devices with their start and end apart: 4, of which 4 were waited for; matrix products, arithmetic and copies ran while one was open for 2% of the time, Pallas kernels for 0%

profile of v11, /device:TPU:32, one launch (start us, length us, event | category | flops | bytes accessed | tf_op | source)
XLA Modules:
  0.0 212.2 jit_solution(8929646040877588487)
XLA Ops:
  6.5 0.0 copy-start
  6.5 0.0 all-gather.2.cloned.1.call-start
  6.5 0.7 all-gather.2.cloned.1.call-update
  7.3 0.8 constant_dynamic-slice_fusion
  8.1 0.1 copy.21
  8.1 0.1 copy.17
  8.3 0.1 copy.22
  8.4 0.1 copy.18
  8.5 0.1 pad.5.clone
  8.6 0.0 copy-done
  8.6 0.8 dynamic-slice_bitcast_fusion
  9.4 0.1 fusion.4
  9.5 26.6 %all_to_all.28 = bf16[16,8,256]{2,1,0:T(8,128)(2,1)S(1)} all-to-all(bf16[16,8,256]{2,1,0:T(8,128)(2,1)S(1)} %fusion.4), channel_id=1, replica_groups=mesh['tm_0'=4,'tm_1'=4,'tm_2'=2,'stream'=16] {'stream'}, dimensions={0} | all-to-all | bytes 131072 | tf_op jit(solution)/shard_map/all_to_all | solution.py:202
  36.1 0.1 broadcast_in_dim.5
  36.2 23.2 %all_to_all.29 = bf16[16,16,8,256]{3,2,1,0:T(8,128)(2,1)S(1)} all-to-all(bf16[16,16,8,256]{3,2,1,0:T(8,128)(2,1)S(1)} %broadcast_in_dim.5), channel_id=1, replica_groups=mesh['tm_0'=4,'tm_1'=4,'tm_2'=2,'stream'=16] {'tm_0','tm_1'}, dimensions={0} | all-to-all | bytes 2097152 | tf_op jit(solution)/shard_map/all_to_all | solution.py:204
  59.4 1.9 collective-permute-start
  61.3 0.1 pad_add_fusion.head_ref.place_ref
  61.4 0.0 copy-start.6
  61.4 2.7 %collective-permute-done = bf16[16,16,8,256]{3,2,1,0:T(8,128)(2,1)} collective-permute-done((bf16[16,16,8,256]{3,2,1,0:T(8,128)(2,1)S(1)}, bf16[16,16,8,256]{3,2,1,0:T(8,128)(2,1)}, u32[]{:S(2)}, u32[]{:S(2)}) %collective-permute-start) | collective-permute-done | bytes 1048608 | tf_op jit(solution)/shard_map/ppermute | solution.py:205
  64.0 1.4 broadcast_select_fusion.1
  65.4 0.2 maximum_bitcast_fusion
  65.6 0.0 copy-start.8
  65.6 0.0 copy-start.9
  65.7 0.2 copy.19
  65.9 51.8 %all-gather.2.cloned.1.call-done.token_ref = bf16[2048,2048]{1,0:T(8,128)(2,1)} async-done(((bf16[128,2048]{1,0:T(8,128)(2,1)}), bf16[2048,2048]{1,0:T(8,128)(2,1)}) %all-gather.2.cloned.1.call-update) | async-done | bytes 8388624 | tf_op jit(solution)/shard_map/all_gather | solution.py:201
  117.6 0.0 copy-done.6
  117.6 0.0 copy-done.8
  117.6 0.0 copy-done.9
  117.6 13.6 %shard_map.91 = (bf16[2048,128]{1,0:T(8,128)(2,1)S(1)}, f32[2048,128]{1,0:T(8,128)S(1)}, bf16[272,128]{1,0:T(8,128)(2,1)S(1)}) custom-call(s32[3]{0:T(128)S(1)} %pad_add_fusion.head_ref.place_ref, f32[16]{0:T(128)S(1)} %copy-done.8, f32[16]{0:T(128)S(1)} %copy-done.9, bf16[2048,2048]{1,0:T(8,128)(2,1)} %all-gather.2.cloned.1.call-done.token_ref, ...), custom_call_target="tpu_custom_call" | custom-call | tf_op jit(solution)/shard_map/pallas_call | solution.py:216
  131.3 0.0 copy-start.1
  131.3 1.0 copy-done.1
  132.2 0.0 copy-start.5
  132.3 2.1 collective-permute-start.1
  134.3 1.2 collective-permute-done.1.other_ref
  135.5 0.0 copy-done.5
  135.5 0.6 copy-done.3
  136.2 2.1 %shard_map.92 = bf16[16,272,128]{2,1,0:T(8,128)(2,1)} custom-call(s32[3]{0:T(128)} %copy-done.6, bf16[272,128]{1,0:T(8,128)(2,1)} %copy-done.5, bf16[272,128]{1,0:T(8,128)(2,1)} %copy-done.3), custom_call_target="tpu_custom_call" | custom-call | tf_op jit(solution)/shard_map/pallas_call | solution.py:249
  138.3 25.3 %all_to_all.30.map_ref = bf16[16,272,128]{2,1,0:T(8,128)(2,1)S(1)} all-to-all(bf16[16,272,128]{2,1,0:T(8,128)(2,1)} %shard_map.92), channel_id=1, replica_groups=mesh['tm_0'=4,'tm_1'=4,'tm_2'=2,'stream'=16] {'tm_0','tm_1'}, dimensions={0} | all-to-all | bytes 2228224 | tf_op jit(solution)/shard_map/all_to_all | solution.py:255
  163.6 0.0 copy-done.7
  163.6 0.0 copy-done.2
  163.6 0.0 copy-done.4
  163.6 0.0 copy-start.10
  163.6 1.8 shard_map.93
  165.4 11.0 %all-to-all-start.3 = ((bf16[16,128,128]{2,1,0:T(8,128)(2,1)}), bf16[16,128,128]{2,1,0:T(8,128)(2,1)S(1)}, u32[]{:S(2)}, u32[]{:S(2)}) async-start(bf16[16,128,128]{2,1,0:T(8,128)(2,1)} %bitcast.11), calls=%async_computation.3 | async-start | bytes 1048576 | tf_op jit(solution)/shard_map/all_to_all | solution.py:263
  176.4 0.0 copy-done.10
  176.4 27.5 %all-to-all-done.3 = bf16[16,128,128]{2,1,0:T(8,128)(2,1)S(1)} async-done(((bf16[16,128,128]{2,1,0:T(8,128)(2,1)}), bf16[16,128,128]{2,1,0:T(8,128)(2,1)S(1)}, u32[]{:S(2)}, u32[]{:S(2)}) %all-to-all-start.3) | async-done | bytes 524320 | tf_op jit(solution)/shard_map/all_to_all | solution.py:263
  203.9 0.3 fusion.2
  204.2 1.1 fusion.3
  (8 shorter events, 0.0 us)
Async XLA Ops:
  6.5 2.1 copy-start
  6.5 111.1 %all-gather.2.cloned.1.call-start = ((), (), s32[]{:S(2)}) async-start(), calls=%async_computation.4 | async-start | bytes 8912896 | tf_op jit(solution)/shard_map/all_gather | solution.py:201
  59.4 4.7 %collective-permute-start = (bf16[16,16,8,256]{3,2,1,0:T(8,128)(2,1)S(1)}, bf16[16,16,8,256]{3,2,1,0:T(8,128)(2,1)}, u32[]{:S(2)}, u32[]{:S(2)}) collective-permute-start(bf16[16,16,8,256]{3,2,1,0:T(8,128)(2,1)S(1)} %all_to_all.29), channel_id=1, source_target_pairs={{0,16},{16,0},{1,17},{17,1},{2,18},{18,2},{3,19},{19,3},{4,20},{20... | collective-permute-start | bytes 3145736 | tf_op jit(solution)/shard_map/ppermute | solution.py:205
  61.4 56.3 %copy-start.6 = (s32[3]{0:T(128)}, s32[3]{0:T(128)S(1)}, u32[]{:S(2)}) copy-start(s32[3]{0:T(128)S(1)} %pad_add_fusion.head_ref.place_ref) | copy-start | bytes 40
  65.6 52.0 %copy-start.8 = (f32[16]{0:T(128)S(1)}, f32[16]{0:T(128)}, u32[]{:S(2)}) copy-start(f32[16]{0:T(128)} %rate_ref.1) | copy-start | bytes 196
  65.6 52.0 %copy-start.9 = (f32[16]{0:T(128)S(1)}, f32[16]{0:T(128)}, u32[]{:S(2)}) copy-start(f32[16]{0:T(128)} %bias_ref.1) | copy-start | bytes 196
  131.3 1.0 copy-start.1
  132.2 3.3 %copy-start.5 = (bf16[272,128]{1,0:T(8,128)(2,1)}, bf16[272,128]{1,0:T(8,128)(2,1)S(1)}, u32[]{:S(2)}) copy-start(bf16[272,128]{1,0:T(8,128)(2,1)S(1)} %get-tuple-element.8.mine_ref) | copy-start | bytes 208900
  132.2 31.4 %copy-start.7 = (s32[3]{0:T(128)S(1)}, s32[3]{0:T(128)}, u32[]{:S(2)}) copy-start(s32[3]{0:T(128)} %copy-done.6) | copy-start | bytes 40
  132.2 31.4 %copy-start.2 = (f32[2048,128]{1,0:T(8,128)S(1)}, f32[2048,128]{1,0:T(8,128)}, u32[]{:S(2)}) copy-start(f32[2048,128]{1,0:T(8,128)} %copy-done.1) | copy-start | bytes 3145732
  132.3 3.3 %collective-permute-start.1 = (bf16[272,128]{1,0:T(8,128)(2,1)S(1)}, bf16[272,128]{1,0:T(8,128)(2,1)S(1)}, u32[]{:S(2)}, u32[]{:S(2)}) collective-permute-start(bf16[272,128]{1,0:T(8,128)(2,1)S(1)} %get-tuple-element.8.mine_ref), channel_id=1, source_target_pairs={{0,16},{16,0},{1,17},{17,1},{2,18},{18,2},{3,19},{19,3},{4,20},{20... | collective-permute-start | bytes 208904 | tf_op jit(solution)/shard_map/ppermute | solution.py:248
  135.5 0.6 copy-start.3
  138.3 25.3 %copy-start.4 = (bf16[272,128]{1,0:T(8,128)(2,1)S(1)}, bf16[272,128]{1,0:T(8,128)(2,1)}, u32[]{:S(2)}) copy-start(bf16[272,128]{1,0:T(8,128)(2,1)} %copy-done.3) | copy-start | bytes 208900
  163.6 12.8 %copy-start.10 = (f32[128]{0:T(128)S(1)}, f32[128]{0:T(128)}, u32[]{:S(2)}) copy-start(f32[128]{0:T(128)} %param.17) | copy-start | bytes 1540
  165.4 38.5 %all-to-all-start.3 = ((bf16[16,128,128]{2,1,0:T(8,128)(2,1)}), bf16[16,128,128]{2,1,0:T(8,128)(2,1)S(1)}, u32[]{:S(2)}, u32[]{:S(2)}) async-start(bf16[16,128,128]{2,1,0:T(8,128)(2,1)} %bitcast.11), calls=%async_computation.3 | async-start | bytes 1048576 | tf_op jit(solution)/shard_map/all_to_all | solution.py:263
Sparse Core Ops, SparseCore 0:
  9.4 108.1 all-gather.1

commit v12 on v11

--- a/solution.py
+++ b/solution.py
@@ -212,7 +212,7 @@
     place = jnp.stack([head, at_y * 4 + at_x, at_c]).astype(jnp.int32)
 
     block_rows, features = all_tokens.shape
-    steps = 2
+    steps = 4
     reach, own, total = pl.pallas_call(
         chunk_kernel,
         out_shape=(

time: 213 us -> 213 us (level)
  no operation moved by 1% of the time
where the time goes in v12:
time: 213 us; the launch traced here: 212 us
  waiting for transfers between devices  83.8 us (39%)
  blocking collectives  75.1 us (35%)
  Pallas kernels  17.7 us (8%)
  starting transfers between devices  15 us (7%)
  between operations  13.6 us (6%)
  local copies, waits for them, and re-layouts  4.03 us (2%)
  other arithmetic  3.22 us (2%)
    all_gather x1, waiting for transfers between devices, shards(): all_tokens = lax.all_gather(tokens, 'stream', axis=0, tiled=True)  51.8 us
    all_to_all x1, waiting for transfers between devices, shards(): lax.all_to_all(readout, 'stream', split_axis=0, concat_axis=1, tiled=True)  27.5 us
    all_to_all x1, blocking collectives, shards(): lax.all_to_all(weights, 'stream', split_axis=0, concat_axis=0, tiled=True)  26.6 us
    all_to_all x1, blocking collectives, shards(): lax.all_to_all(maps, ('tm_0', 'tm_1'), split_axis=0, concat_axis=0, tiled...  25.3 us
    all_to_all x1, blocking collectives, shards(): lax.all_to_all(weights, ('tm_0', 'tm_1'), split_axis=0, concat_axis=0, ti...  23.2 us
    pallas_call x1, Pallas kernels, shards(): pl.pallas_call(chunk_kernel, out_shape=(jax.ShapeDtypeStruct((block_rows,...  13.8 us
    all_to_all x1, starting transfers between devices, shards(): lax.all_to_all(readout, 'stream', split_axis=0, concat_axis=1, tiled=True)  11 us
  transfers between devices with their start and end apart: 4, of which 4 were waited for; matrix products, arithmetic and copies ran while one was open for 2% of the time, Pallas kernels for 0%

profile of v12, /device:TPU:32, one launch (start us, length us, event | category | flops | bytes accessed | tf_op | source)
XLA Modules:
  0.0 212.4 jit_solution(4007650681982243798)
XLA Ops:
  6.5 0.0 copy-start
  6.5 0.0 all-gather.2.cloned.1.call-start
  6.5 0.7 all-gather.2.cloned.1.call-update
  7.3 0.8 constant_dynamic-slice_fusion
  8.1 0.1 copy.21
  8.1 0.1 copy.17
  8.3 0.1 copy.22
  8.4 0.1 copy.18
  8.5 0.1 pad.5.clone
  8.6 0.0 copy-done
  8.6 0.8 dynamic-slice_bitcast_fusion
  9.4 0.1 fusion.4
  9.5 26.6 %all_to_all.28 = bf16[16,8,256]{2,1,0:T(8,128)(2,1)S(1)} all-to-all(bf16[16,8,256]{2,1,0:T(8,128)(2,1)S(1)} %fusion.4), channel_id=1, replica_groups=mesh['tm_0'=4,'tm_1'=4,'tm_2'=2,'stream'=16] {'stream'}, dimensions={0} | all-to-all | bytes 131072 | tf_op jit(solution)/shard_map/all_to_all | solution.py:202
  36.1 0.1 broadcast_in_dim.5
  36.2 23.2 %all_to_all.29 = bf16[16,16,8,256]{3,2,1,0:T(8,128)(2,1)S(1)} all-to-all(bf16[16,16,8,256]{3,2,1,0:T(8,128)(2,1)S(1)} %broadcast_in_dim.5), channel_id=1, replica_groups=mesh['tm_0'=4,'tm_1'=4,'tm_2'=2,'stream'=16] {'tm_0','tm_1'}, dimensions={0} | all-to-all | bytes 2097152 | tf_op jit(solution)/shard_map/all_to_all | solution.py:204
  59.4 1.9 collective-permute-start
  61.3 0.1 pad_add_fusion.head_ref.place_ref
  61.4 0.0 copy-start.6
  61.4 2.7 %collective-permute-done = bf16[16,16,8,256]{3,2,1,0:T(8,128)(2,1)} collective-permute-done((bf16[16,16,8,256]{3,2,1,0:T(8,128)(2,1)S(1)}, bf16[16,16,8,256]{3,2,1,0:T(8,128)(2,1)}, u32[]{:S(2)}, u32[]{:S(2)}) %collective-permute-start) | collective-permute-done | bytes 1048608 | tf_op jit(solution)/shard_map/ppermute | solution.py:205
  64.0 1.4 broadcast_select_fusion.1
  65.4 0.2 maximum_bitcast_fusion
  65.6 0.0 copy-start.8
  65.6 0.0 copy-start.9
  65.7 0.2 copy.19
  65.9 51.8 %all-gather.2.cloned.1.call-done.token_ref = bf16[2048,2048]{1,0:T(8,128)(2,1)} async-done(((bf16[128,2048]{1,0:T(8,128)(2,1)}), bf16[2048,2048]{1,0:T(8,128)(2,1)}) %all-gather.2.cloned.1.call-update) | async-done | bytes 8388624 | tf_op jit(solution)/shard_map/all_gather | solution.py:201
  117.6 0.0 copy-done.6
  117.6 0.0 copy-done.8
  117.6 0.0 copy-done.9
  117.6 13.8 %shard_map.91 = (bf16[2048,128]{1,0:T(8,128)(2,1)S(1)}, f32[2048,128]{1,0:T(8,128)S(1)}, bf16[272,128]{1,0:T(8,128)(2,1)S(1)}) custom-call(s32[3]{0:T(128)S(1)} %pad_add_fusion.head_ref.place_ref, f32[16]{0:T(128)S(1)} %copy-done.8, f32[16]{0:T(128)S(1)} %copy-done.9, bf16[2048,2048]{1,0:T(8,128)(2,1)} %all-gather.2.cloned.1.call-done.token_ref, ...), custom_call_target="tpu_custom_call" | custom-call | tf_op jit(solution)/shard_map/pallas_call | solution.py:216
  131.5 0.0 copy-start.1
  131.5 1.0 copy-done.1
  132.4 0.0 copy-start.5
  132.4 2.1 collective-permute-start.1
  134.5 1.2 collective-permute-done.1.other_ref
  135.7 0.0 copy-done.5
  135.7 0.6 copy-done.3
  136.3 2.1 %shard_map.92 = bf16[16,272,128]{2,1,0:T(8,128)(2,1)} custom-call(s32[3]{0:T(128)} %copy-done.6, bf16[272,128]{1,0:T(8,128)(2,1)} %copy-done.5, bf16[272,128]{1,0:T(8,128)(2,1)} %copy-done.3), custom_call_target="tpu_custom_call" | custom-call | tf_op jit(solution)/shard_map/pallas_call | solution.py:249
  138.5 25.3 %all_to_all.30.map_ref = bf16[16,272,128]{2,1,0:T(8,128)(2,1)S(1)} all-to-all(bf16[16,272,128]{2,1,0:T(8,128)(2,1)} %shard_map.92), channel_id=1, replica_groups=mesh['tm_0'=4,'tm_1'=4,'tm_2'=2,'stream'=16] {'tm_0','tm_1'}, dimensions={0} | all-to-all | bytes 2228224 | tf_op jit(solution)/shard_map/all_to_all | solution.py:255
  163.8 0.0 copy-done.7
  163.8 0.0 copy-done.2
  163.8 0.0 copy-done.4
  163.8 0.0 copy-start.10
  163.8 1.8 shard_map.93
  165.6 11.0 %all-to-all-start.3 = ((bf16[16,128,128]{2,1,0:T(8,128)(2,1)}), bf16[16,128,128]{2,1,0:T(8,128)(2,1)S(1)}, u32[]{:S(2)}, u32[]{:S(2)}) async-start(bf16[16,128,128]{2,1,0:T(8,128)(2,1)} %bitcast.11), calls=%async_computation.3 | async-start | bytes 1048576 | tf_op jit(solution)/shard_map/all_to_all | solution.py:263
  176.6 0.0 copy-done.10
  176.6 27.5 %all-to-all-done.3 = bf16[16,128,128]{2,1,0:T(8,128)(2,1)S(1)} async-done(((bf16[16,128,128]{2,1,0:T(8,128)(2,1)}), bf16[16,128,128]{2,1,0:T(8,128)(2,1)S(1)}, u32[]{:S(2)}, u32[]{:S(2)}) %all-to-all-start.3) | async-done | bytes 524320 | tf_op jit(solution)/shard_map/all_to_all | solution.py:263
  204.1 0.3 fusion.2
  204.4 1.1 fusion.3
  (8 shorter events, 0.0 us)
Async XLA Ops:
  6.5 2.1 copy-start
  6.5 111.1 %all-gather.2.cloned.1.call-start = ((), (), s32[]{:S(2)}) async-start(), calls=%async_computation.4 | async-start | bytes 8912896 | tf_op jit(solution)/shard_map/all_gather | solution.py:201
  59.4 4.7 %collective-permute-start = (bf16[16,16,8,256]{3,2,1,0:T(8,128)(2,1)S(1)}, bf16[16,16,8,256]{3,2,1,0:T(8,128)(2,1)}, u32[]{:S(2)}, u32[]{:S(2)}) collective-permute-start(bf16[16,16,8,256]{3,2,1,0:T(8,128)(2,1)S(1)} %all_to_all.29), channel_id=1, source_target_pairs={{0,16},{16,0},{1,17},{17,1},{2,18},{18,2},{3,19},{19,3},{4,20},{20... | collective-permute-start | bytes 3145736 | tf_op jit(solution)/shard_map/ppermute | solution.py:205
  61.4 56.3 %copy-start.6 = (s32[3]{0:T(128)}, s32[3]{0:T(128)S(1)}, u32[]{:S(2)}) copy-start(s32[3]{0:T(128)S(1)} %pad_add_fusion.head_ref.place_ref) | copy-start | bytes 40
  65.6 52.0 %copy-start.8 = (f32[16]{0:T(128)S(1)}, f32[16]{0:T(128)}, u32[]{:S(2)}) copy-start(f32[16]{0:T(128)} %rate_ref.1) | copy-start | bytes 196
  65.6 52.0 %copy-start.9 = (f32[16]{0:T(128)S(1)}, f32[16]{0:T(128)}, u32[]{:S(2)}) copy-start(f32[16]{0:T(128)} %bias_ref.1) | copy-start | bytes 196
  131.5 1.0 copy-start.1
  132.4 3.3 %copy-start.5 = (bf16[272,128]{1,0:T(8,128)(2,1)}, bf16[272,128]{1,0:T(8,128)(2,1)S(1)}, u32[]{:S(2)}) copy-start(bf16[272,128]{1,0:T(8,128)(2,1)S(1)} %get-tuple-element.8.mine_ref) | copy-start | bytes 208900
  132.4 31.4 %copy-start.7 = (s32[3]{0:T(128)S(1)}, s32[3]{0:T(128)}, u32[]{:S(2)}) copy-start(s32[3]{0:T(128)} %copy-done.6) | copy-start | bytes 40
  132.4 31.4 %copy-start.2 = (f32[2048,128]{1,0:T(8,128)S(1)}, f32[2048,128]{1,0:T(8,128)}, u32[]{:S(2)}) copy-start(f32[2048,128]{1,0:T(8,128)} %copy-done.1) | copy-start | bytes 3145732
  132.4 3.3 %collective-permute-start.1 = (bf16[272,128]{1,0:T(8,128)(2,1)S(1)}, bf16[272,128]{1,0:T(8,128)(2,1)S(1)}, u32[]{:S(2)}, u32[]{:S(2)}) collective-permute-start(bf16[272,128]{1,0:T(8,128)(2,1)S(1)} %get-tuple-element.8.mine_ref), channel_id=1, source_target_pairs={{0,16},{16,0},{1,17},{17,1},{2,18},{18,2},{3,19},{19,3},{4,20},{20... | collective-permute-start | bytes 208904 | tf_op jit(solution)/shard_map/ppermute | solution.py:248
  135.7 0.6 copy-start.3
  138.5 25.3 %copy-start.4 = (bf16[272,128]{1,0:T(8,128)(2,1)S(1)}, bf16[272,128]{1,0:T(8,128)(2,1)}, u32[]{:S(2)}) copy-start(bf16[272,128]{1,0:T(8,128)(2,1)} %copy-done.3) | copy-start | bytes 208900
  163.8 12.8 %copy-start.10 = (f32[128]{0:T(128)S(1)}, f32[128]{0:T(128)}, u32[]{:S(2)}) copy-start(f32[128]{0:T(128)} %param.17) | copy-start | bytes 1540
  165.6 38.5 %all-to-all-start.3 = ((bf16[16,128,128]{2,1,0:T(8,128)(2,1)}), bf16[16,128,128]{2,1,0:T(8,128)(2,1)S(1)}, u32[]{:S(2)}, u32[]{:S(2)}) async-start(bf16[16,128,128]{2,1,0:T(8,128)(2,1)} %bitcast.11), calls=%async_computation.3 | async-start | bytes 1048576 | tf_op jit(solution)/shard_map/all_to_all | solution.py:263
Sparse Core Ops, SparseCore 0:
  9.4 108.1 all-gather.1
